TPU v7x, 32 devices: a whole 2x2x4 slice. The times are simulated.
32 devices in a mesh: dp: 16 (over z, y, x), mp: 2 (over core).
Axes of the slice: x: 2, y: 2, z: 4, core: 2. Of those that a mesh axis runs over, the one named last changes fastest.
Arguments:
- queries: bfloat16 [2048, 8192], P('dp', 'mp'), may hold values from -6 to 6
- query_gain: float32 [8192], P('mp'), may hold values from 0.4 to 1.6
- keys: bfloat16 [2048, 8192], P('dp', 'mp'), may hold values from -24 to 24
- values: bfloat16 [2048, 8192], P('dp', 'mp'), may hold values from -6 to 6
- neighbours: int32 [32, 2], P('dp'), may hold values from 0 to 15, as said below
- d_out: bfloat16 [2048, 8192], P('dp', 'mp'), may hold values from -6 to 6
Outputs:
- attended: bfloat16 [2048, 8192], P('dp', 'mp')
- d_queries: bfloat16 [2048, 8192], P('dp', 'mp')
- d_keys: bfloat16 [2048, 8192], P('dp', 'mp')
- d_values: bfloat16 [2048, 8192], P('dp', 'mp')
Inputs may be any that keep to these rules, and one draw needn't show every extreme that they name: The two neighbours of group c are two different blocks among (c // 2 + k) mod 16 for k = -2, -1, 0, 1, 2; the four neighbours named by the groups of one index of dp are four different blocks.
All inputs are finite; a program needn't handle non-finite values.
Results may differ from a plain program's by a relative error of at most 0.0071.
Values may be sent and summed in bfloat16 or wider, within the bound.
No kernel may reach another device: no remote copies, remote signals or barrier semaphores. Data moves between devices by JAX's collectives and lax.ppermute only.
A program may use at most 128 MiB of HBM per device.

v0:
```python
import functools

import jax
import jax.numpy as jnp
from jax import lax
from jax.experimental import pallas as pl
from jax.experimental.pallas import tpu as pltpu
from jax.sharding import PartitionSpec as P

HEADS = 64
HS = 128
GROUP = 64
FEAT = HEADS * HS
EPSILON = 1e-06
SCALING = 1.0 / HS**0.5
LANES = 128
CHUNK = 8
WIDE = CHUNK * HS
SLOTS = 5
OWN = (0, 2)
PARTNER = (1, 3, 4)


def routes(count):
    def side(i):
        return -4 if i & 2 == 0 else 4

    diagonal = (-3, -1, 1, 3)
    return {
        "y": [(i, i ^ 2) for i in range(count)],
        2: [(i, i ^ 1) for i in range(count)],
        3: [(i, (i + side(i)) % count) for i in range(count)],
        4: [(i, (i + diagonal[i & 3]) % count) for i in range(count)],
    }


def sent(array, route):
    return lax.ppermute(array, "dp", route)


def out_and_back(count):
    route = routes(count)
    back = {s: [(b, a) for a, b in route[s]] for s in (2, 3, 4)}

    def go(parts):
        return [sent(p, route[s]) if s >= 2 else p for s, p in enumerate(parts)]

    def come(parts):
        return [sent(p, back[s]) if s >= 2 else p for s, p in enumerate(parts)]

    return go, come, functools.partial(sent, route=route["y"])


def dot(a, b, left, right):
    return lax.dot_general(a, b, (((left,), (right,)), ((), ())), preferred_element_type=jnp.float32)


def group_numbers(place_ref, near_ref, count, groups):
    place = place_ref[0]
    one = 1 - 2 * (place & 1)
    two = 2 - 2 * (place & 2)
    numbers = []
    for offset in (0, two, one, -two, -one):
        block = lax.rem(place + offset + count, count)
        number = jnp.int32(-1)
        for g in range(groups):
            used = (near_ref[g, 0] == block) | (near_ref[g, 1] == block)
            number = jnp.where(used, g, number)
        numbers.append(number)
    return numbers


def rows_of(number):
    return pl.ds(pl.multiple_of(jnp.maximum(number, 0) * GROUP, GROUP), GROUP)


def lane_partial(x):
    total = x[:, 0:LANES]
    for t in range(1, x.shape[1] // LANES):
        total = total + x[:, t * LANES : (t + 1) * LANES]
    return total


def to_row(x):
    return jnp.sum(x.T, axis=0, keepdims=True)


def to_columns(row):
    return jnp.broadcast_to(row, (row.shape[1], row.shape[1])).T


def prepare_grads_kernel(count, groups, place_ref, near_ref, g_ref, q_ref, *refs):
    slot_refs, squares_ref, total_ref = refs[:SLOTS], refs[SLOTS], refs[SLOTS + 1]
    numbers = group_numbers(place_ref, near_ref, count, groups)
    for s in range(SLOTS):
        slot_refs[s][...] = g_ref[rows_of(numbers[s])]
    step = pl.program_id(0)
    x = q_ref[...].astype(jnp.float32)
    partial = lane_partial(x * x)

    @pl.when(step == 0)
    def _():
        total_ref[...] = partial

    @pl.when(step > 0)
    def _():
        total_ref[...] += partial

    @pl.when(step == pl.num_programs(0) - 1)
    def _():
        squares_ref[...] = to_row(total_ref[...])


def inverse_columns(squares_ref):
    return to_columns(lax.rsqrt(squares_ref[...] / FEAT + EPSILON))


def prepare_queries_kernel(count, groups, place_ref, near_ref, q_ref, gain_ref, squares_ref, *refs):
    slot_refs, normed_ref = refs[:SLOTS], refs[SLOTS]
    numbers = group_numbers(place_ref, near_ref, count, groups)
    inverse = inverse_columns(squares_ref)
    for t in range(q_ref.shape[1] // LANES):
        cols = slice(t * LANES, (t + 1) * LANES)
        x = q_ref[:, cols].astype(jnp.float32)
        normed_ref[:, cols] = (x * gain_ref[:, cols] * inverse).astype(jnp.bfloat16)
    for s in range(SLOTS):
        slot_refs[s][...] = normed_ref[rows_of(numbers[s])]


def head(refs, slots, h):
    cols = slice(h * HS, (h + 1) * HS)
    return jnp.concatenate([refs[s][:, cols] for s in slots], axis=0)


def paired(stats, left, right):
    return jnp.concatenate([stats[left], stats[right]], axis=1)


def scores_kernel(*refs):
    q_refs, k_refs, stat_refs = refs[:SLOTS], refs[SLOTS : SLOTS + 2], refs[SLOTS + 2 :]
    for slots, k_ref in zip((OWN, PARTNER), k_refs):
        tops, totals = [], []
        for h in range(CHUNK):
            cols = slice(h * HS, (h + 1) * HS)
            scores = dot(k_ref[:, cols], head(q_refs, slots, h), 1, 1) * SCALING
            top = jnp.max(scores, axis=0, keepdims=True)
            tops.append(top)
            totals.append(jnp.sum(jnp.exp(scores - top), axis=0, keepdims=True))
        tops = jnp.concatenate(tops, axis=0)
        totals = jnp.concatenate(totals, axis=0)
        for at, s in enumerate(slots):
            lanes = slice(at * GROUP, (at + 1) * GROUP)
            stat_refs[s][...] = jnp.concatenate([tops[:, lanes], totals[:, lanes]], axis=1)


def combine_scores_kernel(count, groups, place_ref, near_ref, *refs):
    stat_refs, back_refs = refs[:SLOTS], refs[SLOTS:]
    numbers = group_numbers(place_ref, near_ref, count, groups)
    heads = stat_refs[0].shape[0]
    shape = (heads, GROUP)
    tops = [r[:, 0:GROUP] for r in stat_refs]
    totals = [r[:, GROUP : 2 * GROUP] for r in stat_refs]
    number_of = [jnp.full(shape, n, jnp.int32) for n in numbers]
    lowest = jnp.full(shape, -jnp.inf, jnp.float32)
    zero = jnp.zeros(shape, jnp.float32)
    merged = []
    for g in range(groups):
        top, total = lowest, zero
        for s in range(SLOTS):
            top = jnp.maximum(top, jnp.where(number_of[s] == g, tops[s], lowest))
        for s in range(SLOTS):
            mine = number_of[s] == g
            factor = jnp.exp(jnp.where(mine, tops[s] - top, zero))
            total = total + jnp.where(mine, totals[s] * factor, zero)
        merged.append((top, 1.0 / total))
    for s in range(SLOTS):
        top, inv = tops[s], zero
        for g in range(groups):
            mine = number_of[s] == g
            top = jnp.where(mine, merged[g][0], top)
            inv = jnp.where(mine, merged[g][1], inv)
        back_refs[s][...] = jnp.concatenate([top, inv], axis=1)


def combine_centres_kernel(count, groups, place_ref, near_ref, *refs):
    stat_refs, back_refs = refs[:SLOTS], refs[SLOTS:]
    numbers = group_numbers(place_ref, near_ref, count, groups)
    shape = stat_refs[0].shape
    number_of = [jnp.full(shape, n, jnp.int32) for n in numbers]
    zero = jnp.zeros(shape, jnp.float32)
    for g in range(groups):
        total = zero
        for s in range(SLOTS):
            total = total + jnp.where(number_of[s] == g, stat_refs[s][...], zero)
        for s in range(SLOTS):
            here = zero if g == 0 else back_refs[s][...]
            back_refs[s][...] = jnp.where(number_of[s] == g, total, here)


def stat_rows(stat_refs, slots, half):
    lanes = slice(half * GROUP, (half + 1) * GROUP)
    return jnp.concatenate([stat_refs[s][:, lanes] for s in slots], axis=1)


def probs_of(k, q, top, inv):
    return jnp.exp(dot(k, q, 1, 1) * SCALING - top) * inv


def context_kernel(*refs):
    q_refs, g_refs, back_refs = (refs[i * SLOTS : (i + 1) * SLOTS] for i in range(3))
    k_refs, v_refs = refs[3 * SLOTS : 3 * SLOTS + 2], refs[3 * SLOTS + 2 : 3 * SLOTS + 4]
    rest = refs[3 * SLOTS + 4 :]
    ctx_refs, centre_refs, dv_refs = rest[:SLOTS], rest[SLOTS : 2 * SLOTS], rest[2 * SLOTS :]
    for slots, k_ref, v_ref, dv_ref in zip((OWN, PARTNER), k_refs, v_refs, dv_refs):
        top, inv = stat_rows(back_refs, slots, 0), stat_rows(back_refs, slots, 1)
        centres = []
        for h in range(CHUNK):
            cols = slice(h * HS, (h + 1) * HS)
            q, g, v = head(q_refs, slots, h), head(g_refs, slots, h), v_ref[:, cols]
            probs = probs_of(k_ref[:, cols], q, top[h : h + 1], inv[h : h + 1])
            low = probs.astype(jnp.bfloat16)
            context = dot(low, v, 0, 0).astype(jnp.bfloat16)
            for at, s in enumerate(slots):
                ctx_refs[s][:, cols] = context[at * GROUP : (at + 1) * GROUP]
            centres.append(jnp.sum(probs * dot(v, g, 1, 1), axis=0, keepdims=True))
            dv_ref[:, cols] = dot(low, g, 1, 0).astype(dv_ref.dtype)
        centres = jnp.concatenate(centres, axis=0)
        empty = jnp.zeros((CHUNK, GROUP), jnp.float32)
        for at, s in enumerate(slots):
            lanes = slice(at * GROUP, (at + 1) * GROUP)
            centre_refs[s][...] = jnp.concatenate([centres[:, lanes], empty], axis=1)


def gradient_kernel(*refs):
    q_refs, g_refs, back_refs, centre_refs = (refs[i * SLOTS : (i + 1) * SLOTS] for i in range(4))
    k_refs, v_refs = refs[4 * SLOTS : 4 * SLOTS + 2], refs[4 * SLOTS + 2 : 4 * SLOTS + 4]
    rest = refs[4 * SLOTS + 4 :]
    grad_refs, dk_refs = rest[:SLOTS], rest[SLOTS:]
    for slots, k_ref, v_ref, dk_ref in zip((OWN, PARTNER), k_refs, v_refs, dk_refs):
        top, inv = stat_rows(back_refs, slots, 0), stat_rows(back_refs, slots, 1)
        centre = stat_rows(centre_refs, slots, 0)
        for h in range(CHUNK):
            cols = slice(h * HS, (h + 1) * HS)
            q, g = head(q_refs, slots, h), head(g_refs, slots, h)
            k, v = k_ref[:, cols], v_ref[:, cols]
            probs = probs_of(k, q, top[h : h + 1], inv[h : h + 1])
            low = (probs * (dot(v, g, 1, 1) - centre[h : h + 1])).astype(jnp.bfloat16)
            grad = (dot(low, k, 0, 0) * SCALING).astype(jnp.bfloat16)
            for at, s in enumerate(slots):
                grad_refs[s][:, cols] = grad[at * GROUP : (at + 1) * GROUP]
            dk_ref[:, cols] = (dot(low, q, 1, 0) * SCALING).astype(dk_ref.dtype)


def gathered(numbers, refs, g):
    total = None
    for s in range(SLOTS):
        part = jnp.where(numbers[s] == g, 1.0, 0.0) * refs[s][...].astype(jnp.float32)
        total = part if total is None else total + part
    return total


def attended_kernel(count, groups, place_ref, near_ref, *refs):
    ctx_refs, own_ref, far_ref, out_ref, dv_ref = (
        refs[:SLOTS], refs[SLOTS], refs[SLOTS + 1], refs[SLOTS + 2], refs[SLOTS + 3]
    )
    numbers = group_numbers(place_ref, near_ref, count, groups)
    for g in range(groups):
        out_ref[g * GROUP : (g + 1) * GROUP] = gathered(numbers, ctx_refs, g).astype(jnp.bfloat16)
    dv_ref[...] = (own_ref[...] + far_ref[...].astype(jnp.float32)).astype(jnp.bfloat16)


def inner_kernel(count, groups, place_ref, near_ref, *refs):
    grad_refs = refs[:SLOTS]
    q_ref, gain_ref, scaled_ref, inner_ref, total_ref = refs[SLOTS:]
    numbers = group_numbers(place_ref, near_ref, count, groups)
    step = pl.program_id(0)

    @pl.when(step == 0)
    def _():
        total_ref[...] = jnp.zeros_like(total_ref)

    for g in range(groups):
        rows = slice(g * GROUP, (g + 1) * GROUP)
        scaled = gathered(numbers, grad_refs, g) * gain_ref[...]
        scaled_ref[rows] = scaled
        total_ref[rows] += lane_partial(scaled * q_ref[rows].astype(jnp.float32))

    @pl.when(step == pl.num_programs(0) - 1)
    def _():
        inner_ref[...] = to_row(total_ref[...])


def finish_kernel(scaled_ref, q_ref, squares_ref, inner_ref, own_ref, far_ref, dq_ref, dk_ref):
    inverse = inverse_columns(squares_ref)
    factor = inverse * inverse * inverse * to_columns(inner_ref[...]) / FEAT
    for t in range(q_ref.shape[1] // LANES):
        cols = slice(t * LANES, (t + 1) * LANES)
        x = q_ref[:, cols].astype(jnp.float32)
        dq_ref[:, cols] = (inverse * scaled_ref[:, cols] - x * factor).astype(jnp.bfloat16)
    dk_ref[...] = (own_ref[...] + far_ref[...].astype(jnp.float32)).astype(jnp.bfloat16)


def kernel_call(body, name, steps, ins, outs, scratch=(), flops=0):
    shapes = [shape for _, shape in outs]
    moved = sum(s.size * s.dtype.itemsize for s in shapes)
    return pl.pallas_call(
        body,
        grid=(steps,),
        in_specs=ins,
        out_specs=[spec for spec, _ in outs],
        out_shape=shapes,
        scratch_shapes=list(scratch),
        name=name,
        cost_estimate=pl.CostEstimate(flops=flops, bytes_accessed=2 * moved, transcendentals=0),
        compiler_params=pltpu.CompilerParams(
            dimension_semantics=("arbitrary",), vmem_limit_bytes=32 * 1024 * 1024
        ),
    )


def local(queries, query_gain, keys, values, neighbours, d_out):
    rows, width = queries.shape
    heads = width // HS
    groups = rows // GROUP
    steps = width // WIDE
    count = lax.axis_size("dp")
    go, come, across = out_and_back(count)
    place = jnp.full((1,), lax.axis_index("dp"), jnp.int32)
    gain = query_gain[None, :]

    scalars = pl.BlockSpec(memory_space=pltpu.SMEM)
    slot = pl.BlockSpec((GROUP, WIDE), lambda i: (0, i))
    tall = pl.BlockSpec((rows, WIDE), lambda i: (0, i))
    line = pl.BlockSpec((1, WIDE), lambda i: (0, i))
    row = pl.BlockSpec((1, rows), lambda i: (0, 0))
    stat = pl.BlockSpec((CHUNK, LANES), lambda i: (i, 0))
    stat_whole = pl.BlockSpec((heads, LANES), lambda i: (0, 0))
    slot_out = (slot, jax.ShapeDtypeStruct((GROUP, width), jnp.bfloat16))
    tall_out = (tall, jax.ShapeDtypeStruct((rows, width), jnp.bfloat16))
    tall_wide = (tall, jax.ShapeDtypeStruct((rows, width), jnp.float32))
    row_out = (row, jax.ShapeDtypeStruct((1, rows), jnp.float32))
    stat_shape = jax.ShapeDtypeStruct((heads, LANES), jnp.float32)
    stat_out, stat_whole_out = (stat, stat_shape), (stat_whole, stat_shape)
    totals = pltpu.VMEM((rows, LANES), jnp.float32)
    product = 2 * SLOTS * GROUP * keys.shape[0] * width

    def with_place(kernel):
        return functools.partial(kernel, count, groups)

    far_keys = across(keys)
    *g_parts, squares = kernel_call(
        with_place(prepare_grads_kernel), "prepare_grads", steps,
        [scalars] * 2 + [tall] * 2, [slot_out] * SLOTS + [row_out], [totals],
    )(place, neighbours, d_out, queries)
    squares = lax.psum(squares, "mp")
    q_parts = kernel_call(
        with_place(prepare_queries_kernel), "prepare_queries", steps,
        [scalars] * 2 + [tall, line, row], [slot_out] * SLOTS,
        [pltpu.VMEM((rows, WIDE), jnp.bfloat16)],
    )(place, neighbours, queries, gain, squares)
    q_slots = go(q_parts)
    far_values = across(values)
    g_slots = go(g_parts)

    stats = kernel_call(
        scores_kernel, "scores", steps, [slot] * SLOTS + [tall] * 2, [stat_out] * SLOTS,
        flops=product,
    )(*q_slots, keys, far_keys)
    back = kernel_call(
        with_place(combine_scores_kernel), "combine_scores", 1,
        [scalars] * 2 + [stat_whole] * SLOTS, [stat_whole_out] * SLOTS,
    )(place, neighbours, *come(stats))
    back = go(back)

    *outs, own_dv, far_dv = kernel_call(
        context_kernel, "context", steps,
        [slot] * (2 * SLOTS) + [stat] * SLOTS + [tall] * 4,
        [slot_out] * SLOTS + [stat_out] * SLOTS + [tall_wide, tall_out],
        flops=4 * product,
    )(*q_slots, *g_slots, *back, keys, far_keys, values, far_values)
    contexts, centres = outs[:SLOTS], outs[SLOTS:]
    centres = kernel_call(
        with_place(combine_centres_kernel), "combine_centres", 1,
        [scalars] * 2 + [stat_whole] * SLOTS, [stat_whole_out] * SLOTS,
    )(place, neighbours, *come(centres))
    centres = go(centres)
    far_dv = across(far_dv)
    contexts = come(contexts)

    *grads, own_dk, far_dk = kernel_call(
        gradient_kernel, "gradient", steps,
        [slot] * (2 * SLOTS) + [stat] * (2 * SLOTS) + [tall] * 4,
        [slot_out] * SLOTS + [tall_wide, tall_out],
        flops=4 * product,
    )(*q_slots, *g_slots, *back, *centres, keys, far_keys, values, far_values)
    far_dk = across(far_dk)
    grads = come(grads)

    attended, d_values = kernel_call(
        with_place(attended_kernel), "attended", steps,
        [scalars] * 2 + [slot] * SLOTS + [tall] * 2, [tall_out] * 2,
    )(place, neighbours, *contexts, own_dv, far_dv)
    scaled, inner = kernel_call(
        with_place(inner_kernel), "inner", steps,
        [scalars] * 2 + [slot] * SLOTS + [tall, line], [tall_wide, row_out], [totals],
    )(place, neighbours, *grads, queries, gain)
    inner = lax.psum(inner, "mp")
    d_queries, d_keys = kernel_call(
        finish_kernel, "finish", steps, [tall, tall, row, row, tall, tall], [tall_out] * 2,
    )(scaled, queries, squares, inner, own_dk, far_dk)
    return (attended, d_queries, d_keys, d_values)


def solution(mesh):
    placed = (P("dp", "mp"), P("mp"), P("dp", "mp"), P("dp", "mp"), P("dp", None), P("dp", "mp"))
    return jax.shard_map(
        local,
        mesh=mesh,
        in_specs=placed,
        out_specs=(P("dp", "mp"), P("dp", "mp"), P("dp", "mp"), P("dp", "mp")),
        check_vma=False,
    )
```

profile of v0, /device:TPU:0, one launch (start us, length us, event | category | flops | bytes accessed | tf_op | source)
XLA Modules:
  0.0 188.2 jit_solution(8574032744296197280)
XLA Ops:
  0.6 3.0 %collective-permute-start.6 = (bf16[128,4096]{1,0:T(8,128)(2,1)}, bf16[128,4096]{1,0:T(8,128)(2,1)S(1)}, u32[]{:S(2)}, u32[]{:S(2)}) collective-permute-start(bf16[128,4096]{1,0:T(8,128)(2,1)} %refs_20_.1), channel_id=1, source_target_pairs={{0,4},{2,6},{4,0},{6,2},{8,12},{10,14},{12,8},{14,10},{16,20},{18,... | collective-permute-start | bytes 3145736 | tf_op jit(solution)/shard_map/ppermute | solution.py:38
  3.7 1.2 copy-done
  4.9 1.2 copy-done.14
  6.1 0.7 copy-done.21
  6.8 1.5 prepare_grads.1
  8.3 0.8 copy-done.6
  9.1 0.8 copy-done.8
  9.9 0.8 copy-done.23
  10.7 0.8 copy-done.24
  11.5 0.8 copy-done.25
  12.3 2.4 %psum.14.squares_ref = f32[1,128]{1,0:T(1,128)S(1)} all-reduce(f32[1,128]{1,0:T(1,128)S(1)} %get-tuple-element.55), channel_id=1, replica_groups=mesh['dp'=16,'mp'=2] {'mp'}, use_global_device_ids=true, to_apply=%region_0.0 | all-reduce | flops 128 | bytes 1024 | tf_op jit(solution)/shard_map/psum | solution.py:355
  14.7 0.7 copy-done.19
  15.4 1.6 prepare_queries.1
  17.0 1.6 collective-permute-start
  18.6 3.6 %collective-permute-start.1 = (bf16[64,4096]{1,0:T(8,128)(2,1)S(1)}, bf16[64,4096]{1,0:T(8,128)(2,1)S(1)}, u32[]{:S(2)}, u32[]{:S(2)}) collective-permute-start(bf16[64,4096]{1,0:T(8,128)(2,1)S(1)} %get-tuple-element.59), channel_id=1, source_target_pairs={{0,24},{2,26},{4,12},{6,14},{8,0},{10,2},{12,20},{14,22},{16,8},{1... | collective-permute-start | bytes 1572872 | tf_op jit(solution)/shard_map/ppermute | solution.py:38
  22.2 0.4 collective-permute-start.2
  22.6 9.3 %collective-permute-done.refs_2_ = bf16[64,4096]{1,0:T(8,128)(2,1)S(1)} collective-permute-done((bf16[64,4096]{1,0:T(8,128)(2,1)S(1)}, bf16[64,4096]{1,0:T(8,128)(2,1)S(1)}, u32[]{:S(2)}, u32[]{:S(2)}) %collective-permute-start) | collective-permute-done | bytes 524320 | tf_op jit(solution)/shard_map/ppermute | solution.py:38
  31.9 0.7 collective-permute-start.3
  32.6 1.9 %collective-permute-done.1.refs_3_ = bf16[64,4096]{1,0:T(8,128)(2,1)S(1)} collective-permute-done((bf16[64,4096]{1,0:T(8,128)(2,1)S(1)}, bf16[64,4096]{1,0:T(8,128)(2,1)S(1)}, u32[]{:S(2)}, u32[]{:S(2)}) %collective-permute-start.1) | collective-permute-done | bytes 524320 | tf_op jit(solution)/shard_map/ppermute | solution.py:38
  34.5 4.3 %collective-permute-start.4 = (bf16[64,4096]{1,0:T(8,128)(2,1)}, bf16[64,4096]{1,0:T(8,128)(2,1)S(1)}, u32[]{:S(2)}, u32[]{:S(2)}) collective-permute-start(bf16[64,4096]{1,0:T(8,128)(2,1)} %copy-done.24), channel_id=1, source_target_pairs={{0,24},{2,26},{4,12},{6,14},{8,0},{10,2},{12,20},{14,22},{16,8},{1... | collective-permute-start | bytes 1572872 | tf_op jit(solution)/shard_map/ppermute | solution.py:38
  38.8 7.0 %collective-permute-done.2.refs_4_ = bf16[64,4096]{1,0:T(8,128)(2,1)S(1)} collective-permute-done((bf16[64,4096]{1,0:T(8,128)(2,1)S(1)}, bf16[64,4096]{1,0:T(8,128)(2,1)S(1)}, u32[]{:S(2)}, u32[]{:S(2)}) %collective-permute-start.2) | collective-permute-done | bytes 524320 | tf_op jit(solution)/shard_map/ppermute | solution.py:38
  45.8 5.2 %collective-permute-start.5 = (bf16[64,4096]{1,0:T(8,128)(2,1)}, bf16[64,4096]{1,0:T(8,128)(2,1)S(1)}, u32[]{:S(2)}, u32[]{:S(2)}) collective-permute-start(bf16[64,4096]{1,0:T(8,128)(2,1)} %copy-done.23), channel_id=1, source_target_pairs={{0,26},{2,0},{4,6},{6,12},{8,2},{10,8},{12,14},{14,20},{16,10},{18... | collective-permute-start | bytes 1572872 | tf_op jit(solution)/shard_map/ppermute | solution.py:38
  51.0 3.7 %scores.1 = (f32[32,128]{1,0:T(8,128)S(1)}, f32[32,128]{1,0:T(8,128)S(1)}, f32[32,128]{1,0:T(8,128)S(1)}, f32[32,128]{1,0:T(8,128)S(1)}, f32[32,128]{1,0:T(8,128)S(1)}) custom-call(bf16[64,4096]{1,0:T(8,128)(2,1)S(1)} %get-tuple-element.56.refs_0_, bf16[64,4096]{1,0:T(8,128)(2,1)S(1)} %get-tuple-element.57.refs_1_, ...), custom_call_target="tpu_custom_call" | custom-call | flops 335544320 | bytes 163840 | tf_op jit(solution)/shard_map/scores/pallas_call | solution.py:365
  54.8 10.4 %collective-permute-done.7.refs_2_ = f32[32,128]{1,0:T(8,128)S(1)} collective-permute-done((f32[32,128]{1,0:T(8,128)S(1)}, f32[32,128]{1,0:T(8,128)S(1)}, u32[]{:S(2)}, u32[]{:S(2)}) %collective-permute-start.7) | collective-permute-done | bytes 16416 | tf_op jit(solution)/shard_map/ppermute | solution.py:38
  65.2 1.6 collective-permute-start.8
  66.7 4.0 %collective-permute-done.8.refs_3_ = f32[32,128]{1,0:T(8,128)S(1)} collective-permute-done((f32[32,128]{1,0:T(8,128)S(1)}, f32[32,128]{1,0:T(8,128)S(1)}, u32[]{:S(2)}, u32[]{:S(2)}) %collective-permute-start.8) | collective-permute-done | bytes 16416 | tf_op jit(solution)/shard_map/ppermute | solution.py:38
  70.7 2.6 %collective-permute-start.9 = (f32[32,128]{1,0:T(8,128)S(1)}, f32[32,128]{1,0:T(8,128)S(1)}, u32[]{:S(2)}, u32[]{:S(2)}) collective-permute-start(f32[32,128]{1,0:T(8,128)S(1)} %get-tuple-element.70), channel_id=1, source_target_pairs={{26,0},{0,2},{6,4},{12,6},{2,8},{8,10},{14,12},{20,14},{10,16},{16... | collective-permute-start | bytes 49160 | tf_op jit(solution)/shard_map/ppermute | solution.py:38
  73.3 3.8 %collective-permute-done.9.refs_4_ = f32[32,128]{1,0:T(8,128)S(1)} collective-permute-done((f32[32,128]{1,0:T(8,128)S(1)}, f32[32,128]{1,0:T(8,128)S(1)}, u32[]{:S(2)}, u32[]{:S(2)}) %collective-permute-start.9) | collective-permute-done | bytes 16416 | tf_op jit(solution)/shard_map/ppermute | solution.py:38
  77.1 0.7 combine_scores.1
  77.9 0.1 collective-permute-start.10
  77.9 0.3 collective-permute-start.11
  78.2 1.6 collective-permute-start.12
  79.9 1.8 collective-permute-done.10.refs_12_
  81.7 0.1 collective-permute-done.11.refs_13_
  81.7 0.2 collective-permute-done.12.refs_14_
  82.0 15.0 %context.1 = (bf16[64,4096]{1,0:T(8,128)(2,1)S(1)}, bf16[64,4096]{1,0:T(8,128)(2,1)S(1)}, bf16[64,4096]{1,0:T(8,128)(2,1)}, bf16[64,4096]{1,0:T(8,128)(2,1)}, bf...) custom-call(bf16[64,4096]{1,0:T(8,128)(2,1)S(1)} %get-tuple-element., ...), custom_call_target="tpu_custom_call" | custom-call | flops 1342177280 | bytes 11698176 | tf_op jit(solution)/shard_map/context/pallas_call | solution.py:375
  97.0 1.4 copy-done.4
  98.4 2.7 %collective-permute-start.18 = (f32[32,128]{1,0:T(8,128)S(1)}, f32[32,128]{1,0:T(8,128)S(1)}, u32[]{:S(2)}, u32[]{:S(2)}) collective-permute-start(f32[32,128]{1,0:T(8,128)S(1)} %get-tuple-element.86), channel_id=1, source_target_pairs={{2,0},{0,2},{6,4},{4,6},{10,8},{8,10},{14,12},{12,14},{18,16},{16,... | collective-permute-start | bytes 49160 | tf_op jit(solution)/shard_map/ppermute | solution.py:38
  101.0 2.0 %collective-permute-start.19 = (f32[32,128]{1,0:T(8,128)S(1)}, f32[32,128]{1,0:T(8,128)S(1)}, u32[]{:S(2)}, u32[]{:S(2)}) collective-permute-start(f32[32,128]{1,0:T(8,128)S(1)} %get-tuple-element.87), channel_id=1, source_target_pairs={{24,0},{26,2},{12,4},{14,6},{0,8},{2,10},{20,12},{22,14},{8,16},{1... | collective-permute-start | bytes 49160 | tf_op jit(solution)/shard_map/ppermute | solution.py:38
  103.0 3.6 %collective-permute-done.19.refs_3_ = f32[32,128]{1,0:T(8,128)S(1)} collective-permute-done((f32[32,128]{1,0:T(8,128)S(1)}, f32[32,128]{1,0:T(8,128)S(1)}, u32[]{:S(2)}, u32[]{:S(2)}) %collective-permute-start.19) | collective-permute-done | bytes 16416 | tf_op jit(solution)/shard_map/ppermute | solution.py:38
  106.6 2.9 %collective-permute-done.20.refs_4_ = f32[32,128]{1,0:T(8,128)S(1)} collective-permute-done((f32[32,128]{1,0:T(8,128)S(1)}, f32[32,128]{1,0:T(8,128)S(1)}, u32[]{:S(2)}, u32[]{:S(2)}) %collective-permute-start.20) | collective-permute-done | bytes 16416 | tf_op jit(solution)/shard_map/ppermute | solution.py:38
  109.5 0.6 combine_centres.1
  110.0 0.1 collective-permute-start.21
  110.1 0.3 collective-permute-start.22
  110.4 1.6 collective-permute-start.23
  112.0 1.8 collective-permute-done.21.refs_17_
  113.9 0.2 collective-permute-done.23.refs_19_
  114.2 17.9 %gradient.1 = (bf16[64,4096]{1,0:T(8,128)(2,1)S(1)}, bf16[64,4096]{1,0:T(8,128)(2,1)S(1)}, bf16[64,4096]{1,0:T(8,128)(2,1)S(1)}, bf16[64,4096]{1,0:T(8,128)(2,1)...) custom-call(bf16[64,4096]{1,0:T(8,128)(2,1)S(1)} %get-tuple-element.56.refs_0_, ...), custom_call_target="tpu_custom_call" | custom-call | flops 1342177280 | bytes 11534336 | tf_op jit(solution)/shard_map/gradient/pallas_call | solution.py:390
  132.1 1.3 copy-done.10
  133.4 2.7 %collective-permute-start.24 = (bf16[64,4096]{1,0:T(8,128)(2,1)S(1)}, bf16[64,4096]{1,0:T(8,128)(2,1)S(1)}, u32[]{:S(2)}, u32[]{:S(2)}) collective-permute-start(bf16[64,4096]{1,0:T(8,128)(2,1)S(1)} %get-tuple-element.96), channel_id=1, source_target_pairs={{2,0},{0,2},{6,4},{4,6},{10,8},{8,10},{14,12},{12,14},{18,16},{16,... | collective-permute-start | bytes 1572872 | tf_op jit(solution)/shard_map/ppermute | solution.py:38
  136.1 2.0 %collective-permute-start.25 = (bf16[64,4096]{1,0:T(8,128)(2,1)S(1)}, bf16[64,4096]{1,0:T(8,128)(2,1)S(1)}, u32[]{:S(2)}, u32[]{:S(2)}) collective-permute-start(bf16[64,4096]{1,0:T(8,128)(2,1)S(1)} %get-tuple-element.97), channel_id=1, source_target_pairs={{24,0},{26,2},{12,4},{14,6},{0,8},{2,10},{20,12},{22,14},{8,16},{1... | collective-permute-start | bytes 1572872 | tf_op jit(solution)/shard_map/ppermute | solution.py:38
  138.1 5.0 %collective-permute-start.17 = (bf16[128,4096]{1,0:T(8,128)(2,1)}, bf16[128,4096]{1,0:T(8,128)(2,1)}, u32[]{:S(2)}, u32[]{:S(2)}) collective-permute-start(bf16[128,4096]{1,0:T(8,128)(2,1)} %get-tuple-element.82), channel_id=1, source_target_pairs={{0,4},{2,6},{4,0},{6,2},{8,12},{10,14},{12,8},{14,10},{16,20},{18,... | collective-permute-start | bytes 3145736 | tf_op jit(solution)/shard_map/ppermute | solution.py:38
  143.2 13.2 %collective-permute-done.24.refs_2_ = bf16[64,4096]{1,0:T(8,128)(2,1)S(1)} collective-permute-done((bf16[64,4096]{1,0:T(8,128)(2,1)S(1)}, bf16[64,4096]{1,0:T(8,128)(2,1)S(1)}, u32[]{:S(2)}, u32[]{:S(2)}) %collective-permute-start.24) | collective-permute-done | bytes 524320 | tf_op jit(solution)/shard_map/ppermute | solution.py:38
  156.4 0.4 collective-permute-start.15
  156.7 6.9 %collective-permute-done.26.refs_4_ = bf16[64,4096]{1,0:T(8,128)(2,1)S(1)} collective-permute-done((bf16[64,4096]{1,0:T(8,128)(2,1)S(1)}, bf16[64,4096]{1,0:T(8,128)(2,1)S(1)}, u32[]{:S(2)}, u32[]{:S(2)}) %collective-permute-start.26) | collective-permute-done | bytes 524320 | tf_op jit(solution)/shard_map/ppermute | solution.py:38
  163.6 2.6 %inner.1 = (f32[128,4096]{1,0:T(8,128)S(1)}, f32[1,128]{1,0:T(1,128)S(1)}) custom-call(s32[1]{0:T(128)} %bitcast.place_ref, s32[2,2]{1,0:T(2,128)S(1)} %copy-done.22, bf16[64,4096]{1,0:T(8,128)(2,1)S(1)} %get-tuple-element.94.refs_0_, bf16[64,4096]{1,0:T(8,128)(2,1)S(1)} %get-tuple-element.95.refs_1_, bf16[64,4096]{1,0:T(8,128)(2,1)S(1)} %collective-permute-done.24.refs_2_, ...), custom_call_target="tpu_custom_call" | custom-call | bytes 4195328 | tf_op jit(solution)/shard_map/inner/pallas_call | solution.py:403
  166.2 1.3 copy-done.12
  167.5 2.4 %psum.15.inner_ref = f32[1,128]{1,0:T(1,128)S(1)} all-reduce(f32[1,128]{1,0:T(1,128)S(1)} %get-tuple-element.100), channel_id=1, replica_groups=mesh['dp'=16,'mp'=2] {'mp'}, use_global_device_ids=true, to_apply=%region_1.0 | all-reduce | flops 128 | bytes 1024 | tf_op jit(solution)/shard_map/psum | solution.py:407
  170.0 1.7 collective-permute-done.14.refs_2_
  171.7 5.7 %collective-permute-done.16.refs_4_ = bf16[64,4096]{1,0:T(8,128)(2,1)} collective-permute-done((bf16[64,4096]{1,0:T(8,128)(2,1)}, bf16[64,4096]{1,0:T(8,128)(2,1)}, u32[]{:S(2)}, u32[]{:S(2)}) %collective-permute-start.16) | collective-permute-done | bytes 524320 | tf_op jit(solution)/shard_map/ppermute | solution.py:38
  177.3 1.0 copy-done.16
  178.4 1.0 copy-done.18
  179.4 4.7 %attended.1 = (bf16[128,4096]{1,0:T(8,128)(2,1)}, bf16[128,4096]{1,0:T(8,128)(2,1)}) custom-call(s32[1]{0:T(128)} %bitcast.place_ref, s32[2,2]{1,0:T(2,128)S(1)} %copy-done.22, bf16[64,4096]{1,0:T(8,128)(2,1)S(1)} %copy-done.16, bf16[64,4096]{1,0:T(8,128)(2,1)S(1)} %copy-done.18, bf16[64,4096]{1,0:T(8,128)(2,1)} %collective-permute-done.14.refs_2_, ...), custom_call_target="tpu_custom_call" | custom-call | bytes 4194304 | tf_op jit(solution)/shard_map/attended/pallas_call | solution.py:399
  184.1 4.0 %finish.1 = (bf16[128,4096]{1,0:T(8,128)(2,1)}, bf16[128,4096]{1,0:T(8,128)(2,1)}) custom-call(f32[128,4096]{1,0:T(8,128)S(1)} %copy-done.13, bf16[128,4096]{1,0:T(8,128)(2,1)S(1)} %copy-done.1, f32[1,128]{1,0:T(1,128)S(1)} %psum.14.squares_ref, f32[1,128]{1,0:T(1,128)S(1)} %psum.15.inner_ref, f32[128,4096]{1,0:T(8,128)S(1)} %copy-done.11, ...), custom_call_target="tpu_custom_call" | custom-call | bytes 4194304 | tf_op jit(solution)/shard_map/finish/pallas_call | solution.py:408
  (56 shorter events, 0.2 us)
Async XLA Ops:
  0.6 14.1 %copy-start.22 = (s32[2,2]{1,0:T(2,128)S(1)}, s32[2,2]{1,0:T(2,128)}, u32[]{:S(2)}) copy-start(s32[2,2]{1,0:T(2,128)} %near_ref.11) | copy-start | bytes 52
  0.6 50.4 %collective-permute-start.6 = (bf16[128,4096]{1,0:T(8,128)(2,1)}, bf16[128,4096]{1,0:T(8,128)(2,1)S(1)}, u32[]{:S(2)}, u32[]{:S(2)}) collective-permute-start(bf16[128,4096]{1,0:T(8,128)(2,1)} %refs_20_.1), channel_id=1, source_target_pairs={{0,4},{2,6},{4,0},{6,2},{8,12},{10,14},{12,8},{14,10},{16,20},{18,... | collective-permute-start | bytes 3145736 | tf_op jit(solution)/shard_map/ppermute | solution.py:38
  3.7 1.2 copy-start
  4.9 1.2 copy-start.14
  6.1 0.7 copy-start.21
  6.8 7.9 %copy-start.1 = (bf16[128,4096]{1,0:T(8,128)(2,1)S(1)}, bf16[128,4096]{1,0:T(8,128)(2,1)}, u32[]{:S(2)}) copy-start(bf16[128,4096]{1,0:T(8,128)(2,1)} %q_ref.5) | copy-start | bytes 3145732
  6.8 44.2 %copy-start.2 = (bf16[128,4096]{1,0:T(8,128)(2,1)S(1)}, bf16[128,4096]{1,0:T(8,128)(2,1)}, u32[]{:S(2)}) copy-start(bf16[128,4096]{1,0:T(8,128)(2,1)} %refs_20_.1) | copy-start | bytes 3145732
  8.3 0.8 copy-start.6
  9.1 0.8 copy-start.8
  9.9 0.8 copy-start.23
  10.7 0.8 copy-start.24
  11.5 0.8 copy-start.25
  14.7 0.7 copy-start.19
  17.0 14.8 %collective-permute-start = (bf16[64,4096]{1,0:T(8,128)(2,1)S(1)}, bf16[64,4096]{1,0:T(8,128)(2,1)S(1)}, u32[]{:S(2)}, u32[]{:S(2)}) collective-permute-start(bf16[64,4096]{1,0:T(8,128)(2,1)S(1)} %get-tuple-element.58), channel_id=1, source_target_pairs={{0,2},{2,0},{4,6},{6,4},{8,10},{10,8},{12,14},{14,12},{16,18},{18,... | collective-permute-start | bytes 1572872 | tf_op jit(solution)/shard_map/ppermute | solution.py:38
  18.6 15.9 %collective-permute-start.1 = (bf16[64,4096]{1,0:T(8,128)(2,1)S(1)}, bf16[64,4096]{1,0:T(8,128)(2,1)S(1)}, u32[]{:S(2)}, u32[]{:S(2)}) collective-permute-start(bf16[64,4096]{1,0:T(8,128)(2,1)S(1)} %get-tuple-element.59), channel_id=1, source_target_pairs={{0,24},{2,26},{4,12},{6,14},{8,0},{10,2},{12,20},{14,22},{16,8},{1... | collective-permute-start | bytes 1572872 | tf_op jit(solution)/shard_map/ppermute | solution.py:38
  22.2 23.6 %collective-permute-start.2 = (bf16[64,4096]{1,0:T(8,128)(2,1)S(1)}, bf16[64,4096]{1,0:T(8,128)(2,1)S(1)}, u32[]{:S(2)}, u32[]{:S(2)}) collective-permute-start(bf16[64,4096]{1,0:T(8,128)(2,1)S(1)} %get-tuple-element.60), channel_id=1, source_target_pairs={{0,26},{2,0},{4,6},{6,12},{8,2},{10,8},{12,14},{14,20},{16,10},{18... | collective-permute-start | bytes 1572872 | tf_op jit(solution)/shard_map/ppermute | solution.py:38
  22.6 57.2 %collective-permute-start.13 = (bf16[128,4096]{1,0:T(8,128)(2,1)}, bf16[128,4096]{1,0:T(8,128)(2,1)S(1)}, u32[]{:S(2)}, u32[]{:S(2)}) collective-permute-start(bf16[128,4096]{1,0:T(8,128)(2,1)} %refs_22_.1), channel_id=1, source_target_pairs={{0,4},{2,6},{4,0},{6,2},{8,12},{10,14},{12,8},{14,10},{16,20},{18,... | collective-permute-start | bytes 3145736 | tf_op jit(solution)/shard_map/ppermute | solution.py:38
  31.9 46.1 %collective-permute-start.3 = (bf16[64,4096]{1,0:T(8,128)(2,1)}, bf16[64,4096]{1,0:T(8,128)(2,1)S(1)}, u32[]{:S(2)}, u32[]{:S(2)}) collective-permute-start(bf16[64,4096]{1,0:T(8,128)(2,1)} %copy-done.25), channel_id=1, source_target_pairs={{0,2},{2,0},{4,6},{6,4},{8,10},{10,8},{12,14},{14,12},{16,18},{18,... | collective-permute-start | bytes 1572872 | tf_op jit(solution)/shard_map/ppermute | solution.py:38
  34.5 43.7 %collective-permute-start.4 = (bf16[64,4096]{1,0:T(8,128)(2,1)}, bf16[64,4096]{1,0:T(8,128)(2,1)S(1)}, u32[]{:S(2)}, u32[]{:S(2)}) collective-permute-start(bf16[64,4096]{1,0:T(8,128)(2,1)} %copy-done.24), channel_id=1, source_target_pairs={{0,24},{2,26},{4,12},{6,14},{8,0},{10,2},{12,20},{14,22},{16,8},{1... | collective-permute-start | bytes 1572872 | tf_op jit(solution)/shard_map/ppermute | solution.py:38
  45.8 34.1 %collective-permute-start.5 = (bf16[64,4096]{1,0:T(8,128)(2,1)}, bf16[64,4096]{1,0:T(8,128)(2,1)S(1)}, u32[]{:S(2)}, u32[]{:S(2)}) collective-permute-start(bf16[64,4096]{1,0:T(8,128)(2,1)} %copy-done.23), channel_id=1, source_target_pairs={{0,26},{2,0},{4,6},{6,12},{8,2},{10,8},{12,14},{14,20},{16,10},{18... | collective-permute-start | bytes 1572872 | tf_op jit(solution)/shard_map/ppermute | solution.py:38
  51.0 31.0 %copy-start.3 = (bf16[128,4096]{1,0:T(8,128)(2,1)S(1)}, bf16[128,4096]{1,0:T(8,128)(2,1)}, u32[]{:S(2)}) copy-start(bf16[128,4096]{1,0:T(8,128)(2,1)} %refs_22_.1) | copy-start | bytes 3145732
  51.0 31.0 %copy-start.7 = (bf16[64,4096]{1,0:T(8,128)(2,1)S(1)}, bf16[64,4096]{1,0:T(8,128)(2,1)}, u32[]{:S(2)}) copy-start(bf16[64,4096]{1,0:T(8,128)(2,1)} %copy-done.6) | copy-start | bytes 1572868
  51.0 31.0 %copy-start.9 = (bf16[64,4096]{1,0:T(8,128)(2,1)S(1)}, bf16[64,4096]{1,0:T(8,128)(2,1)}, u32[]{:S(2)}) copy-start(bf16[64,4096]{1,0:T(8,128)(2,1)} %copy-done.8) | copy-start | bytes 1572868
  54.7 10.5 %collective-permute-start.7 = (f32[32,128]{1,0:T(8,128)S(1)}, f32[32,128]{1,0:T(8,128)S(1)}, u32[]{:S(2)}, u32[]{:S(2)}) collective-permute-start(f32[32,128]{1,0:T(8,128)S(1)} %get-tuple-element.68), channel_id=1, source_target_pairs={{2,0},{0,2},{6,4},{4,6},{10,8},{8,10},{14,12},{12,14},{18,16},{16,... | collective-permute-start | bytes 49160 | tf_op jit(solution)/shard_map/ppermute | solution.py:38
  65.2 5.5 %collective-permute-start.8 = (f32[32,128]{1,0:T(8,128)S(1)}, f32[32,128]{1,0:T(8,128)S(1)}, u32[]{:S(2)}, u32[]{:S(2)}) collective-permute-start(f32[32,128]{1,0:T(8,128)S(1)} %get-tuple-element.69), channel_id=1, source_target_pairs={{24,0},{26,2},{12,4},{14,6},{0,8},{2,10},{20,12},{22,14},{8,16},{1... | collective-permute-start | bytes 49160 | tf_op jit(solution)/shard_map/ppermute | solution.py:38
  70.7 6.4 %collective-permute-start.9 = (f32[32,128]{1,0:T(8,128)S(1)}, f32[32,128]{1,0:T(8,128)S(1)}, u32[]{:S(2)}, u32[]{:S(2)}) collective-permute-start(f32[32,128]{1,0:T(8,128)S(1)} %get-tuple-element.70), channel_id=1, source_target_pairs={{26,0},{0,2},{6,4},{12,6},{2,8},{8,10},{14,12},{20,14},{10,16},{16... | collective-permute-start | bytes 49160 | tf_op jit(solution)/shard_map/ppermute | solution.py:38
  77.9 3.8 %collective-permute-start.10 = (f32[32,128]{1,0:T(8,128)S(1)}, f32[32,128]{1,0:T(8,128)S(1)}, u32[]{:S(2)}, u32[]{:S(2)}) collective-permute-start(f32[32,128]{1,0:T(8,128)S(1)} %get-tuple-element.73), channel_id=1, source_target_pairs={{0,2},{2,0},{4,6},{6,4},{8,10},{10,8},{12,14},{14,12},{16,18},{18,... | collective-permute-start | bytes 49160 | tf_op jit(solution)/shard_map/ppermute | solution.py:38
  77.9 3.8 %collective-permute-start.11 = (f32[32,128]{1,0:T(8,128)S(1)}, f32[32,128]{1,0:T(8,128)S(1)}, u32[]{:S(2)}, u32[]{:S(2)}) collective-permute-start(f32[32,128]{1,0:T(8,128)S(1)} %get-tuple-element.74), channel_id=1, source_target_pairs={{0,24},{2,26},{4,12},{6,14},{8,0},{10,2},{12,20},{14,22},{16,8},{1... | collective-permute-start | bytes 49160 | tf_op jit(solution)/shard_map/ppermute | solution.py:38
  78.2 3.7 %collective-permute-start.12 = (f32[32,128]{1,0:T(8,128)S(1)}, f32[32,128]{1,0:T(8,128)S(1)}, u32[]{:S(2)}, u32[]{:S(2)}) collective-permute-start(f32[32,128]{1,0:T(8,128)S(1)} %get-tuple-element.75), channel_id=1, source_target_pairs={{0,26},{2,0},{4,6},{6,12},{8,2},{10,8},{12,14},{14,20},{16,10},{18... | collective-permute-start | bytes 49160 | tf_op jit(solution)/shard_map/ppermute | solution.py:38
  97.0 1.4 copy-start.4
  98.4 33.7 %copy-start.15 = (bf16[64,4096]{1,0:T(8,128)(2,1)}, bf16[64,4096]{1,0:T(8,128)(2,1)S(1)}, u32[]{:S(2)}) copy-start(bf16[64,4096]{1,0:T(8,128)(2,1)S(1)} %get-tuple-element.76.refs_0_) | copy-start | bytes 1572868
  98.4 33.7 %copy-start.17 = (bf16[64,4096]{1,0:T(8,128)(2,1)}, bf16[64,4096]{1,0:T(8,128)(2,1)S(1)}, u32[]{:S(2)}) copy-start(bf16[64,4096]{1,0:T(8,128)(2,1)S(1)} %get-tuple-element.77.refs_1_) | copy-start | bytes 1572868
  98.4 4.7 %collective-permute-start.18 = (f32[32,128]{1,0:T(8,128)S(1)}, f32[32,128]{1,0:T(8,128)S(1)}, u32[]{:S(2)}, u32[]{:S(2)}) collective-permute-start(f32[32,128]{1,0:T(8,128)S(1)} %get-tuple-element.86), channel_id=1, source_target_pairs={{2,0},{0,2},{6,4},{4,6},{10,8},{8,10},{14,12},{12,14},{18,16},{16,... | collective-permute-start | bytes 49160 | tf_op jit(solution)/shard_map/ppermute | solution.py:38
  101.0 5.5 %collective-permute-start.19 = (f32[32,128]{1,0:T(8,128)S(1)}, f32[32,128]{1,0:T(8,128)S(1)}, u32[]{:S(2)}, u32[]{:S(2)}) collective-permute-start(f32[32,128]{1,0:T(8,128)S(1)} %get-tuple-element.87), channel_id=1, source_target_pairs={{24,0},{26,2},{12,4},{14,6},{0,8},{2,10},{20,12},{22,14},{8,16},{1... | collective-permute-start | bytes 49160 | tf_op jit(solution)/shard_map/ppermute | solution.py:38
  103.0 6.4 %collective-permute-start.20 = (f32[32,128]{1,0:T(8,128)S(1)}, f32[32,128]{1,0:T(8,128)S(1)}, u32[]{:S(2)}, u32[]{:S(2)}) collective-permute-start(f32[32,128]{1,0:T(8,128)S(1)} %get-tuple-element.88), channel_id=1, source_target_pairs={{26,0},{0,2},{6,4},{12,6},{2,8},{8,10},{14,12},{20,14},{10,16},{16... | collective-permute-start | bytes 49160 | tf_op jit(solution)/shard_map/ppermute | solution.py:38
  110.0 3.8 %collective-permute-start.21 = (f32[32,128]{1,0:T(8,128)S(1)}, f32[32,128]{1,0:T(8,128)S(1)}, u32[]{:S(2)}, u32[]{:S(2)}) collective-permute-start(f32[32,128]{1,0:T(8,128)S(1)} %get-tuple-element.91), channel_id=1, source_target_pairs={{0,2},{2,0},{4,6},{6,4},{8,10},{10,8},{12,14},{14,12},{16,18},{18,... | collective-permute-start | bytes 49160 | tf_op jit(solution)/shard_map/ppermute | solution.py:38
  110.1 3.8 %collective-permute-start.22 = (f32[32,128]{1,0:T(8,128)S(1)}, f32[32,128]{1,0:T(8,128)S(1)}, u32[]{:S(2)}, u32[]{:S(2)}) collective-permute-start(f32[32,128]{1,0:T(8,128)S(1)} %get-tuple-element.92), channel_id=1, source_target_pairs={{0,24},{2,26},{4,12},{6,14},{8,0},{10,2},{12,20},{14,22},{16,8},{1... | collective-permute-start | bytes 49160 | tf_op jit(solution)/shard_map/ppermute | solution.py:38
  110.4 3.7 %collective-permute-start.23 = (f32[32,128]{1,0:T(8,128)S(1)}, f32[32,128]{1,0:T(8,128)S(1)}, u32[]{:S(2)}, u32[]{:S(2)}) collective-permute-start(f32[32,128]{1,0:T(8,128)S(1)} %get-tuple-element.93), channel_id=1, source_target_pairs={{0,26},{2,0},{4,6},{6,12},{8,2},{10,8},{12,14},{14,20},{16,10},{18... | collective-permute-start | bytes 49160 | tf_op jit(solution)/shard_map/ppermute | solution.py:38
  114.1 49.4 %copy-start.20 = (f32[4096]{0:T(1024)S(1)}, f32[4096]{0:T(1024)}, u32[]{:S(2)}) copy-start(f32[4096]{0:T(1024)} %param.7) | copy-start | bytes 49156
  132.1 1.3 copy-start.10
  133.4 43.9 %copy-start.5 = (f32[128,4096]{1,0:T(8,128)S(1)}, f32[128,4096]{1,0:T(8,128)}, u32[]{:S(2)}) copy-start(f32[128,4096]{1,0:T(8,128)} %copy-done.4) | copy-start | bytes 6291460
  133.4 22.9 %collective-permute-start.24 = (bf16[64,4096]{1,0:T(8,128)(2,1)S(1)}, bf16[64,4096]{1,0:T(8,128)(2,1)S(1)}, u32[]{:S(2)}, u32[]{:S(2)}) collective-permute-start(bf16[64,4096]{1,0:T(8,128)(2,1)S(1)} %get-tuple-element.96), channel_id=1, source_target_pairs={{2,0},{0,2},{6,4},{4,6},{10,8},{8,10},{14,12},{12,14},{18,16},{16,... | collective-permute-start | bytes 1572872 | tf_op jit(solution)/shard_map/ppermute | solution.py:38
  136.1 20.2 %collective-permute-start.25 = (bf16[64,4096]{1,0:T(8,128)(2,1)S(1)}, bf16[64,4096]{1,0:T(8,128)(2,1)S(1)}, u32[]{:S(2)}, u32[]{:S(2)}) collective-permute-start(bf16[64,4096]{1,0:T(8,128)(2,1)S(1)} %get-tuple-element.97), channel_id=1, source_target_pairs={{24,0},{26,2},{12,4},{14,6},{0,8},{2,10},{20,12},{22,14},{8,16},{1... | collective-permute-start | bytes 1572872 | tf_op jit(solution)/shard_map/ppermute | solution.py:38
  138.1 25.5 %collective-permute-start.26 = (bf16[64,4096]{1,0:T(8,128)(2,1)S(1)}, bf16[64,4096]{1,0:T(8,128)(2,1)S(1)}, u32[]{:S(2)}, u32[]{:S(2)}) collective-permute-start(bf16[64,4096]{1,0:T(8,128)(2,1)S(1)} %get-tuple-element.98), channel_id=1, source_target_pairs={{26,0},{0,2},{6,4},{12,6},{2,8},{8,10},{14,12},{20,14},{10,16},{16... | collective-permute-start | bytes 1572872 | tf_op jit(solution)/shard_map/ppermute | solution.py:38
  138.1 39.2 %collective-permute-start.17 = (bf16[128,4096]{1,0:T(8,128)(2,1)}, bf16[128,4096]{1,0:T(8,128)(2,1)}, u32[]{:S(2)}, u32[]{:S(2)}) collective-permute-start(bf16[128,4096]{1,0:T(8,128)(2,1)} %get-tuple-element.82), channel_id=1, source_target_pairs={{0,4},{2,6},{4,0},{6,2},{8,12},{10,14},{12,8},{14,10},{16,20},{18,... | collective-permute-start | bytes 3145736 | tf_op jit(solution)/shard_map/ppermute | solution.py:38
  143.1 41.0 %collective-permute-start.27 = (bf16[128,4096]{1,0:T(8,128)(2,1)}, bf16[128,4096]{1,0:T(8,128)(2,1)}, u32[]{:S(2)}, u32[]{:S(2)}) collective-permute-start(bf16[128,4096]{1,0:T(8,128)(2,1)} %get-tuple-element.102), channel_id=1, source_target_pairs={{0,4},{2,6},{4,0},{6,2},{8,12},{10,14},{12,8},{14,10},{16,20},{18,... | collective-permute-start | bytes 3145736 | tf_op jit(solution)/shard_map/ppermute | solution.py:38
  156.4 15.3 %collective-permute-start.14 = (bf16[64,4096]{1,0:T(8,128)(2,1)}, bf16[64,4096]{1,0:T(8,128)(2,1)}, u32[]{:S(2)}, u32[]{:S(2)}) collective-permute-start(bf16[64,4096]{1,0:T(8,128)(2,1)} %get-tuple-element.78), channel_id=1, source_target_pairs={{2,0},{0,2},{6,4},{4,6},{10,8},{8,10},{14,12},{12,14},{18,16},{16,... | collective-permute-start | bytes 1572872 | tf_op jit(solution)/shard_map/ppermute | solution.py:38
  156.4 15.3 %collective-permute-start.15 = (bf16[64,4096]{1,0:T(8,128)(2,1)}, bf16[64,4096]{1,0:T(8,128)(2,1)}, u32[]{:S(2)}, u32[]{:S(2)}) collective-permute-start(bf16[64,4096]{1,0:T(8,128)(2,1)} %get-tuple-element.79), channel_id=1, source_target_pairs={{24,0},{26,2},{12,4},{14,6},{0,8},{2,10},{20,12},{22,14},{8,16},{1... | collective-permute-start | bytes 1572872 | tf_op jit(solution)/shard_map/ppermute | solution.py:38
  163.6 13.7 %collective-permute-start.16 = (bf16[64,4096]{1,0:T(8,128)(2,1)}, bf16[64,4096]{1,0:T(8,128)(2,1)}, u32[]{:S(2)}, u32[]{:S(2)}) collective-permute-start(bf16[64,4096]{1,0:T(8,128)(2,1)} %get-tuple-element.80), channel_id=1, source_target_pairs={{26,0},{0,2},{6,4},{12,6},{2,8},{8,10},{14,12},{20,14},{10,16},{16... | collective-permute-start | bytes 1572872 | tf_op jit(solution)/shard_map/ppermute | solution.py:38
  166.2 1.4 copy-start.12
  177.3 1.0 copy-start.16
  178.4 1.0 copy-start.18
  179.4 4.7 %copy-start.11 = (f32[128,4096]{1,0:T(8,128)S(1)}, f32[128,4096]{1,0:T(8,128)}, u32[]{:S(2)}) copy-start(f32[128,4096]{1,0:T(8,128)} %copy-done.10) | copy-start | bytes 6291460
  179.4 4.7 %copy-start.13 = (f32[128,4096]{1,0:T(8,128)S(1)}, f32[128,4096]{1,0:T(8,128)}, u32[]{:S(2)}) copy-start(f32[128,4096]{1,0:T(8,128)} %copy-done.12) | copy-start | bytes 6291460
where the time goes:
time: 189 us; the launch traced here: 188 us
  waiting for transfers between devices  74.4 us (39%)
  Pallas kernels  52.3 us (28%)
  starting transfers between devices  41.8 us (22%)
  local copies, waits for them, and re-layouts  14 us (7%)
  blocking collectives  4.89 us (3%)
    ppermute x28, waiting for transfers between devices, sent(): return lax.ppermute(array, 'dp', route)  74.4 us
    ppermute x28, starting transfers between devices, sent(): return lax.ppermute(array, 'dp', route)  41.8 us
    pallas_call x1, Pallas kernels, local(): kernel_call(gradient_kernel, 'gradient', steps, [slot] * (2 * SLOTS) + [s...  17.9 us
    pallas_call x1, Pallas kernels, local(): kernel_call(context_kernel, 'context', steps, [slot] * (2 * SLOTS) + [sta...  15 us
    unnamed x52, local copies, waits for them, and re-layouts  14 us
    pallas_call x1, Pallas kernels, local(): kernel_call(with_place(attended_kernel), 'attended', steps, [scalars] * 2...  4.67 us
    pallas_call x1, Pallas kernels, local(): kernel_call(finish_kernel, 'finish', steps, [tall, tall, row, row, tall,...  4.04 us
  transfers between devices with their start and end apart: 28, of which 18 were waited for; matrix products, arithmetic and copies ran while one was open for 0% of the time, Pallas kernels for 8%

commit v1 on v0

v1 whole, which is shorter than its diff:
```python
import functools

import jax
import jax.numpy as jnp
from jax import lax
from jax.experimental import pallas as pl
from jax.experimental.pallas import tpu as pltpu
from jax.sharding import PartitionSpec as P

HEADS = 64
HS = 128
GROUP = 64
FEAT = HEADS * HS
EPSILON = 1e-06
SCALING = 1.0 / HS**0.5
LANES = 128
CHUNK = 8
VMEM_LIMIT = 16 * 1024 * 1024
SLOTS = 5
OWN = (0, 2)
PARTNER = (1, 3, 4)


def routes(count):
    def side(i):
        return -4 if i & 2 == 0 else 4

    diagonal = (-3, -1, 1, 3)
    return {
        "y": [(i, i ^ 2) for i in range(count)],
        2: [(i, i ^ 1) for i in range(count)],
        3: [(i, (i + side(i)) % count) for i in range(count)],
        4: [(i, (i + diagonal[i & 3]) % count) for i in range(count)],
    }


def sent(array, route):
    return lax.ppermute(array, "dp", route)


def out_and_back(count):
    route = routes(count)
    back = {s: [(b, a) for a, b in route[s]] for s in (2, 3, 4)}

    return route, back, functools.partial(sent, route=route["y"])


def dot(a, b, left, right):
    return lax.dot_general(a, b, (((left,), (right,)), ((), ())), preferred_element_type=jnp.float32)


def group_numbers(place_ref, near_ref, count, groups):
    place = place_ref[0]
    one = 1 - 2 * (place & 1)
    two = 2 - 2 * (place & 2)
    numbers = []
    for offset in (0, two, one, -two, -one):
        block = lax.rem(place + offset + count, count)
        number = jnp.int32(-1)
        for g in range(groups):
            used = (near_ref[g, 0] == block) | (near_ref[g, 1] == block)
            number = jnp.where(used, g, number)
        numbers.append(number)
    return numbers


def rows_of(number):
    return pl.ds(pl.multiple_of(jnp.maximum(number, 0) * GROUP, GROUP), GROUP)


def to_row(x):
    return jnp.sum(x.T, axis=0, keepdims=True)


def to_columns(row):
    return jnp.broadcast_to(row, (row.shape[1], row.shape[1])).T


def tile(t):
    return slice(t * LANES, (t + 1) * LANES)


def squares_kernel(q_ref, squares_ref):
    x = q_ref[:, tile(0)].astype(jnp.float32)
    total = x * x
    for t in range(1, q_ref.shape[1] // LANES):
        x = q_ref[:, tile(t)].astype(jnp.float32)
        total = total + x * x
    squares_ref[...] = to_row(total)


def prepare_grads_kernel(count, groups, place_ref, near_ref, g_ref, *slot_refs):
    numbers = group_numbers(place_ref, near_ref, count, groups)
    for s in range(SLOTS):
        slot_refs[s][...] = g_ref[rows_of(numbers[s])]


def inverse_columns(squares_ref):
    return to_columns(lax.rsqrt(squares_ref[...] / FEAT + EPSILON))


def prepare_queries_kernel(count, groups, place_ref, near_ref, q_ref, gain_ref, squares_ref, *refs):
    slot_refs, normed_ref = refs[:SLOTS], refs[SLOTS]
    numbers = group_numbers(place_ref, near_ref, count, groups)
    inverse = inverse_columns(squares_ref)
    for t in range(q_ref.shape[1] // LANES):
        x = q_ref[:, tile(t)].astype(jnp.float32)
        normed_ref[:, tile(t)] = (x * gain_ref[:, tile(t)] * inverse).astype(jnp.bfloat16)
    for s in range(SLOTS):
        slot_refs[s][...] = normed_ref[rows_of(numbers[s])]


def head(refs, slots, cols):
    return jnp.concatenate([refs[s][:, cols] for s in slots], axis=0)


def each_chunk(heads, unit, body):
    def step(i, carry):
        first = i * unit
        cols = [pl.ds(pl.multiple_of((first + h) * HS, HS), HS) for h in range(unit)]
        body(pl.ds(pl.multiple_of(first, unit), unit), cols)
        return carry

    lax.fori_loop(0, heads // unit, step, 0)


def scores_kernel(*refs):
    q_refs, k_refs, stat_refs = refs[:SLOTS], refs[SLOTS : SLOTS + 2], refs[SLOTS + 2 :]

    def body(rows, cols):
        for slots, k_ref in zip((OWN, PARTNER), k_refs):
            scores = [dot(k_ref[:, c], head(q_refs, slots, c), 1, 1) * SCALING for c in cols]
            tops = [jnp.max(x, axis=0, keepdims=True) for x in scores]
            totals = [
                jnp.sum(jnp.exp(x - top), axis=0, keepdims=True) for x, top in zip(scores, tops)
            ]
            tops = jnp.concatenate(tops, axis=0)
            totals = jnp.concatenate(totals, axis=0)
            for at, s in enumerate(slots):
                lanes = slice(at * GROUP, (at + 1) * GROUP)
                stat_refs[s][rows] = jnp.concatenate([tops[:, lanes], totals[:, lanes]], axis=1)

    each_chunk(stat_refs[0].shape[0], CHUNK, body)


def combine_scores_kernel(count, groups, place_ref, near_ref, *refs):
    stat_refs, back_refs = refs[:SLOTS], refs[SLOTS:]
    numbers = group_numbers(place_ref, near_ref, count, groups)
    heads = stat_refs[0].shape[0]
    shape = (heads, GROUP)
    tops = [r[:, 0:GROUP] for r in stat_refs]
    totals = [r[:, GROUP : 2 * GROUP] for r in stat_refs]
    number_of = [jnp.full(shape, n, jnp.int32) for n in numbers]
    lowest = jnp.full(shape, -jnp.inf, jnp.float32)
    zero = jnp.zeros(shape, jnp.float32)
    merged = []
    for g in range(groups):
        top, total = lowest, zero
        for s in range(SLOTS):
            top = jnp.maximum(top, jnp.where(number_of[s] == g, tops[s], lowest))
        for s in range(SLOTS):
            mine = number_of[s] == g
            factor = jnp.exp(jnp.where(mine, tops[s] - top, zero))
            total = total + jnp.where(mine, totals[s] * factor, zero)
        merged.append((top, 1.0 / total))
    for s in range(SLOTS):
        top, inv = tops[s], zero
        for g in range(groups):
            mine = number_of[s] == g
            top = jnp.where(mine, merged[g][0], top)
            inv = jnp.where(mine, merged[g][1], inv)
        back_refs[s][...] = jnp.concatenate([top, inv], axis=1)


def combine_centres_kernel(count, groups, place_ref, near_ref, *refs):
    stat_refs, back_refs = refs[:SLOTS], refs[SLOTS:]
    numbers = group_numbers(place_ref, near_ref, count, groups)
    shape = stat_refs[0].shape
    number_of = [jnp.full(shape, n, jnp.int32) for n in numbers]
    zero = jnp.zeros(shape, jnp.float32)
    totals = []
    for g in range(groups):
        total = zero
        for s in range(SLOTS):
            total = total + jnp.where(number_of[s] == g, stat_refs[s][...], zero)
        totals.append(total)
    for s in range(SLOTS):
        here = zero
        for g in range(groups):
            here = jnp.where(number_of[s] == g, totals[g], here)
        back_refs[s][...] = here


def stat_rows(stat_refs, slots, rows, half):
    lanes = slice(half * GROUP, (half + 1) * GROUP)
    return jnp.concatenate([stat_refs[s][rows, lanes] for s in slots], axis=1)


def units(rows, slots, back_refs, q_refs, k_ref, cols):
    top, inv = stat_rows(back_refs, slots, rows, 0), stat_rows(back_refs, slots, rows, 1)
    scores = [dot(k_ref[:, c], head(q_refs, slots, c), 1, 1) for c in cols]
    return [
        jnp.exp(x * SCALING - top[h : h + 1]) * inv[h : h + 1] for h, x in enumerate(scores)
    ]


def context_kernel(*refs):
    q_refs, g_refs, back_refs = (refs[i * SLOTS : (i + 1) * SLOTS] for i in range(3))
    k_refs, v_refs = refs[3 * SLOTS : 3 * SLOTS + 2], refs[3 * SLOTS + 2 : 3 * SLOTS + 4]
    rest = refs[3 * SLOTS + 4 :]
    ctx_refs, centre_refs, dv_ref = rest[:SLOTS], rest[SLOTS : 2 * SLOTS], rest[2 * SLOTS]

    def body(rows, cols):
        work = []
        for slots, k_ref, v_ref in zip((OWN, PARTNER), k_refs, v_refs):
            probs = units(rows, slots, back_refs, q_refs, k_ref, cols)
            work.append((slots, v_ref, probs))
        for slots, v_ref, probs in work:
            centres = []
            for c, p in zip(cols, probs):
                low, g, v = p.astype(jnp.bfloat16), head(g_refs, slots, c), v_ref[:, c]
                context = dot(low, v, 0, 0).astype(jnp.bfloat16)
                for at, s in enumerate(slots):
                    ctx_refs[s][:, c] = context[at * GROUP : (at + 1) * GROUP]
                centres.append(jnp.sum(p * dot(v, g, 1, 1), axis=0, keepdims=True))
                if slots is PARTNER:
                    dv_ref[:, c] = dot(low, g, 1, 0).astype(jnp.bfloat16)
            centres = jnp.concatenate(centres, axis=0)
            empty = jnp.zeros((centres.shape[0], GROUP), jnp.float32)
            for at, s in enumerate(slots):
                lanes = slice(at * GROUP, (at + 1) * GROUP)
                centre_refs[s][rows] = jnp.concatenate([centres[:, lanes], empty], axis=1)

    each_chunk(centre_refs[0].shape[0], CHUNK, body)


def gradient_kernel(*refs):
    q_refs, g_refs, back_refs, centre_refs = (refs[i * SLOTS : (i + 1) * SLOTS] for i in range(4))
    k_refs, v_refs = refs[4 * SLOTS : 4 * SLOTS + 2], refs[4 * SLOTS + 2 : 4 * SLOTS + 4]
    rest = refs[4 * SLOTS + 4 :]
    grad_refs, dk_ref = rest[:SLOTS], rest[SLOTS]

    def body(rows, cols):
        work = []
        for slots, k_ref, v_ref in zip((OWN, PARTNER), k_refs, v_refs):
            probs = units(rows, slots, back_refs, q_refs, k_ref, cols)
            centre = stat_rows(centre_refs, slots, rows, 0)
            products = [dot(v_ref[:, c], head(g_refs, slots, c), 1, 1) for c in cols]
            lows = [
                (p * (x - centre[h : h + 1])).astype(jnp.bfloat16)
                for h, (p, x) in enumerate(zip(probs, products))
            ]
            work.append((slots, k_ref, lows))
        for slots, k_ref, lows in work:
            for c, low in zip(cols, lows):
                grad = (dot(low, k_ref[:, c], 0, 0) * SCALING).astype(jnp.bfloat16)
                for at, s in enumerate(slots):
                    grad_refs[s][:, c] = grad[at * GROUP : (at + 1) * GROUP]
                if slots is PARTNER:
                    product = dot(low, head(q_refs, slots, c), 1, 0) * SCALING
                    dk_ref[:, c] = product.astype(jnp.bfloat16)

    each_chunk(back_refs[0].shape[0], CHUNK, body)


def own_kernel(*refs):
    pairs = [dict(zip(OWN, refs[i * 2 : i * 2 + 2])) for i in range(4)]
    q_refs, g_refs, back_refs, centre_refs = pairs
    k_ref, v_ref, far_ref, dv_ref, dk_ref = refs[8:]

    def body(rows, cols):
        probs = units(rows, OWN, back_refs, q_refs, k_ref, cols)
        centre = stat_rows(centre_refs, OWN, rows, 0)
        grads = [head(g_refs, OWN, c) for c in cols]
        products = [dot(v_ref[:, c], g, 1, 1) for c, g in zip(cols, grads)]
        for h, (c, p, g, x) in enumerate(zip(cols, probs, grads, products)):
            total = dot(p.astype(jnp.bfloat16), g, 1, 0) + far_ref[:, c].astype(jnp.float32)
            dv_ref[:, c] = total.astype(jnp.bfloat16)
            low = (p * (x - centre[h : h + 1])).astype(jnp.bfloat16)
            dk_ref[:, c] = dot(low, head(q_refs, OWN, c), 1, 0) * SCALING

    each_chunk(back_refs[0].shape[0], CHUNK, body)


def gathered(weights, refs, t):
    total = None
    for s in range(SLOTS):
        part = weights[s] * refs[s][:, tile(t)].astype(jnp.float32)
        total = part if total is None else total + part
    return total


def weights_of(numbers, g):
    return [jnp.where(n == g, 1.0, 0.0) for n in numbers]


def attended_kernel(count, groups, place_ref, near_ref, *refs):
    ctx_refs, out_ref = refs[:SLOTS], refs[SLOTS]
    numbers = group_numbers(place_ref, near_ref, count, groups)
    for g in range(groups):
        weights = weights_of(numbers, g)
        rows = slice(g * GROUP, (g + 1) * GROUP)
        for t in range(out_ref.shape[1] // LANES):
            out_ref[rows, tile(t)] = gathered(weights, ctx_refs, t).astype(jnp.bfloat16)


def inner_kernel(count, groups, place_ref, near_ref, *refs):
    grad_refs = refs[:SLOTS]
    q_ref, gain_ref, scaled_ref, inner_ref = refs[SLOTS:]
    numbers = group_numbers(place_ref, near_ref, count, groups)
    totals = []
    for g in range(groups):
        weights = weights_of(numbers, g)
        rows = slice(g * GROUP, (g + 1) * GROUP)
        total = jnp.zeros((GROUP, LANES), jnp.float32)
        for t in range(q_ref.shape[1] // LANES):
            scaled = gathered(weights, grad_refs, t) * gain_ref[:, tile(t)]
            scaled_ref[rows, tile(t)] = scaled
            total = total + scaled * q_ref[rows, tile(t)].astype(jnp.float32)
        totals.append(total)
    inner_ref[...] = to_row(jnp.concatenate(totals, axis=0))


def finish_kernel(scaled_ref, q_ref, squares_ref, inner_ref, dq_ref):
    inverse = inverse_columns(squares_ref)
    factor = inverse * inverse * inverse * to_columns(inner_ref[...]) / FEAT
    for t in range(q_ref.shape[1] // LANES):
        x = q_ref[:, tile(t)].astype(jnp.float32)
        dq_ref[:, tile(t)] = (inverse * scaled_ref[:, tile(t)] - x * factor).astype(jnp.bfloat16)


def in_vmem(array):
    return pltpu.with_memory_space_constraint(array, pltpu.VMEM)


def after(values, *tokens):
    return lax.optimization_barrier((values, tokens))[0]


def kernel_call(body, name, outs, scratch=(), scalars=0, last=()):
    vmem = pl.BlockSpec(memory_space=pltpu.VMEM)

    def call(*args):
        small, large = args[:scalars], [in_vmem(a) for a in args[scalars:]]
        shapes = [
            (jax.ShapeDtypeStruct if i in last else pltpu.VMEM)(shape, dtype)
            for i, (shape, dtype) in enumerate(outs)
        ]
        results = pl.pallas_call(
            body,
            in_specs=[pl.BlockSpec(memory_space=pltpu.SMEM)] * scalars + [vmem] * len(large),
            out_specs=[vmem] * len(outs),
            out_shape=shapes,
            scratch_shapes=list(scratch),
            name=name,
            cost_estimate=pl.CostEstimate(flops=0, bytes_accessed=0, transcendentals=0),
            compiler_params=pltpu.CompilerParams(vmem_limit_bytes=VMEM_LIMIT),
        )(*small, *large)
        return list(results)

    return call


def local(queries, query_gain, keys, values, neighbours, d_out):
    rows, width = queries.shape
    heads = width // HS
    groups = rows // GROUP
    count = lax.axis_size("dp")
    route, back_route, across = out_and_back(count)
    place = jnp.full((1,), lax.axis_index("dp"), jnp.int32)
    gain = query_gain[None, :]

    slot = ((GROUP, width), jnp.bfloat16)
    tall = ((rows, width), jnp.bfloat16)
    tall_wide = ((rows, width), jnp.float32)
    row = ((1, rows), jnp.float32)
    stat = ((heads, LANES), jnp.float32)

    def go(parts):
        return [sent(p, route[s]) if s >= 2 else p for s, p in enumerate(parts)]

    def come(parts):
        return [sent(p, back_route[s]) if s >= 2 else p for s, p in enumerate(parts)]

    def placed(kernel, name, outs, scratch=(), last=()):
        call = kernel_call(
            functools.partial(kernel, count, groups), name, outs, scratch, 2, last
        )
        return functools.partial(call, place, neighbours)

    far_keys = across(keys)
    far_values = across(values)
    (squares,) = kernel_call(squares_kernel, "squares", [row])(queries)
    squares = lax.psum(squares, "mp")
    q_parts = placed(
        prepare_queries_kernel, "prepare_queries", [slot] * SLOTS, [pltpu.VMEM(*tall)]
    )(queries, gain, squares)
    q_slots = go(q_parts)
    g_parts = placed(prepare_grads_kernel, "prepare_grads", [slot] * SLOTS)(
        after(d_out, q_parts[0])
    )

    stats = kernel_call(scores_kernel, "scores", [stat] * SLOTS)(*q_slots, keys, far_keys)
    stats = come(stats)
    g_parts[4] = after(g_parts[4], *stats[2:])
    g_slots = go(g_parts)
    back = placed(combine_scores_kernel, "combine_scores", [stat] * SLOTS)(*stats)
    back = go(back)

    *outs, far_dv = kernel_call(
        context_kernel, "context", [slot] * SLOTS + [stat] * SLOTS + [tall]
    )(*q_slots, *g_slots, *back, keys, far_keys, values, far_values)
    contexts, centres = outs[:SLOTS], outs[SLOTS:]
    centres = come(centres)
    far_dv = across(far_dv)
    centres = placed(combine_centres_kernel, "combine_centres", [stat] * SLOTS)(*centres)
    centres = go(centres)
    contexts[4] = after(contexts[4], *centres[2:])
    contexts = come(contexts)

    *grads, far_dk = kernel_call(gradient_kernel, "gradient", [slot] * SLOTS + [tall])(
        *q_slots, *g_slots, *back, *centres, keys, far_keys, values, far_values
    )
    own = [part[s] for part in (q_slots, g_slots, back, centres) for s in OWN]
    own[0] = after(own[0], far_dk)
    far_dk = across(far_dk)
    grads = come(grads)

    d_values, own_dk = kernel_call(own_kernel, "own", [tall, tall_wide], last=(0,))(
        *own, keys, values, far_dv
    )
    (attended,) = placed(attended_kernel, "attended", [tall], last=(0,))(*contexts)
    grads = after(grads, attended, d_values)
    scaled, inner = placed(inner_kernel, "inner", [tall_wide, row])(*grads, queries, gain)
    inner = lax.psum(inner, "mp")
    (d_queries,) = kernel_call(finish_kernel, "finish", [tall], last=(0,))(
        scaled, queries, squares, inner
    )
    d_keys = (own_dk + far_dk.astype(jnp.float32)).astype(jnp.bfloat16)
    return (attended, d_queries, d_keys, d_values)


def solution(mesh):
    placed = (P("dp", "mp"), P("mp"), P("dp", "mp"), P("dp", "mp"), P("dp", None), P("dp", "mp"))
    return jax.shard_map(
        local,
        mesh=mesh,
        in_specs=placed,
        out_specs=(P("dp", "mp"), P("dp", "mp"), P("dp", "mp"), P("dp", "mp")),
        check_vma=False,
    )
```

time: 189 us -> 145 us (0.77)
  Pallas kernels: 52.3 us -> 29.4 us
  waiting for transfers between devices: 74.4 us -> 58.1 us
  local copies, waits for them, and re-layouts: 14 us -> 5.23 us
  other arithmetic: 0 us -> 2.47 us
    pallas_call x10 -> x12, Pallas kernels: 52.3 us -> 29.4 us  [call(): pl.pallas_call(body, in_specs=[pl.BlockSpec(memory_space=pltpu.SMEM)] * s...]
    ppermute x28, waiting for transfers between devices: 74.4 us -> 58.1 us  [sent(): return lax.ppermute(array, 'dp', route)]
    unnamed x52 -> x24, local copies, waits for them, and re-layouts: 14 us -> 5.23 us
    convert_element_type x0 -> x1, other arithmetic: none -> 2.47 us  [local(): d_keys = (own_dk + far_dk.astype(jnp.float32)).astype(jnp.bfloat16)]
  transfers between devices with their start and end apart: 28 -> 28, of which waited for: 18 -> 14; matrix products, arithmetic and copies ran while one was open for 0% -> 0% of each run, Pallas kernels for 8% -> 16%
where the time goes in v1:
time: 145 us
  waiting for transfers between devices  58.1 us (40%)
  starting transfers between devices  43.6 us (30%)
  Pallas kernels  29.4 us (20%)
  local copies, waits for them, and re-layouts  5.23 us (4%)
  blocking collectives  4.94 us (3%)
  other arithmetic  2.47 us (2%)
    ppermute x28, waiting for transfers between devices, sent(): return lax.ppermute(array, 'dp', route)  58.1 us
    ppermute x28, starting transfers between devices, sent(): return lax.ppermute(array, 'dp', route)  43.6 us
    pallas_call x12, Pallas kernels, call(): pl.pallas_call(body, in_specs=[pl.BlockSpec(memory_space=pltpu.SMEM)] * s...  29.4 us
    unnamed x24, local copies, waits for them, and re-layouts  5.23 us
  transfers between devices with their start and end apart: 28, of which 14 were waited for; matrix products, arithmetic and copies ran while one was open for 0% of the time, Pallas kernels for 16%

profile of v1, /device:TPU:0, one launch (start us, length us, event | category | flops | bytes accessed | tf_op | source)
XLA Modules:
  0.0 144.6 jit_solution(12743041625025429540)
XLA Ops:
  0.6 3.0 %collective-permute-start.5 = (bf16[128,4096]{1,0:T(8,128)(2,1)}, bf16[128,4096]{1,0:T(8,128)(2,1)S(1)}, u32[]{:S(2)}, u32[]{:S(2)}) collective-permute-start(bf16[128,4096]{1,0:T(8,128)(2,1)} %refs_8_.1), channel_id=1, source_target_pairs={{0,4},{2,6},{4,0},{6,2},{8,12},{10,14},{12,8},{14,10},{16,20},{18,... | collective-permute-start | bytes 3145736 | tf_op jit(solution)/shard_map/ppermute | solution.py:38
  3.7 1.2 copy-done
  4.9 0.3 squares.1
  5.2 2.5 %psum.14.squares_ref = f32[1,128]{1,0:T(1,128)S(1)} all-reduce(f32[1,128]{1,0:T(1,128)S(1)} %squares.1), channel_id=1, replica_groups=mesh['dp'=16,'mp'=2] {'mp'}, use_global_device_ids=true, to_apply=%region_0.0 | all-reduce | flops 128 | bytes 1024 | tf_op jit(solution)/shard_map/psum | solution.py:394
  7.7 1.2 copy-done.1
  8.9 0.7 copy-done.8
  9.6 0.7 copy-done.10
  10.3 1.1 prepare_queries.1
  11.4 1.6 %collective-permute-start = (bf16[64,4096]{1,0:T(8,128)(2,1)S(1)}, bf16[64,4096]{1,0:T(8,128)(2,1)S(1)}, u32[]{:S(2)}, u32[]{:S(2)}) collective-permute-start(bf16[64,4096]{1,0:T(8,128)(2,1)S(1)} %get-tuple-element.61), channel_id=1, source_target_pairs={{0,2},{2,0},{4,6},{6,4},{8,10},{10,8},{12,14},{14,12},{16,18},{18,... | collective-permute-start | bytes 1572872 | tf_op jit(solution)/shard_map/ppermute | solution.py:38
  12.9 3.6 %collective-permute-start.1 = (bf16[64,4096]{1,0:T(8,128)(2,1)S(1)}, bf16[64,4096]{1,0:T(8,128)(2,1)S(1)}, u32[]{:S(2)}, u32[]{:S(2)}) collective-permute-start(bf16[64,4096]{1,0:T(8,128)(2,1)S(1)} %get-tuple-element.62), channel_id=1, source_target_pairs={{0,24},{2,26},{4,12},{6,14},{8,0},{10,2},{12,20},{14,22},{16,8},{1... | collective-permute-start | bytes 1572872 | tf_op jit(solution)/shard_map/ppermute | solution.py:38
  16.5 0.4 collective-permute-start.2
  17.0 9.3 %collective-permute-done.refs_2_.refs_1_ = bf16[64,4096]{1,0:T(8,128)(2,1)S(1)} collective-permute-done((bf16[64,4096]{1,0:T(8,128)(2,1)S(1)}, bf16[64,4096]{1,0:T(8,128)(2,1)S(1)}, u32[]{:S(2)}, u32[]{:S(2)}) %collective-permute-start) | collective-permute-done | bytes 524320 | tf_op jit(solution)/shard_map/ppermute | solution.py:38
  26.2 2.6 %collective-permute-done.1.refs_3_ = bf16[64,4096]{1,0:T(8,128)(2,1)S(1)} collective-permute-done((bf16[64,4096]{1,0:T(8,128)(2,1)S(1)}, bf16[64,4096]{1,0:T(8,128)(2,1)S(1)}, u32[]{:S(2)}, u32[]{:S(2)}) %collective-permute-start.1) | collective-permute-done | bytes 524320 | tf_op jit(solution)/shard_map/ppermute | solution.py:38
  28.9 10.1 %collective-permute-done.2.refs_4_ = bf16[64,4096]{1,0:T(8,128)(2,1)S(1)} collective-permute-done((bf16[64,4096]{1,0:T(8,128)(2,1)S(1)}, bf16[64,4096]{1,0:T(8,128)(2,1)S(1)}, u32[]{:S(2)}, u32[]{:S(2)}) %collective-permute-start.2) | collective-permute-done | bytes 524320 | tf_op jit(solution)/shard_map/ppermute | solution.py:38
  39.0 3.4 %scores.1 = (f32[32,128]{1,0:T(8,128)S(1)}, f32[32,128]{1,0:T(8,128)S(1)}, f32[32,128]{1,0:T(8,128)S(1)}, f32[32,128]{1,0:T(8,128)S(1)}, f32[32,128]{1,0:T(8,128)S(1)}) custom-call(bf16[64,4096]{1,0:T(8,128)(2,1)S(1)} %get-tuple-element.103.refs_0_, bf16[64,4096]{1,0:T(8,128)(2,1)S(1)} %get-tuple-element.60.refs_1_, ...), custom_call_target="tpu_custom_call" | custom-call | tf_op jit(solution)/shard_map/scores/pallas_call | solution.py:349
  42.4 0.4 collective-permute-start.6
  42.8 0.7 prepare_grads.1
  43.5 1.7 %collective-permute-start.3 = (bf16[64,4096]{1,0:T(8,128)(2,1)S(1)}, bf16[64,4096]{1,0:T(8,128)(2,1)S(1)}, u32[]{:S(2)}, u32[]{:S(2)}) collective-permute-start(bf16[64,4096]{1,0:T(8,128)(2,1)S(1)} %get-tuple-element.67), channel_id=1, source_target_pairs={{0,2},{2,0},{4,6},{6,4},{8,10},{10,8},{12,14},{14,12},{16,18},{18,... | collective-permute-start | bytes 1572872 | tf_op jit(solution)/shard_map/ppermute | solution.py:38
  45.3 0.0 collective-permute-start.7
  45.3 1.9 %collective-permute-start.8 = (f32[32,128]{1,0:T(8,128)S(1)}, f32[32,128]{1,0:T(8,128)S(1)}, u32[]{:S(2)}, u32[]{:S(2)}) collective-permute-start(f32[32,128]{1,0:T(8,128)S(1)} %get-tuple-element.72), channel_id=1, source_target_pairs={{26,0},{0,2},{6,4},{12,6},{2,8},{8,10},{14,12},{20,14},{10,16},{16... | collective-permute-start | bytes 49160 | tf_op jit(solution)/shard_map/ppermute | solution.py:38
  47.2 0.0 collective-permute-done.6.refs_2_
  47.2 3.8 %collective-permute-start.4 = (bf16[64,4096]{1,0:T(8,128)(2,1)S(1)}, bf16[64,4096]{1,0:T(8,128)(2,1)S(1)}, u32[]{:S(2)}, u32[]{:S(2)}) collective-permute-start(bf16[64,4096]{1,0:T(8,128)(2,1)S(1)} %get-tuple-element.68), channel_id=1, source_target_pairs={{0,24},{2,26},{4,12},{6,14},{8,0},{10,2},{12,20},{14,22},{16,8},{1... | collective-permute-start | bytes 1572872 | tf_op jit(solution)/shard_map/ppermute | solution.py:38
  51.0 0.0 collective-permute-done.7.refs_3_
  51.0 4.7 %collective-permute-done.8.refs_4_ = f32[32,128]{1,0:T(8,128)S(1)} collective-permute-done((f32[32,128]{1,0:T(8,128)S(1)}, f32[32,128]{1,0:T(8,128)S(1)}, u32[]{:S(2)}, u32[]{:S(2)}) %collective-permute-start.8) | collective-permute-done | bytes 16416 | tf_op jit(solution)/shard_map/ppermute | solution.py:38
  55.7 9.6 %collective-permute-start.9 = (bf16[64,4096]{1,0:T(8,128)(2,1)S(1)}, bf16[64,4096]{1,0:T(8,128)(2,1)S(1)}, u32[]{:S(2)}, u32[]{:S(2)}) collective-permute-start(bf16[64,4096]{1,0:T(8,128)(2,1)S(1)} %get-tuple-element.73), channel_id=1, source_target_pairs={{0,26},{2,0},{4,6},{6,12},{8,2},{10,8},{12,14},{14,20},{16,10},{18... | collective-permute-start | bytes 1572872 | tf_op jit(solution)/shard_map/ppermute | solution.py:38
  65.3 0.7 combine_scores.1
  66.1 0.1 collective-permute-start.10
  66.1 2.3 %collective-permute-start.11 = (f32[32,128]{1,0:T(8,128)S(1)}, f32[32,128]{1,0:T(8,128)S(1)}, u32[]{:S(2)}, u32[]{:S(2)}) collective-permute-start(f32[32,128]{1,0:T(8,128)S(1)} %get-tuple-element.79), channel_id=1, source_target_pairs={{0,24},{2,26},{4,12},{6,14},{8,0},{10,2},{12,20},{14,22},{16,8},{1... | collective-permute-start | bytes 49160 | tf_op jit(solution)/shard_map/ppermute | solution.py:38
  68.4 0.0 collective-permute-done.4.refs_8_
  68.4 0.0 collective-permute-start.12
  68.4 0.0 collective-permute-done.13.refs_18_.refs_23_
  68.4 1.4 collective-permute-done.10.refs_12_.refs_5_
  69.9 2.5 %collective-permute-done.11.refs_13_ = f32[32,128]{1,0:T(8,128)S(1)} collective-permute-done((f32[32,128]{1,0:T(8,128)S(1)}, f32[32,128]{1,0:T(8,128)S(1)}, u32[]{:S(2)}, u32[]{:S(2)}) %collective-permute-start.11) | collective-permute-done | bytes 16416 | tf_op jit(solution)/shard_map/ppermute | solution.py:38
  72.3 0.2 collective-permute-done.12.refs_14_
  72.5 0.0 collective-permute-done.9.refs_9_
  72.5 6.0 %context.1 = (bf16[64,4096]{1,0:T(8,128)(2,1)S(1)}, bf16[64,4096]{1,0:T(8,128)(2,1)S(1)}, bf16[64,4096]{1,0:T(8,128)(2,1)S(1)}, bf16[64,4096]{1,0:T(8,128)(2,1)S...) custom-call(bf16[64,4096]{1,0:T(8,128)(2,1)S(1)} %get-tuple-element., ...), custom_call_target="tpu_custom_call" | custom-call | tf_op jit(solution)/shard_map/context/pallas_call | solution.py:349
  78.5 0.7 collective-permute-start.16
  79.1 2.6 %collective-permute-start.17 = (f32[32,128]{1,0:T(8,128)S(1)}, f32[32,128]{1,0:T(8,128)S(1)}, u32[]{:S(2)}, u32[]{:S(2)}) collective-permute-start(f32[32,128]{1,0:T(8,128)S(1)} %get-tuple-element.89), channel_id=1, source_target_pairs={{24,0},{26,2},{12,4},{14,6},{0,8},{2,10},{20,12},{22,14},{8,16},{1... | collective-permute-start | bytes 49160 | tf_op jit(solution)/shard_map/ppermute | solution.py:38
  81.7 0.4 collective-permute-start.18
  82.1 0.1 collective-permute-done.16.refs_2_
  82.2 3.7 %collective-permute-done.17.refs_3_ = f32[32,128]{1,0:T(8,128)S(1)} collective-permute-done((f32[32,128]{1,0:T(8,128)S(1)}, f32[32,128]{1,0:T(8,128)S(1)}, u32[]{:S(2)}, u32[]{:S(2)}) %collective-permute-start.17) | collective-permute-done | bytes 16416 | tf_op jit(solution)/shard_map/ppermute | solution.py:38
  86.0 2.3 %collective-permute-done.18.refs_4_ = f32[32,128]{1,0:T(8,128)S(1)} collective-permute-done((f32[32,128]{1,0:T(8,128)S(1)}, f32[32,128]{1,0:T(8,128)S(1)}, u32[]{:S(2)}, u32[]{:S(2)}) %collective-permute-start.18) | collective-permute-done | bytes 16416 | tf_op jit(solution)/shard_map/ppermute | solution.py:38
  88.2 0.6 combine_centres.1
  88.8 0.1 collective-permute-start.19
  88.9 0.8 collective-permute-start.20
  89.7 3.3 %collective-permute-start.21 = (f32[32,128]{1,0:T(8,128)S(1)}, f32[32,128]{1,0:T(8,128)S(1)}, u32[]{:S(2)}, u32[]{:S(2)}) collective-permute-start(f32[32,128]{1,0:T(8,128)S(1)} %get-tuple-element.93), channel_id=1, source_target_pairs={{0,26},{2,0},{4,6},{6,12},{8,2},{10,8},{12,14},{14,20},{16,10},{18... | collective-permute-start | bytes 49160 | tf_op jit(solution)/shard_map/ppermute | solution.py:38
  93.0 0.1 collective-permute-start.15
  93.1 2.7 %collective-permute-start.26 = (bf16[128,4096]{1,0:T(8,128)(2,1)S(1)}, bf16[128,4096]{1,0:T(8,128)(2,1)S(1)}, u32[]{:S(2)}, u32[]{:S(2)}) collective-permute-start(bf16[128,4096]{1,0:T(8,128)(2,1)S(1)} %get-tuple-element.104), channel_id=1, source_target_pairs={{0,4},{2,6},{4,0},{6,2},{8,12},{10,14},{12,8},{14,10},{16,20},{18,... | collective-permute-start | bytes 3145736 | tf_op jit(solution)/shard_map/ppermute | solution.py:38
  95.8 2.3 %collective-permute-start.22 = (bf16[64,4096]{1,0:T(8,128)(2,1)S(1)}, bf16[64,4096]{1,0:T(8,128)(2,1)S(1)}, u32[]{:S(2)}, u32[]{:S(2)}) collective-permute-start(bf16[64,4096]{1,0:T(8,128)(2,1)S(1)} %get-tuple-element.94), channel_id=1, source_target_pairs={{26,0},{0,2},{6,4},{12,6},{2,8},{8,10},{14,12},{20,14},{10,16},{16... | collective-permute-start | bytes 1572872 | tf_op jit(solution)/shard_map/ppermute | solution.py:38
  98.2 6.8 %gradient.1 = (bf16[64,4096]{1,0:T(8,128)(2,1)S(1)}, bf16[64,4096]{1,0:T(8,128)(2,1)S(1)}, bf16[64,4096]{1,0:T(8,128)(2,1)S(1)}, bf16[64,4096]{1,0:T(8,128)(2,1)...) custom-call(bf16[64,4096]{1,0:T(8,128)(2,1)S(1)} %get-tuple-element.103.refs_0_, ...), custom_call_target="tpu_custom_call" | custom-call | tf_op jit(solution)/shard_map/gradient/pallas_call | solution.py:349
  105.0 2.2 %collective-permute-start.27 = (bf16[128,4096]{1,0:T(8,128)(2,1)}, bf16[128,4096]{1,0:T(8,128)(2,1)}, u32[]{:S(2)}, u32[]{:S(2)}) collective-permute-start(bf16[128,4096]{1,0:T(8,128)(2,1)} %get-tuple-element.102), channel_id=1, source_target_pairs={{0,4},{2,6},{4,0},{6,2},{8,12},{10,14},{12,8},{14,10},{16,20},{18,... | collective-permute-start | bytes 3145736 | tf_op jit(solution)/shard_map/ppermute | solution.py:38
  107.2 6.8 %collective-permute-done.14.refs_2_ = bf16[64,4096]{1,0:T(8,128)(2,1)S(1)} collective-permute-done((bf16[64,4096]{1,0:T(8,128)(2,1)S(1)}, bf16[64,4096]{1,0:T(8,128)(2,1)S(1)}, u32[]{:S(2)}, u32[]{:S(2)}) %collective-permute-start.14) | collective-permute-done | bytes 524320 | tf_op jit(solution)/shard_map/ppermute | solution.py:38
  114.0 0.0 collective-permute-done.15.refs_3_
  114.0 0.0 collective-permute-start.24
  114.0 8.3 %collective-permute-done.22.refs_4_ = bf16[64,4096]{1,0:T(8,128)(2,1)S(1)} collective-permute-done((bf16[64,4096]{1,0:T(8,128)(2,1)S(1)}, bf16[64,4096]{1,0:T(8,128)(2,1)S(1)}, u32[]{:S(2)}, u32[]{:S(2)}) %collective-permute-start.22) | collective-permute-done | bytes 524320 | tf_op jit(solution)/shard_map/ppermute | solution.py:38
  122.3 2.6 %attended.1 = bf16[128,4096]{1,0:T(8,128)(2,1)} custom-call(s32[1]{0:T(128)} %bitcast.place_ref, s32[2,2]{1,0:T(2,128)S(1)} %copy-done.11, bf16[64,4096]{1,0:T(8,128)(2,1)S(1)} %get-tuple-element.81.refs_0_, bf16[64,4096]{1,0:T(8,128)(2,1)S(1)} %get-tuple-element.82.refs_1_, bf16[64,4096]{1,0:T(8,128)(2,1)S(1)} %collective-permute-done.14.refs_2_, ...), custom_call_target="tpu_custom_call" | custom-call | tf_op jit(solution)/shard_map/attended/pallas_call | solution.py:349
  124.9 3.7 %own.1 = (bf16[128,4096]{1,0:T(8,128)(2,1)}, f32[128,4096]{1,0:T(8,128)S(1)}) custom-call(bf16[64,4096]{1,0:T(8,128)(2,1)S(1)} %get-tuple-element.103.refs_0_, bf16[64,4096]{1,0:T(8,128)(2,1)S(1)} %collective-permute-done.refs_2_.refs_1_, bf16[64,4096]{1,0:T(8,128)(2,1)S(1)} %get-tuple-element.65.refs_5_.refs_2_, ...), custom_call_target="tpu_custom_call" | custom-call | tf_op jit(solution)/shard_map/own/pallas_call | solution.py:349
  128.6 1.4 copy-done.5
  129.9 0.5 collective-permute-done.23.refs_2_
  130.4 5.7 %collective-permute-done.25.refs_4_ = bf16[64,4096]{1,0:T(8,128)(2,1)S(1)} collective-permute-done((bf16[64,4096]{1,0:T(8,128)(2,1)S(1)}, bf16[64,4096]{1,0:T(8,128)(2,1)S(1)}, u32[]{:S(2)}, u32[]{:S(2)}) %collective-permute-start.25) | collective-permute-done | bytes 524320 | tf_op jit(solution)/shard_map/ppermute | solution.py:38
  136.1 2.0 %inner.1 = (f32[128,4096]{1,0:T(8,128)S(1)}, f32[1,128]{1,0:T(1,128)S(1)}) custom-call(s32[1]{0:T(128)} %bitcast.place_ref, s32[2,2]{1,0:T(2,128)S(1)} %copy-done.11, bf16[64,4096]{1,0:T(8,128)(2,1)S(1)} %get-tuple-element.106.refs_0_, bf16[64,4096]{1,0:T(8,128)(2,1)S(1)} %get-tuple-element.107.refs_1_, ...), custom_call_target="tpu_custom_call" | custom-call | tf_op jit(solution)/shard_map/inner/pallas_call | solution.py:349
  138.0 2.5 %psum.15.inner_ref = f32[1,128]{1,0:T(1,128)S(1)} all-reduce(f32[1,128]{1,0:T(1,128)S(1)} %get-tuple-element.112), channel_id=1, replica_groups=mesh['dp'=16,'mp'=2] {'mp'}, use_global_device_ids=true, to_apply=%region_1.0 | all-reduce | flops 128 | bytes 1024 | tf_op jit(solution)/shard_map/psum | solution.py:435
  140.5 1.6 %finish.1 = bf16[128,4096]{1,0:T(8,128)(2,1)} custom-call(f32[128,4096]{1,0:T(8,128)S(1)} %get-tuple-element.111.scaled_ref, bf16[128,4096]{1,0:T(8,128)(2,1)S(1)} %copy-done.2, f32[1,128]{1,0:T(1,128)S(1)} %psum.14.squares_ref, f32[1,128]{1,0:T(1,128)S(1)} %psum.15.inner_ref), custom_call_target="tpu_custom_call" | custom-call | tf_op jit(solution)/shard_map/finish/pallas_call | solution.py:349
  142.1 2.5 %add_convert_fusion = bf16[128,4096]{1,0:T(8,128)(2,1)} fusion(f32[128,4096]{1,0:T(8,128)S(1)} %copy-done.6, bf16[128,4096]{1,0:T(8,128)(2,1)} %collective-permute-done.27), kind=kLoop, calls=%fused_computation | loop fusion | flops 1572864 | bytes 4194304 | tf_op jit(solution)/shard_map/convert_element_type | solution.py:439
  (31 shorter events, 0.1 us)
Async XLA Ops:
  0.6 38.4 %collective-permute-start.5 = (bf16[128,4096]{1,0:T(8,128)(2,1)}, bf16[128,4096]{1,0:T(8,128)(2,1)S(1)}, u32[]{:S(2)}, u32[]{:S(2)}) collective-permute-start(bf16[128,4096]{1,0:T(8,128)(2,1)} %refs_8_.1), channel_id=1, source_target_pairs={{0,4},{2,6},{4,0},{6,2},{8,12},{10,14},{12,8},{14,10},{16,20},{18,... | collective-permute-start | bytes 3145736 | tf_op jit(solution)/shard_map/ppermute | solution.py:38
  3.7 1.2 copy-start
  4.9 34.1 %copy-start.3 = (bf16[128,4096]{1,0:T(8,128)(2,1)S(1)}, bf16[128,4096]{1,0:T(8,128)(2,1)}, u32[]{:S(2)}) copy-start(bf16[128,4096]{1,0:T(8,128)(2,1)} %refs_8_.1) | copy-start | bytes 3145732
  7.7 1.2 copy-start.1
  8.9 0.7 copy-start.8
  9.6 0.7 copy-start.10
  11.4 14.8 %collective-permute-start = (bf16[64,4096]{1,0:T(8,128)(2,1)S(1)}, bf16[64,4096]{1,0:T(8,128)(2,1)S(1)}, u32[]{:S(2)}, u32[]{:S(2)}) collective-permute-start(bf16[64,4096]{1,0:T(8,128)(2,1)S(1)} %get-tuple-element.61), channel_id=1, source_target_pairs={{0,2},{2,0},{4,6},{6,4},{8,10},{10,8},{12,14},{14,12},{16,18},{18,... | collective-permute-start | bytes 1572872 | tf_op jit(solution)/shard_map/ppermute | solution.py:38
  12.9 15.9 %collective-permute-start.1 = (bf16[64,4096]{1,0:T(8,128)(2,1)S(1)}, bf16[64,4096]{1,0:T(8,128)(2,1)S(1)}, u32[]{:S(2)}, u32[]{:S(2)}) collective-permute-start(bf16[64,4096]{1,0:T(8,128)(2,1)S(1)} %get-tuple-element.62), channel_id=1, source_target_pairs={{0,24},{2,26},{4,12},{6,14},{8,0},{10,2},{12,20},{14,22},{16,8},{1... | collective-permute-start | bytes 1572872 | tf_op jit(solution)/shard_map/ppermute | solution.py:38
  16.5 22.5 %collective-permute-start.2 = (bf16[64,4096]{1,0:T(8,128)(2,1)S(1)}, bf16[64,4096]{1,0:T(8,128)(2,1)S(1)}, u32[]{:S(2)}, u32[]{:S(2)}) collective-permute-start(bf16[64,4096]{1,0:T(8,128)(2,1)S(1)} %get-tuple-element.63), channel_id=1, source_target_pairs={{0,26},{2,0},{4,6},{6,12},{8,2},{10,8},{12,14},{14,20},{16,10},{18... | collective-permute-start | bytes 1572872 | tf_op jit(solution)/shard_map/ppermute | solution.py:38
  17.0 51.5 %collective-permute-start.13 = (bf16[128,4096]{1,0:T(8,128)(2,1)}, bf16[128,4096]{1,0:T(8,128)(2,1)S(1)}, u32[]{:S(2)}, u32[]{:S(2)}) collective-permute-start(bf16[128,4096]{1,0:T(8,128)(2,1)} %refs_9_.1), channel_id=1, source_target_pairs={{0,4},{2,6},{4,0},{6,2},{8,12},{10,14},{12,8},{14,10},{16,20},{18,... | collective-permute-start | bytes 3145736 | tf_op jit(solution)/shard_map/ppermute | solution.py:38
  39.0 3.8 %copy-start.7 = (bf16[128,4096]{1,0:T(8,128)(2,1)S(1)}, bf16[128,4096]{1,0:T(8,128)(2,1)}, u32[]{:S(2)}) copy-start(bf16[128,4096]{1,0:T(8,128)(2,1)} %g_ref) | copy-start | bytes 3145732
  39.0 33.5 %copy-start.4 = (bf16[128,4096]{1,0:T(8,128)(2,1)S(1)}, bf16[128,4096]{1,0:T(8,128)(2,1)}, u32[]{:S(2)}) copy-start(bf16[128,4096]{1,0:T(8,128)(2,1)} %refs_9_.1) | copy-start | bytes 3145732
  42.4 4.8 %collective-permute-start.6 = (f32[32,128]{1,0:T(8,128)S(1)}, f32[32,128]{1,0:T(8,128)S(1)}, u32[]{:S(2)}, u32[]{:S(2)}) collective-permute-start(f32[32,128]{1,0:T(8,128)S(1)} %get-tuple-element.70), channel_id=1, source_target_pairs={{2,0},{0,2},{6,4},{4,6},{10,8},{8,10},{14,12},{12,14},{18,16},{16,... | collective-permute-start | bytes 49160 | tf_op jit(solution)/shard_map/ppermute | solution.py:38
  43.5 22.6 %collective-permute-start.3 = (bf16[64,4096]{1,0:T(8,128)(2,1)S(1)}, bf16[64,4096]{1,0:T(8,128)(2,1)S(1)}, u32[]{:S(2)}, u32[]{:S(2)}) collective-permute-start(bf16[64,4096]{1,0:T(8,128)(2,1)S(1)} %get-tuple-element.67), channel_id=1, source_target_pairs={{0,2},{2,0},{4,6},{6,4},{8,10},{10,8},{12,14},{14,12},{16,18},{18,... | collective-permute-start | bytes 1572872 | tf_op jit(solution)/shard_map/ppermute | solution.py:38
  45.3 5.8 %collective-permute-start.7 = (f32[32,128]{1,0:T(8,128)S(1)}, f32[32,128]{1,0:T(8,128)S(1)}, u32[]{:S(2)}, u32[]{:S(2)}) collective-permute-start(f32[32,128]{1,0:T(8,128)S(1)} %get-tuple-element.71), channel_id=1, source_target_pairs={{24,0},{26,2},{12,4},{14,6},{0,8},{2,10},{20,12},{22,14},{8,16},{1... | collective-permute-start | bytes 49160 | tf_op jit(solution)/shard_map/ppermute | solution.py:38
  45.3 10.4 %collective-permute-start.8 = (f32[32,128]{1,0:T(8,128)S(1)}, f32[32,128]{1,0:T(8,128)S(1)}, u32[]{:S(2)}, u32[]{:S(2)}) collective-permute-start(f32[32,128]{1,0:T(8,128)S(1)} %get-tuple-element.72), channel_id=1, source_target_pairs={{26,0},{0,2},{6,4},{12,6},{2,8},{8,10},{14,12},{20,14},{10,16},{16... | collective-permute-start | bytes 49160 | tf_op jit(solution)/shard_map/ppermute | solution.py:38
  47.2 21.2 %collective-permute-start.4 = (bf16[64,4096]{1,0:T(8,128)(2,1)S(1)}, bf16[64,4096]{1,0:T(8,128)(2,1)S(1)}, u32[]{:S(2)}, u32[]{:S(2)}) collective-permute-start(bf16[64,4096]{1,0:T(8,128)(2,1)S(1)} %get-tuple-element.68), channel_id=1, source_target_pairs={{0,24},{2,26},{4,12},{6,14},{8,0},{10,2},{12,20},{14,22},{16,8},{1... | collective-permute-start | bytes 1572872 | tf_op jit(solution)/shard_map/ppermute | solution.py:38
  55.7 16.8 %collective-permute-start.9 = (bf16[64,4096]{1,0:T(8,128)(2,1)S(1)}, bf16[64,4096]{1,0:T(8,128)(2,1)S(1)}, u32[]{:S(2)}, u32[]{:S(2)}) collective-permute-start(bf16[64,4096]{1,0:T(8,128)(2,1)S(1)} %get-tuple-element.73), channel_id=1, source_target_pairs={{0,26},{2,0},{4,6},{6,12},{8,2},{10,8},{12,14},{14,20},{16,10},{18... | collective-permute-start | bytes 1572872 | tf_op jit(solution)/shard_map/ppermute | solution.py:38
  66.1 3.8 %collective-permute-start.10 = (f32[32,128]{1,0:T(8,128)S(1)}, f32[32,128]{1,0:T(8,128)S(1)}, u32[]{:S(2)}, u32[]{:S(2)}) collective-permute-start(f32[32,128]{1,0:T(8,128)S(1)} %get-tuple-element.78), channel_id=1, source_target_pairs={{0,2},{2,0},{4,6},{6,4},{8,10},{10,8},{12,14},{14,12},{16,18},{18,... | collective-permute-start | bytes 49160 | tf_op jit(solution)/shard_map/ppermute | solution.py:38
  66.1 6.2 %collective-permute-start.11 = (f32[32,128]{1,0:T(8,128)S(1)}, f32[32,128]{1,0:T(8,128)S(1)}, u32[]{:S(2)}, u32[]{:S(2)}) collective-permute-start(f32[32,128]{1,0:T(8,128)S(1)} %get-tuple-element.79), channel_id=1, source_target_pairs={{0,24},{2,26},{4,12},{6,14},{8,0},{10,2},{12,20},{14,22},{16,8},{1... | collective-permute-start | bytes 49160 | tf_op jit(solution)/shard_map/ppermute | solution.py:38
  68.4 4.1 %collective-permute-start.12 = (f32[32,128]{1,0:T(8,128)S(1)}, f32[32,128]{1,0:T(8,128)S(1)}, u32[]{:S(2)}, u32[]{:S(2)}) collective-permute-start(f32[32,128]{1,0:T(8,128)S(1)} %get-tuple-element.80), channel_id=1, source_target_pairs={{0,26},{2,0},{4,6},{6,12},{8,2},{10,8},{12,14},{14,20},{16,10},{18... | collective-permute-start | bytes 49160 | tf_op jit(solution)/shard_map/ppermute | solution.py:38
  78.5 3.8 %collective-permute-start.16 = (f32[32,128]{1,0:T(8,128)S(1)}, f32[32,128]{1,0:T(8,128)S(1)}, u32[]{:S(2)}, u32[]{:S(2)}) collective-permute-start(f32[32,128]{1,0:T(8,128)S(1)} %get-tuple-element.88), channel_id=1, source_target_pairs={{2,0},{0,2},{6,4},{4,6},{10,8},{8,10},{14,12},{12,14},{18,16},{16,... | collective-permute-start | bytes 49160 | tf_op jit(solution)/shard_map/ppermute | solution.py:38
  79.1 6.8 %collective-permute-start.17 = (f32[32,128]{1,0:T(8,128)S(1)}, f32[32,128]{1,0:T(8,128)S(1)}, u32[]{:S(2)}, u32[]{:S(2)}) collective-permute-start(f32[32,128]{1,0:T(8,128)S(1)} %get-tuple-element.89), channel_id=1, source_target_pairs={{24,0},{26,2},{12,4},{14,6},{0,8},{2,10},{20,12},{22,14},{8,16},{1... | collective-permute-start | bytes 49160 | tf_op jit(solution)/shard_map/ppermute | solution.py:38
  81.7 6.5 %collective-permute-start.18 = (f32[32,128]{1,0:T(8,128)S(1)}, f32[32,128]{1,0:T(8,128)S(1)}, u32[]{:S(2)}, u32[]{:S(2)}) collective-permute-start(f32[32,128]{1,0:T(8,128)S(1)} %get-tuple-element.90), channel_id=1, source_target_pairs={{26,0},{0,2},{6,4},{12,6},{2,8},{8,10},{14,12},{20,14},{10,16},{16... | collective-permute-start | bytes 49160 | tf_op jit(solution)/shard_map/ppermute | solution.py:38
  88.8 4.3 %collective-permute-start.19 = (f32[32,128]{1,0:T(8,128)S(1)}, f32[32,128]{1,0:T(8,128)S(1)}, u32[]{:S(2)}, u32[]{:S(2)}) collective-permute-start(f32[32,128]{1,0:T(8,128)S(1)} %get-tuple-element.91), channel_id=1, source_target_pairs={{0,2},{2,0},{4,6},{6,4},{8,10},{10,8},{12,14},{14,12},{16,18},{18,... | collective-permute-start | bytes 49160 | tf_op jit(solution)/shard_map/ppermute | solution.py:38
  88.9 6.9 %collective-permute-start.20 = (f32[32,128]{1,0:T(8,128)S(1)}, f32[32,128]{1,0:T(8,128)S(1)}, u32[]{:S(2)}, u32[]{:S(2)}) collective-permute-start(f32[32,128]{1,0:T(8,128)S(1)} %get-tuple-element.92), channel_id=1, source_target_pairs={{0,24},{2,26},{4,12},{6,14},{8,0},{10,2},{12,20},{14,22},{16,8},{1... | collective-permute-start | bytes 49160 | tf_op jit(solution)/shard_map/ppermute | solution.py:38
  89.7 6.1 %collective-permute-start.21 = (f32[32,128]{1,0:T(8,128)S(1)}, f32[32,128]{1,0:T(8,128)S(1)}, u32[]{:S(2)}, u32[]{:S(2)}) collective-permute-start(f32[32,128]{1,0:T(8,128)S(1)} %get-tuple-element.93), channel_id=1, source_target_pairs={{0,26},{2,0},{4,6},{6,12},{8,2},{10,8},{12,14},{14,20},{16,10},{18... | collective-permute-start | bytes 49160 | tf_op jit(solution)/shard_map/ppermute | solution.py:38
  93.0 21.0 %collective-permute-start.14 = (bf16[64,4096]{1,0:T(8,128)(2,1)S(1)}, bf16[64,4096]{1,0:T(8,128)(2,1)S(1)}, u32[]{:S(2)}, u32[]{:S(2)}) collective-permute-start(bf16[64,4096]{1,0:T(8,128)(2,1)S(1)} %get-tuple-element.83), channel_id=1, source_target_pairs={{2,0},{0,2},{6,4},{4,6},{10,8},{8,10},{14,12},{12,14},{18,16},{16,... | collective-permute-start | bytes 1572872 | tf_op jit(solution)/shard_map/ppermute | solution.py:38
  93.0 21.0 %collective-permute-start.15 = (bf16[64,4096]{1,0:T(8,128)(2,1)S(1)}, bf16[64,4096]{1,0:T(8,128)(2,1)S(1)}, u32[]{:S(2)}, u32[]{:S(2)}) collective-permute-start(bf16[64,4096]{1,0:T(8,128)(2,1)S(1)} %get-tuple-element.84), channel_id=1, source_target_pairs={{24,0},{26,2},{12,4},{14,6},{0,8},{2,10},{20,12},{22,14},{8,16},{1... | collective-permute-start | bytes 1572872 | tf_op jit(solution)/shard_map/ppermute | solution.py:38
  93.1 31.8 %collective-permute-start.26 = (bf16[128,4096]{1,0:T(8,128)(2,1)S(1)}, bf16[128,4096]{1,0:T(8,128)(2,1)S(1)}, u32[]{:S(2)}, u32[]{:S(2)}) collective-permute-start(bf16[128,4096]{1,0:T(8,128)(2,1)S(1)} %get-tuple-element.104), channel_id=1, source_target_pairs={{0,4},{2,6},{4,0},{6,2},{8,12},{10,14},{12,8},{14,10},{16,20},{18,... | collective-permute-start | bytes 3145736 | tf_op jit(solution)/shard_map/ppermute | solution.py:38
  95.8 26.5 %collective-permute-start.22 = (bf16[64,4096]{1,0:T(8,128)(2,1)S(1)}, bf16[64,4096]{1,0:T(8,128)(2,1)S(1)}, u32[]{:S(2)}, u32[]{:S(2)}) collective-permute-start(bf16[64,4096]{1,0:T(8,128)(2,1)S(1)} %get-tuple-element.94), channel_id=1, source_target_pairs={{26,0},{0,2},{6,4},{12,6},{2,8},{8,10},{14,12},{20,14},{10,16},{16... | collective-permute-start | bytes 1572872 | tf_op jit(solution)/shard_map/ppermute | solution.py:38
  98.2 24.1 %copy-start.11 = (s32[2,2]{1,0:T(2,128)S(1)}, s32[2,2]{1,0:T(2,128)}, u32[]{:S(2)}) copy-start(s32[2,2]{1,0:T(2,128)} %near_ref.11) | copy-start | bytes 52
  105.0 37.1 %collective-permute-start.27 = (bf16[128,4096]{1,0:T(8,128)(2,1)}, bf16[128,4096]{1,0:T(8,128)(2,1)}, u32[]{:S(2)}, u32[]{:S(2)}) collective-permute-start(bf16[128,4096]{1,0:T(8,128)(2,1)} %get-tuple-element.102), channel_id=1, source_target_pairs={{0,4},{2,6},{4,0},{6,2},{8,12},{10,14},{12,8},{14,10},{16,20},{18,... | collective-permute-start | bytes 3145736 | tf_op jit(solution)/shard_map/ppermute | solution.py:38
  114.0 16.4 %collective-permute-start.23 = (bf16[64,4096]{1,0:T(8,128)(2,1)S(1)}, bf16[64,4096]{1,0:T(8,128)(2,1)S(1)}, u32[]{:S(2)}, u32[]{:S(2)}) collective-permute-start(bf16[64,4096]{1,0:T(8,128)(2,1)S(1)} %get-tuple-element.99), channel_id=1, source_target_pairs={{2,0},{0,2},{6,4},{4,6},{10,8},{8,10},{14,12},{12,14},{18,16},{16,... | collective-permute-start | bytes 1572872 | tf_op jit(solution)/shard_map/ppermute | solution.py:38
  114.0 16.4 %collective-permute-start.24 = (bf16[64,4096]{1,0:T(8,128)(2,1)S(1)}, bf16[64,4096]{1,0:T(8,128)(2,1)S(1)}, u32[]{:S(2)}, u32[]{:S(2)}) collective-permute-start(bf16[64,4096]{1,0:T(8,128)(2,1)S(1)} %get-tuple-element.100), channel_id=1, source_target_pairs={{24,0},{26,2},{12,4},{14,6},{0,8},{2,10},{20,12},{22,14},{8,16},{1... | collective-permute-start | bytes 1572872 | tf_op jit(solution)/shard_map/ppermute | solution.py:38
  122.3 13.7 %collective-permute-start.25 = (bf16[64,4096]{1,0:T(8,128)(2,1)S(1)}, bf16[64,4096]{1,0:T(8,128)(2,1)S(1)}, u32[]{:S(2)}, u32[]{:S(2)}) collective-permute-start(bf16[64,4096]{1,0:T(8,128)(2,1)S(1)} %get-tuple-element.101), channel_id=1, source_target_pairs={{26,0},{0,2},{6,4},{12,6},{2,8},{8,10},{14,12},{20,14},{10,16},{16... | collective-permute-start | bytes 1572872 | tf_op jit(solution)/shard_map/ppermute | solution.py:38
  124.9 11.2 %copy-start.2 = (bf16[128,4096]{1,0:T(8,128)(2,1)S(1)}, bf16[128,4096]{1,0:T(8,128)(2,1)}, u32[]{:S(2)}) copy-start(bf16[128,4096]{1,0:T(8,128)(2,1)} %q_ref.5) | copy-start | bytes 3145732
  124.9 11.2 %copy-start.9 = (f32[4096]{0:T(1024)S(1)}, f32[4096]{0:T(1024)}, u32[]{:S(2)}) copy-start(f32[4096]{0:T(1024)} %param.7) | copy-start | bytes 49156
  128.6 1.4 copy-start.5
  140.5 1.6 %copy-start.6 = (f32[128,4096]{1,0:T(8,128)S(1)}, f32[128,4096]{1,0:T(8,128)}, u32[]{:S(2)}) copy-start(f32[128,4096]{1,0:T(8,128)} %copy-done.5) | copy-start | bytes 6291460

commit v2 on v1

v2 whole, which is shorter than its diff:
```python
import functools

import jax
import jax.numpy as jnp
from jax import lax
from jax.experimental import pallas as pl
from jax.experimental.pallas import tpu as pltpu
from jax.sharding import PartitionSpec as P

HEADS = 64
HS = 128
GROUP = 64
FEAT = HEADS * HS
EPSILON = 1e-06
SCALING = 1.0 / HS**0.5
LANES = 128
CHUNK = 8
VMEM_LIMIT = 8 * 1024 * 1024
WORK = 8 * 1024 * 1024
SLOTS = 5
OWN = (0, 2)
PARTNER = (1, 3, 4)


def routes(count):
    def side(i):
        return -4 if i & 2 == 0 else 4

    diagonal = (-3, -1, 1, 3)
    return {
        "y": [(i, i ^ 2) for i in range(count)],
        2: [(i, i ^ 1) for i in range(count)],
        3: [(i, (i + side(i)) % count) for i in range(count)],
        4: [(i, (i + diagonal[i & 3]) % count) for i in range(count)],
    }


def sent(array, route):
    return lax.ppermute(array, "dp", route)


def out_and_back(count):
    route = routes(count)
    back = {s: [(b, a) for a, b in route[s]] for s in (2, 3, 4)}

    return route, back, functools.partial(sent, route=route["y"])


def dot(a, b, left, right):
    return lax.dot_general(a, b, (((left,), (right,)), ((), ())), preferred_element_type=jnp.float32)


def group_numbers(place_ref, near_ref, count, groups):
    place = place_ref[0]
    one = 1 - 2 * (place & 1)
    two = 2 - 2 * (place & 2)
    numbers = []
    for offset in (0, two, one, -two, -one):
        block = lax.rem(place + offset + count, count)
        number = jnp.int32(-1)
        for g in range(groups):
            used = (near_ref[g, 0] == block) | (near_ref[g, 1] == block)
            number = jnp.where(used, g, number)
        numbers.append(number)
    return numbers


def rows_of(number):
    return pl.ds(pl.multiple_of(jnp.maximum(number, 0) * GROUP, GROUP), GROUP)


def to_row(x):
    return jnp.sum(x.T, axis=0, keepdims=True)


def to_columns(row):
    return jnp.broadcast_to(row, (row.shape[1], row.shape[1])).T


def tile(t):
    return slice(t * LANES, (t + 1) * LANES)


def squares_kernel(q_ref, squares_ref):
    x = q_ref[:, tile(0)].astype(jnp.float32)
    total = x * x
    for t in range(1, q_ref.shape[1] // LANES):
        x = q_ref[:, tile(t)].astype(jnp.float32)
        total = total + x * x
    squares_ref[...] = to_row(total)


def pick_kernel(slots, count, groups, place_ref, near_ref, g_ref, *slot_refs):
    numbers = group_numbers(place_ref, near_ref, count, groups)
    for s, slot_ref in zip(slots, slot_refs):
        slot_ref[...] = g_ref[rows_of(numbers[s])]


def added(refs):
    total = refs[0][...]
    for ref in refs[1:]:
        total = total + ref[...]
    return total


def inverse_columns(squares_refs):
    return to_columns(lax.rsqrt(added(squares_refs) / FEAT + EPSILON))


def prepare_queries_kernel(count, groups, place_ref, near_ref, q_ref, gain_ref, *refs):
    *squares_refs, normed_ref, _, _, _ = refs
    slot_refs = refs[-3:]
    numbers = group_numbers(place_ref, near_ref, count, groups)
    inverse = inverse_columns(squares_refs)
    for t in range(q_ref.shape[1] // LANES):
        x = q_ref[:, tile(t)].astype(jnp.float32)
        normed_ref[:, tile(t)] = (x * gain_ref[:, tile(t)] * inverse).astype(jnp.bfloat16)
    for slot_ref, number in zip(slot_refs, numbers[2:]):
        slot_ref[...] = normed_ref[rows_of(number)]


def slot_views(numbers, whole_ref, slot_refs):
    own = [whole_ref.at[rows_of(numbers[s])] for s in range(SLOTS - len(slot_refs))]
    return own + list(slot_refs)


def head(refs, slots, cols):
    return jnp.concatenate([refs[s][:, cols] for s in slots], axis=0)


def each_chunk(heads, unit, body):
    def step(i, carry):
        first = i * unit
        cols = [pl.ds(pl.multiple_of((first + h) * HS, HS), HS) for h in range(unit)]
        body(pl.ds(pl.multiple_of(first, unit), unit), cols)
        return carry

    lax.fori_loop(0, heads // unit, step, 0)


def scores_kernel(count, groups, place_ref, near_ref, *refs):
    numbers = group_numbers(place_ref, near_ref, count, groups)
    q_refs = slot_views(numbers, refs[0], refs[1:4])
    k_refs, stat_refs, weight_refs = refs[4:6], refs[6 : 6 + SLOTS], refs[6 + SLOTS :]

    def body(rows, cols):
        for slots, k_ref, weight_ref in zip((OWN, PARTNER), k_refs, weight_refs):
            scores = [dot(k_ref[:, c], head(q_refs, slots, c), 1, 1) * SCALING for c in cols]
            tops = [jnp.max(x, axis=0, keepdims=True) for x in scores]
            totals = []
            for c, x, top in zip(cols, scores, tops):
                weights = jnp.exp(x - top)
                weight_ref[c] = weights
                totals.append(jnp.sum(weights, axis=0, keepdims=True))
            tops = jnp.concatenate(tops, axis=0)
            totals = jnp.concatenate(totals, axis=0)
            for at, s in enumerate(slots):
                lanes = slice(at * GROUP, (at + 1) * GROUP)
                stat_refs[s][rows] = jnp.concatenate([tops[:, lanes], totals[:, lanes]], axis=1)

    each_chunk(stat_refs[0].shape[0], CHUNK, body)


def combine_scores_kernel(count, groups, place_ref, near_ref, *refs):
    stat_refs, back_refs = refs[:SLOTS], refs[SLOTS:]
    numbers = group_numbers(place_ref, near_ref, count, groups)
    heads = stat_refs[0].shape[0]
    shape = (heads, GROUP)
    tops = [r[:, 0:GROUP] for r in stat_refs]
    totals = [r[:, GROUP : 2 * GROUP] for r in stat_refs]
    number_of = [jnp.full(shape, n, jnp.int32) for n in numbers]
    lowest = jnp.full(shape, -jnp.inf, jnp.float32)
    zero = jnp.zeros(shape, jnp.float32)
    merged = []
    for g in range(groups):
        top, total = lowest, zero
        for s in range(SLOTS):
            top = jnp.maximum(top, jnp.where(number_of[s] == g, tops[s], lowest))
        for s in range(SLOTS):
            mine = number_of[s] == g
            factor = jnp.exp(jnp.where(mine, tops[s] - top, zero))
            total = total + jnp.where(mine, totals[s] * factor, zero)
        merged.append((top, 1.0 / total))
    for s in range(SLOTS):
        share = zero
        for g in range(groups):
            mine = number_of[s] == g
            factor = jnp.exp(jnp.where(mine, tops[s] - merged[g][0], zero))
            share = jnp.where(mine, factor * merged[g][1], share)
        back_refs[s][...] = jnp.concatenate([share, zero], axis=1)


def combine_centres_kernel(count, groups, place_ref, near_ref, *refs):
    stat_refs, back_refs = refs[:SLOTS], refs[SLOTS:]
    numbers = group_numbers(place_ref, near_ref, count, groups)
    shape = stat_refs[0].shape
    number_of = [jnp.full(shape, n, jnp.int32) for n in numbers]
    zero = jnp.zeros(shape, jnp.float32)
    totals = []
    for g in range(groups):
        total = zero
        for s in range(SLOTS):
            total = total + jnp.where(number_of[s] == g, stat_refs[s][...], zero)
        totals.append(total)
    for s in range(SLOTS):
        here = zero
        for g in range(groups):
            here = jnp.where(number_of[s] == g, totals[g], here)
        back_refs[s][...] = here


def stat_rows(stat_refs, slots, rows):
    return jnp.concatenate([stat_refs[s][rows, 0:GROUP] for s in slots], axis=1)


def probs_of(rows, slots, back_refs, weight_ref, cols):
    shares = stat_rows(back_refs, slots, rows)
    return [weight_ref[c] * shares[h : h + 1] for h, c in enumerate(cols)]


def centres_kernel(count, groups, place_ref, near_ref, *refs):
    numbers = group_numbers(place_ref, near_ref, count, groups)
    g_refs = slot_views(numbers, refs[0], refs[1:4])
    v_refs, weight_refs, back_refs = refs[4:6], refs[6:8], refs[8 : 8 + SLOTS]
    centre_refs = refs[8 + SLOTS : 8 + 2 * SLOTS]
    *product_refs, dv_ref = refs[8 + 2 * SLOTS :]

    def body(rows, cols):
        for slots, v_ref, weight_ref, product_ref in zip(
            (OWN, PARTNER), v_refs, weight_refs, product_refs
        ):
            products = [dot(v_ref[:, c], head(g_refs, slots, c), 1, 1) for c in cols]
            probs = probs_of(rows, slots, back_refs, weight_ref, cols)
            for c, x, p in zip(cols, products, probs):
                product_ref[c] = x
                if slots is PARTNER:
                    product = dot(p.astype(jnp.bfloat16), head(g_refs, slots, c), 1, 0)
                    dv_ref[:, c] = product.astype(jnp.bfloat16)
            centres = [jnp.sum(p * x, axis=0, keepdims=True) for p, x in zip(probs, products)]
            centres = jnp.concatenate(centres, axis=0)
            empty = jnp.zeros((centres.shape[0], GROUP), jnp.float32)
            for at, s in enumerate(slots):
                lanes = slice(at * GROUP, (at + 1) * GROUP)
                centre_refs[s][rows] = jnp.concatenate([centres[:, lanes], empty], axis=1)

    each_chunk(centre_refs[0].shape[0], CHUNK, body)


def context_kernel(*refs):
    v_refs, weight_refs, back_refs = refs[0:2], refs[2:4], refs[4 : 4 + SLOTS]
    ctx_refs = refs[4 + SLOTS :]

    def body(rows, cols):
        for slots, v_ref, weight_ref in zip((OWN, PARTNER), v_refs, weight_refs):
            probs = probs_of(rows, slots, back_refs, weight_ref, cols)
            for c, p in zip(cols, probs):
                context = dot(p.astype(jnp.bfloat16), v_ref[:, c], 0, 0).astype(jnp.bfloat16)
                for at, s in enumerate(slots):
                    ctx_refs[s][:, c] = context[at * GROUP : (at + 1) * GROUP]

    each_chunk(back_refs[0].shape[0], CHUNK, body)


def grad_scores_of(rows, slots, back_refs, centre_refs, weight_ref, product_ref, cols):
    probs = probs_of(rows, slots, back_refs, weight_ref, cols)
    centre = stat_rows(centre_refs, slots, rows)
    return probs, [
        (p * (product_ref[c] - centre[h : h + 1])).astype(jnp.bfloat16)
        for h, (c, p) in enumerate(zip(cols, probs))
    ]


def gradient_kernel(count, groups, place_ref, near_ref, *refs):
    numbers = group_numbers(place_ref, near_ref, count, groups)
    q_refs = slot_views(numbers, refs[0], refs[1:4])
    k_refs, weight_refs, product_refs, rest = refs[4:6], refs[6:8], refs[8:10], refs[10:]
    back_refs, centre_refs, grad_refs = (rest[i * SLOTS : (i + 1) * SLOTS] for i in range(3))
    dk_ref = rest[3 * SLOTS]

    def body(rows, cols):
        for slots, k_ref, weight_ref, product_ref in zip(
            (OWN, PARTNER), k_refs, weight_refs, product_refs
        ):
            _, lows = grad_scores_of(
                rows, slots, back_refs, centre_refs, weight_ref, product_ref, cols
            )
            for c, low in zip(cols, lows):
                grad = (dot(low, k_ref[:, c], 0, 0) * SCALING).astype(jnp.bfloat16)
                for at, s in enumerate(slots):
                    grad_refs[s][:, c] = grad[at * GROUP : (at + 1) * GROUP]
                if slots is PARTNER:
                    product = dot(low, head(q_refs, slots, c), 1, 0) * SCALING
                    dk_ref[:, c] = product.astype(jnp.bfloat16)

    each_chunk(back_refs[0].shape[0], CHUNK, body)


def own_kernel(count, groups, place_ref, near_ref, *refs):
    numbers = group_numbers(place_ref, near_ref, count, groups)
    normed_ref, q_ref, grad_ref, g_ref, weight_ref, product_ref = refs[:6]
    q_refs = dict(zip(OWN, (normed_ref.at[rows_of(numbers[0])], q_ref)))
    g_refs = dict(zip(OWN, (grad_ref.at[rows_of(numbers[0])], g_ref)))
    back_refs, centre_refs = dict(zip(OWN, refs[6:8])), dict(zip(OWN, refs[8:10]))
    far_dv_ref, far_dk_ref, dv_ref, dk_ref = refs[10:]

    def body(rows, cols):
        probs, lows = grad_scores_of(
            rows, OWN, back_refs, centre_refs, weight_ref, product_ref, cols
        )
        for c, p, low in zip(cols, probs, lows):
            total = dot(p.astype(jnp.bfloat16), head(g_refs, OWN, c), 1, 0)
            total = total + far_dv_ref[:, c].astype(jnp.float32)
            dv_ref[:, c] = total.astype(jnp.bfloat16)
            total = dot(low, head(q_refs, OWN, c), 1, 0) * SCALING
            total = total + far_dk_ref[:, c].astype(jnp.float32)
            dk_ref[:, c] = total.astype(jnp.bfloat16)

    each_chunk(refs[6].shape[0], CHUNK, body)


def gathered(weights, refs, t):
    total = None
    for s in range(SLOTS):
        part = weights[s] * refs[s][:, tile(t)].astype(jnp.float32)
        total = part if total is None else total + part
    return total


def weights_of(numbers, g):
    return [jnp.where(n == g, 1.0, 0.0) for n in numbers]


def attended_kernel(count, groups, place_ref, near_ref, *refs):
    ctx_refs, out_ref = refs[:SLOTS], refs[SLOTS]
    numbers = group_numbers(place_ref, near_ref, count, groups)
    for g in range(groups):
        weights = weights_of(numbers, g)
        rows = slice(g * GROUP, (g + 1) * GROUP)
        for t in range(out_ref.shape[1] // LANES):
            out_ref[rows, tile(t)] = gathered(weights, ctx_refs, t).astype(jnp.bfloat16)


def inner_kernel(count, groups, place_ref, near_ref, *refs):
    grad_refs = refs[:SLOTS]
    q_ref, gain_ref, scaled_ref, inner_ref = refs[SLOTS:]
    numbers = group_numbers(place_ref, near_ref, count, groups)
    totals = []
    for g in range(groups):
        weights = weights_of(numbers, g)
        rows = slice(g * GROUP, (g + 1) * GROUP)
        total = jnp.zeros((GROUP, LANES), jnp.float32)
        for t in range(q_ref.shape[1] // LANES):
            scaled = gathered(weights, grad_refs, t) * gain_ref[:, tile(t)]
            scaled_ref[rows, tile(t)] = scaled
            total = total + scaled * q_ref[rows, tile(t)].astype(jnp.float32)
        totals.append(total)
    inner_ref[...] = to_row(jnp.concatenate(totals, axis=0))


def finish_kernel(scaled_ref, q_ref, *refs):
    *sum_refs, dq_ref = refs
    half = len(sum_refs) // 2
    inverse = inverse_columns(sum_refs[:half])
    factor = inverse * inverse * inverse * to_columns(added(sum_refs[half:])) / FEAT
    for t in range(q_ref.shape[1] // LANES):
        x = q_ref[:, tile(t)].astype(jnp.float32)
        dq_ref[:, tile(t)] = (inverse * scaled_ref[:, tile(t)] - x * factor).astype(jnp.bfloat16)


def spread(array, axis):
    count = lax.axis_size(axis)
    shifts = [[(i, (i + k) % count) for i in range(count)] for k in range(1, count)]
    return [array] + [lax.ppermute(array, axis, shift) for shift in shifts]


def in_vmem(array):
    return pltpu.with_memory_space_constraint(array, pltpu.VMEM)


def after(values, *tokens):
    return lax.optimization_barrier((values, tokens))[0]


def kernel_call(body, name, outs, scratch=(), scalars=0, last=(), cost=0):
    vmem = pl.BlockSpec(memory_space=pltpu.VMEM)

    def call(*args):
        small, large = args[:scalars], [in_vmem(a) for a in args[scalars:]]
        shapes = [
            (jax.ShapeDtypeStruct if i in last else pltpu.VMEM)(shape, dtype)
            for i, (shape, dtype) in enumerate(outs)
        ]
        results = pl.pallas_call(
            body,
            in_specs=[pl.BlockSpec(memory_space=pltpu.SMEM)] * scalars + [vmem] * len(large),
            out_specs=[vmem] * len(outs),
            out_shape=shapes,
            scratch_shapes=list(scratch),
            name=name,
            cost_estimate=pl.CostEstimate(flops=0, bytes_accessed=cost, transcendentals=0),
            compiler_params=pltpu.CompilerParams(vmem_limit_bytes=VMEM_LIMIT),
        )(*small, *large)
        return list(results)

    return call


def local(queries, query_gain, keys, values, neighbours, d_out):
    rows, width = queries.shape
    heads = width // HS
    groups = rows // GROUP
    count = lax.axis_size("dp")
    route, back_route, across = out_and_back(count)
    place = jnp.full((1,), lax.axis_index("dp"), jnp.int32)
    gain = query_gain[None, :]

    slot = ((GROUP, width), jnp.bfloat16)
    tall = ((rows, width), jnp.bfloat16)
    row = ((1, rows), jnp.float32)
    stat = ((heads, LANES), jnp.float32)

    def out(part, s):
        return sent(part, route[s])

    def home(part, s):
        return sent(part, back_route[s])

    def go(parts):
        return [out(p, s) if s >= 2 else p for s, p in enumerate(parts)]

    def come(parts):
        return [home(p, s) if s >= 2 else p for s, p in enumerate(parts)]

    def placed(kernel, name, outs, scratch=(), last=(), cost=0):
        call = kernel_call(
            functools.partial(kernel, count, groups), name, outs, scratch, 2, last, cost
        )
        return functools.partial(call, place, neighbours)

    def picked(slots, array):
        return placed(functools.partial(pick_kernel, slots), "pick", [slot] * len(slots))(array)

    far_keys = across(keys)
    (squares,) = kernel_call(squares_kernel, "squares", [row])(queries)
    squares = spread(squares, "mp")
    normed, *q_parts = placed(
        prepare_queries_kernel, "prepare_queries", [tall] + [slot] * 3
    )(queries, gain, *squares)
    q_slots = [out(q, s) for q, s in zip(q_parts, (2, 3, 4))]
    far_values = across(values)
    g2, g3 = picked((2, 3), after(d_out, q_parts[2]))
    g2, g3 = out(g2, 2), out(g3, 3)

    own_scores = ((width, len(OWN) * GROUP), jnp.float32)
    far_scores = ((width, len(PARTNER) * GROUP), jnp.float32)
    *stats, own_weights, far_weights = placed(
        scores_kernel, "scores", [stat] * SLOTS + [own_scores, far_scores]
    )(normed, *q_slots, keys, far_keys)
    stats[2:] = after(stats[2:], g2, g3)
    stats = come(stats)
    (g4,) = picked((4,), after(d_out, *stats[2:]))
    g_slots = [g2, g3, out(g4, 4)]
    back = placed(combine_scores_kernel, "combine_scores", [stat] * SLOTS)(*stats)
    back = go(back)

    inputs = [d_out, *g_slots, values, far_values, own_weights, far_weights]
    contexts = kernel_call(context_kernel, "context", [slot] * SLOTS)(
        *inputs[-4:], after(back[0], g_slots[2]), *back[1:]
    )
    held = [after(back[0], contexts[0]), *back[1:]]
    *centres, own_products, far_products, far_dv = placed(
        centres_kernel, "centres", [stat] * SLOTS + [own_scores, far_scores, tall]
    )(*inputs, *held)
    contexts[2:4] = [home(contexts[s], s) for s in (2, 3)]
    far_dv = across(after(far_dv, contexts[2], contexts[3]))
    centres[2:] = after(centres[2:], contexts[2], contexts[3])
    centres = come(centres)
    centres = placed(combine_centres_kernel, "combine_centres", [stat] * SLOTS)(*centres)
    centres = go(centres)
    contexts[4] = home(after(contexts[4], centres[2]), 4)

    *grads, far_dk = placed(gradient_kernel, "gradient", [slot] * SLOTS + [tall])(
        normed, *q_slots, keys, far_keys, own_weights, far_weights, own_products, far_products,
        *back, *centres,
    )
    far_dk = across(after(far_dk, far_dv))
    grads[4] = after(grads[4], contexts[4])
    grads = come(grads)

    d_values, d_keys = placed(own_kernel, "own", [tall, tall], last=(0, 1))(
        normed, q_slots[0], d_out, g2, own_weights, own_products, back[0], back[2], centres[0], centres[2],
        far_dv, far_dk,
    )
    (attended,) = placed(attended_kernel, "attended", [tall], last=(0,))(*contexts)
    grads[2:] = after(grads[2:], attended, d_values)
    scaled, inner = placed(inner_kernel, "inner", [((rows, width), jnp.float32), row])(
        *grads, queries, gain
    )
    inner = spread(inner, "mp")
    (d_queries,) = kernel_call(finish_kernel, "finish", [tall], last=(0,))(
        scaled, queries, *squares, *inner
    )
    return (attended, d_queries, d_keys, d_values)


def solution(mesh):
    placed = (P("dp", "mp"), P("mp"), P("dp", "mp"), P("dp", "mp"), P("dp", None), P("dp", "mp"))
    return jax.shard_map(
        local,
        mesh=mesh,
        in_specs=placed,
        out_specs=(P("dp", "mp"), P("dp", "mp"), P("dp", "mp"), P("dp", "mp")),
        check_vma=False,
    )
```

time: 145 us -> 138 us (0.952)
  waiting for transfers between devices: 58.1 us -> 74.3 us
  starting transfers between devices: 43.6 us -> 31.3 us
  blocking collectives: 4.94 us -> 0 us
  other arithmetic: 2.47 us -> 0 us
  Pallas kernels: 29.4 us -> 27.2 us
    ppermute x28, waiting for transfers between devices: 58.1 us -> 73.2 us  [sent(): return lax.ppermute(array, 'dp', route)]
    ppermute x28, starting transfers between devices: 43.6 us -> 30.7 us  [sent(): return lax.ppermute(array, 'dp', route)]
    psum x2 -> x0, blocking collectives: 4.94 us -> none  [the longest x1 2.47 us: local(): squares = lax.psum(squares, 'mp')]
    convert_element_type x1 -> x0, other arithmetic: 2.47 us -> none  [local(): d_keys = (own_dk + far_dk.astype(jnp.float32)).astype(jnp.bfloat16)]
    pallas_call x12 -> x14, Pallas kernels: 29.4 us -> 27.2 us  [call(): pl.pallas_call(body, in_specs=[pl.BlockSpec(memory_space=pltpu.SMEM)] * s...]
    unnamed x24 -> x20, local copies, waits for them, and re-layouts: 5.23 us -> 3.95 us
  transfers between devices with their start and end apart: 28 -> 30, of which waited for: 14 -> 22; matrix products, arithmetic and copies ran while one was open for 0% -> 0% of each run, Pallas kernels for 16% -> 15%
where the time goes in v2:
time: 138 us
  waiting for transfers between devices  74.3 us (54%)
  starting transfers between devices  31.3 us (23%)
  Pallas kernels  27.2 us (20%)
  local copies, waits for them, and re-layouts  3.95 us (3%)
    ppermute x28, waiting for transfers between devices, sent(): return lax.ppermute(array, 'dp', route)  73.2 us
    ppermute x28, starting transfers between devices, sent(): return lax.ppermute(array, 'dp', route)  30.7 us
    pallas_call x14, Pallas kernels, call(): pl.pallas_call(body, in_specs=[pl.BlockSpec(memory_space=pltpu.SMEM)] * s...  27.2 us
    unnamed x20, local copies, waits for them, and re-layouts  3.95 us
  transfers between devices with their start and end apart: 30, of which 22 were waited for; matrix products, arithmetic and copies ran while one was open for 0% of the time, Pallas kernels for 15%

profile of v2, /device:TPU:0, one launch (start us, length us, event | category | flops | bytes accessed | tf_op | source)
XLA Modules:
  0.0 137.5 jit_solution(11449890623845913568)
XLA Ops:
  0.6 0.0 copy-start.1
  0.7 1.3 copy-done.1
  2.0 0.3 squares.1.refs_0_
  2.3 0.5 collective-permute-start.1
  2.8 2.6 %collective-permute-start.5 = (bf16[128,4096]{1,0:T(8,128)(2,1)}, bf16[128,4096]{1,0:T(8,128)(2,1)S(1)}, u32[]{:S(2)}, u32[]{:S(2)}) collective-permute-start(bf16[128,4096]{1,0:T(8,128)(2,1)} %refs_4_.5), channel_id=1, source_target_pairs={{0,4},{2,6},{4,0},{6,2},{8,12},{10,14},{12,8},{14,10},{16,20},{18,... | collective-permute-start | bytes 3145736 | tf_op jit(solution)/shard_map/ppermute | solution.py:39
  5.4 1.2 copy-done.2
  6.6 0.7 copy-done.6
  7.3 0.7 copy-done.8
  8.0 1.0 prepare_queries.1
  9.0 1.6 %collective-permute-start.2 = (bf16[64,4096]{1,0:T(8,128)(2,1)S(1)}, bf16[64,4096]{1,0:T(8,128)(2,1)S(1)}, u32[]{:S(2)}, u32[]{:S(2)}) collective-permute-start(bf16[64,4096]{1,0:T(8,128)(2,1)S(1)} %get-tuple-element.68), channel_id=1, source_target_pairs={{0,2},{2,0},{4,6},{6,4},{8,10},{10,8},{12,14},{14,12},{16,18},{18,... | collective-permute-start | bytes 1572872 | tf_op jit(solution)/shard_map/ppermute | solution.py:39
  10.6 3.6 %collective-permute-start.3 = (bf16[64,4096]{1,0:T(8,128)(2,1)S(1)}, bf16[64,4096]{1,0:T(8,128)(2,1)S(1)}, u32[]{:S(2)}, u32[]{:S(2)}) collective-permute-start(bf16[64,4096]{1,0:T(8,128)(2,1)S(1)} %get-tuple-element.69), channel_id=1, source_target_pairs={{0,24},{2,26},{4,12},{6,14},{8,0},{10,2},{12,20},{14,22},{16,8},{1... | collective-permute-start | bytes 1572872 | tf_op jit(solution)/shard_map/ppermute | solution.py:39
  14.2 0.4 collective-permute-start.4
  14.6 0.6 pick.2
  15.3 1.7 %collective-permute-start.6 = (bf16[64,4096]{1,0:T(8,128)(2,1)S(1)}, bf16[64,4096]{1,0:T(8,128)(2,1)S(1)}, u32[]{:S(2)}, u32[]{:S(2)}) collective-permute-start(bf16[64,4096]{1,0:T(8,128)(2,1)S(1)} %get-tuple-element.79), channel_id=1, source_target_pairs={{0,2},{2,0},{4,6},{6,4},{8,10},{10,8},{12,14},{14,12},{16,18},{18,... | collective-permute-start | bytes 1572872 | tf_op jit(solution)/shard_map/ppermute | solution.py:39
  16.9 6.9 %collective-permute-done.2.refs_1_ = bf16[64,4096]{1,0:T(8,128)(2,1)S(1)} collective-permute-done((bf16[64,4096]{1,0:T(8,128)(2,1)S(1)}, bf16[64,4096]{1,0:T(8,128)(2,1)S(1)}, u32[]{:S(2)}, u32[]{:S(2)}) %collective-permute-start.2) | collective-permute-done | bytes 524320 | tf_op jit(solution)/shard_map/ppermute | solution.py:39
  23.9 3.6 %collective-permute-start.7 = (bf16[64,4096]{1,0:T(8,128)(2,1)S(1)}, bf16[64,4096]{1,0:T(8,128)(2,1)S(1)}, u32[]{:S(2)}, u32[]{:S(2)}) collective-permute-start(bf16[64,4096]{1,0:T(8,128)(2,1)S(1)} %get-tuple-element.80), channel_id=1, source_target_pairs={{0,24},{2,26},{4,12},{6,14},{8,0},{10,2},{12,20},{14,22},{16,8},{1... | collective-permute-start | bytes 1572872 | tf_op jit(solution)/shard_map/ppermute | solution.py:39
  27.5 10.3 %collective-permute-done.4.refs_3_ = bf16[64,4096]{1,0:T(8,128)(2,1)S(1)} collective-permute-done((bf16[64,4096]{1,0:T(8,128)(2,1)S(1)}, bf16[64,4096]{1,0:T(8,128)(2,1)S(1)}, u32[]{:S(2)}, u32[]{:S(2)}) %collective-permute-start.4) | collective-permute-done | bytes 524320 | tf_op jit(solution)/shard_map/ppermute | solution.py:39
  37.8 3.9 %scores.1 = (f32[32,128]{1,0:T(8,128)S(1)}, f32[32,128]{1,0:T(8,128)S(1)}, f32[32,128]{1,0:T(8,128)S(1)}, f32[32,128]{1,0:T(8,128)S(1)}, f32[32,128]{1,0:T(8,128...) custom-call(s32[1]{0:T(128)} %bitcast.place_ref, s32[2,2]{1,0:T(2,128)S(1)} %copy-done.7, ...), custom_call_target="tpu_custom_call" | custom-call | tf_op jit(solution)/shard_map/scores/pallas_call | solution.py:393
  41.7 3.9 %collective-permute-done.6.refs_1_.refs_3_ = bf16[64,4096]{1,0:T(8,128)(2,1)S(1)} collective-permute-done((bf16[64,4096]{1,0:T(8,128)(2,1)S(1)}, bf16[64,4096]{1,0:T(8,128)(2,1)S(1)}, u32[]{:S(2)}, u32[]{:S(2)}) %collective-permute-start.6) | collective-permute-done | bytes 524320 | tf_op jit(solution)/shard_map/ppermute | solution.py:39
  45.6 2.3 %collective-permute-done.7.refs_2_ = bf16[64,4096]{1,0:T(8,128)(2,1)S(1)} collective-permute-done((bf16[64,4096]{1,0:T(8,128)(2,1)S(1)}, bf16[64,4096]{1,0:T(8,128)(2,1)S(1)}, u32[]{:S(2)}, u32[]{:S(2)}) %collective-permute-start.7) | collective-permute-done | bytes 524320 | tf_op jit(solution)/shard_map/ppermute | solution.py:39
  47.9 0.7 collective-permute-start.9
  48.6 1.8 %collective-permute-start.10 = (f32[32,128]{1,0:T(8,128)S(1)}, f32[32,128]{1,0:T(8,128)S(1)}, u32[]{:S(2)}, u32[]{:S(2)}) collective-permute-start(f32[32,128]{1,0:T(8,128)S(1)} %get-tuple-element.83), channel_id=1, source_target_pairs={{26,0},{0,2},{6,4},{12,6},{2,8},{8,10},{14,12},{20,14},{10,16},{16... | collective-permute-start | bytes 49160 | tf_op jit(solution)/shard_map/ppermute | solution.py:39
  50.4 1.2 collective-permute-done.8.refs_2_
  51.6 2.3 %collective-permute-done.9.refs_3_ = f32[32,128]{1,0:T(8,128)S(1)} collective-permute-done((f32[32,128]{1,0:T(8,128)S(1)}, f32[32,128]{1,0:T(8,128)S(1)}, u32[]{:S(2)}, u32[]{:S(2)}) %collective-permute-start.9) | collective-permute-done | bytes 16416 | tf_op jit(solution)/shard_map/ppermute | solution.py:39
  54.0 1.6 %collective-permute-done.10.refs_4_ = f32[32,128]{1,0:T(8,128)S(1)} collective-permute-done((f32[32,128]{1,0:T(8,128)S(1)}, f32[32,128]{1,0:T(8,128)S(1)}, u32[]{:S(2)}, u32[]{:S(2)}) %collective-permute-start.10) | collective-permute-done | bytes 16416 | tf_op jit(solution)/shard_map/ppermute | solution.py:39
  55.6 0.6 pick.3
  56.2 1.9 %collective-permute-start.11 = (bf16[64,4096]{1,0:T(8,128)(2,1)S(1)}, bf16[64,4096]{1,0:T(8,128)(2,1)S(1)}, u32[]{:S(2)}, u32[]{:S(2)}) collective-permute-start(bf16[64,4096]{1,0:T(8,128)(2,1)S(1)} %pick.3), channel_id=1, source_target_pairs={{0,26},{2,0},{4,6},{6,12},{8,2},{10,8},{12,14},{14,20},{16,10},{18... | collective-permute-start | bytes 1572872 | tf_op jit(solution)/shard_map/ppermute | solution.py:39
  58.1 0.8 combine_scores.1
  58.9 0.2 collective-permute-start.12
  59.1 2.0 %collective-permute-start.13 = (f32[32,128]{1,0:T(8,128)S(1)}, f32[32,128]{1,0:T(8,128)S(1)}, u32[]{:S(2)}, u32[]{:S(2)}) collective-permute-start(f32[32,128]{1,0:T(8,128)S(1)} %get-tuple-element.89), channel_id=1, source_target_pairs={{0,24},{2,26},{4,12},{6,14},{8,0},{10,2},{12,20},{14,22},{16,8},{1... | collective-permute-start | bytes 49160 | tf_op jit(solution)/shard_map/ppermute | solution.py:39
  61.1 1.3 collective-permute-start.14
  62.4 5.8 %collective-permute-done.11.refs_3_ = bf16[64,4096]{1,0:T(8,128)(2,1)S(1)} collective-permute-done((bf16[64,4096]{1,0:T(8,128)(2,1)S(1)}, bf16[64,4096]{1,0:T(8,128)(2,1)S(1)}, u32[]{:S(2)}, u32[]{:S(2)}) %collective-permute-start.11) | collective-permute-done | bytes 524320 | tf_op jit(solution)/shard_map/ppermute | solution.py:39
  68.2 0.2 collective-permute-done.12.refs_6_.refs_10_.refs_12_.refs_7_
  68.4 0.2 collective-permute-done.14.refs_8_.refs_12_.refs_14_
  68.6 2.1 %context.1 = (bf16[64,4096]{1,0:T(8,128)(2,1)S(1)}, bf16[64,4096]{1,0:T(8,128)(2,1)S(1)}, bf16[64,4096]{1,0:T(8,128)(2,1)S(1)}, bf16[64,4096]{1,0:T(8,128)(2,1)S(1)}, bf16[64,4096]{1,0:T(8,128)(2,1)S(1)}) custom-call(bf16[128,4096]{1,0:T(8,128)(2,1)S(1)} %copy-done.4, bf16[128,4096]{1,0:T(8,128)(2,1)S(1)} %collective-permute-done.refs_1_.refs_5_, ...), custom_call_target="tpu_custom_call" | custom-call | tf_op jit(solution)/shard_map/context/pallas_call | solution.py:393
  70.7 1.4 %collective-permute-start.15 = (bf16[64,4096]{1,0:T(8,128)(2,1)S(1)}, bf16[64,4096]{1,0:T(8,128)(2,1)S(1)}, u32[]{:S(2)}, u32[]{:S(2)}) collective-permute-start(bf16[64,4096]{1,0:T(8,128)(2,1)S(1)} %get-tuple-element.93), channel_id=1, source_target_pairs={{2,0},{0,2},{6,4},{4,6},{10,8},{8,10},{14,12},{12,14},{18,16},{16,... | collective-permute-start | bytes 1572872 | tf_op jit(solution)/shard_map/ppermute | solution.py:39
  72.1 0.6 collective-permute-start.16
  72.7 3.9 %centres.1 = (f32[32,128]{1,0:T(8,128)S(1)}, f32[32,128]{1,0:T(8,128)S(1)}, f32[32,128]{1,0:T(8,128)S(1)}, f32[32,128]{1,0:T(8,128)S(1)}, f32[32,128]{1,0:T(8,12...) custom-call(s32[1]{0:T(128)} %bitcast.place_ref, s32[2,2]{1,0:T(2,128)S(1)} %copy-done.7, ...), custom_call_target="tpu_custom_call" | custom-call | tf_op jit(solution)/shard_map/centres/pallas_call | solution.py:393
  76.6 4.9 %collective-permute-done.15.refs_2_ = bf16[64,4096]{1,0:T(8,128)(2,1)S(1)} collective-permute-done((bf16[64,4096]{1,0:T(8,128)(2,1)S(1)}, bf16[64,4096]{1,0:T(8,128)(2,1)S(1)}, u32[]{:S(2)}, u32[]{:S(2)}) %collective-permute-start.15) | collective-permute-done | bytes 524320 | tf_op jit(solution)/shard_map/ppermute | solution.py:39
  81.5 3.1 %collective-permute-done.16.refs_3_ = bf16[64,4096]{1,0:T(8,128)(2,1)S(1)} collective-permute-done((bf16[64,4096]{1,0:T(8,128)(2,1)S(1)}, bf16[64,4096]{1,0:T(8,128)(2,1)S(1)}, u32[]{:S(2)}, u32[]{:S(2)}) %collective-permute-start.16) | collective-permute-done | bytes 524320 | tf_op jit(solution)/shard_map/ppermute | solution.py:39
  84.7 1.2 collective-permute-start.17
  85.9 0.8 collective-permute-start.19
  86.7 1.7 %collective-permute-done.17.refs_2_ = f32[32,128]{1,0:T(8,128)S(1)} collective-permute-done((f32[32,128]{1,0:T(8,128)S(1)}, f32[32,128]{1,0:T(8,128)S(1)}, u32[]{:S(2)}, u32[]{:S(2)}) %collective-permute-start.17) | collective-permute-done | bytes 16416 | tf_op jit(solution)/shard_map/ppermute | solution.py:39
  88.4 3.0 %collective-permute-done.18.refs_3_ = f32[32,128]{1,0:T(8,128)S(1)} collective-permute-done((f32[32,128]{1,0:T(8,128)S(1)}, f32[32,128]{1,0:T(8,128)S(1)}, u32[]{:S(2)}, u32[]{:S(2)}) %collective-permute-start.18) | collective-permute-done | bytes 16416 | tf_op jit(solution)/shard_map/ppermute | solution.py:39
  91.4 0.9 collective-permute-done.19.refs_4_
  92.3 0.6 combine_centres.1
  92.9 0.1 collective-permute-start.20
  93.0 2.2 %collective-permute-start.22 = (f32[32,128]{1,0:T(8,128)S(1)}, f32[32,128]{1,0:T(8,128)S(1)}, u32[]{:S(2)}, u32[]{:S(2)}) collective-permute-start(f32[32,128]{1,0:T(8,128)S(1)} %get-tuple-element.111), channel_id=1, source_target_pairs={{0,24},{2,26},{4,12},{6,14},{8,0},{10,2},{12,20},{14,22},{16,8},{1... | collective-permute-start | bytes 49160 | tf_op jit(solution)/shard_map/ppermute | solution.py:39
  95.2 1.6 %collective-permute-start.23 = (f32[32,128]{1,0:T(8,128)S(1)}, f32[32,128]{1,0:T(8,128)S(1)}, u32[]{:S(2)}, u32[]{:S(2)}) collective-permute-start(f32[32,128]{1,0:T(8,128)S(1)} %get-tuple-element.112), channel_id=1, source_target_pairs={{0,26},{2,0},{4,6},{6,12},{8,2},{10,8},{12,14},{14,20},{16,10},{18... | collective-permute-start | bytes 49160 | tf_op jit(solution)/shard_map/ppermute | solution.py:39
  96.8 1.6 %collective-permute-done.20.refs_17_.refs_9_ = f32[32,128]{1,0:T(8,128)S(1)} collective-permute-done((f32[32,128]{1,0:T(8,128)S(1)}, f32[32,128]{1,0:T(8,128)S(1)}, u32[]{:S(2)}, u32[]{:S(2)}) %collective-permute-start.20) | collective-permute-done | bytes 16416 | tf_op jit(solution)/shard_map/ppermute | solution.py:39
  98.3 2.8 %collective-permute-done.23.refs_19_ = f32[32,128]{1,0:T(8,128)S(1)} collective-permute-done((f32[32,128]{1,0:T(8,128)S(1)}, f32[32,128]{1,0:T(8,128)S(1)}, u32[]{:S(2)}, u32[]{:S(2)}) %collective-permute-start.23) | collective-permute-done | bytes 16416 | tf_op jit(solution)/shard_map/ppermute | solution.py:39
  101.2 3.7 %gradient.1 = (bf16[64,4096]{1,0:T(8,128)(2,1)S(1)}, bf16[64,4096]{1,0:T(8,128)(2,1)S(1)}, bf16[64,4096]{1,0:T(8,128)(2,1)S(1)}, bf16[64,4096]{1,0:T(8,128)(2,1)...) custom-call(s32[1]{0:T(128)} %bitcast.place_ref, s32[2,2]{1,0:T(2,128)S(1)} %copy-done.7, ...), custom_call_target="tpu_custom_call" | custom-call | tf_op jit(solution)/shard_map/gradient/pallas_call | solution.py:393
  104.9 3.1 %collective-permute-done.27.refs_10_ = bf16[128,4096]{1,0:T(8,128)(2,1)S(1)} collective-permute-done((bf16[128,4096]{1,0:T(8,128)(2,1)S(1)}, bf16[128,4096]{1,0:T(8,128)(2,1)S(1)}, u32[]{:S(2)}, u32[]{:S(2)}) %collective-permute-start.27) | collective-permute-done | bytes 1048608 | tf_op jit(solution)/shard_map/ppermute | solution.py:39
  108.0 1.2 collective-permute-start.24
  109.2 4.6 %collective-permute-done.21.refs_4_ = bf16[64,4096]{1,0:T(8,128)(2,1)S(1)} collective-permute-done((bf16[64,4096]{1,0:T(8,128)(2,1)S(1)}, bf16[64,4096]{1,0:T(8,128)(2,1)S(1)}, u32[]{:S(2)}, u32[]{:S(2)}) %collective-permute-start.21) | collective-permute-done | bytes 524320 | tf_op jit(solution)/shard_map/ppermute | solution.py:39
  113.8 0.2 collective-permute-start.26
  114.0 2.6 %attended.1 = bf16[128,4096]{1,0:T(8,128)(2,1)} custom-call(s32[1]{0:T(128)} %bitcast.place_ref, s32[2,2]{1,0:T(2,128)S(1)} %copy-done.7, bf16[64,4096]{1,0:T(8,128)(2,1)S(1)} %get-tuple-element.91.refs_0_, bf16[64,4096]{1,0:T(8,128)(2,1)S(1)} %get-tuple-element.92.refs_1_, bf16[64,4096]{1,0:T(8,128)(2,1)S(1)} %collective-permute-done.15.refs_2_, ...), custom_call_target="tpu_custom_call" | custom-call | tf_op jit(solution)/shard_map/attended/pallas_call | solution.py:393
  116.6 11.6 %collective-permute-done.28.refs_11_ = bf16[128,4096]{1,0:T(8,128)(2,1)S(1)} collective-permute-done((bf16[128,4096]{1,0:T(8,128)(2,1)S(1)}, bf16[128,4096]{1,0:T(8,128)(2,1)S(1)}, u32[]{:S(2)}, u32[]{:S(2)}) %collective-permute-start.28) | collective-permute-done | bytes 1048608 | tf_op jit(solution)/shard_map/ppermute | solution.py:39
  128.1 3.5 %own.1 = (bf16[128,4096]{1,0:T(8,128)(2,1)}, bf16[128,4096]{1,0:T(8,128)(2,1)}) custom-call(s32[1]{0:T(128)} %bitcast.place_ref, s32[2,2]{1,0:T(2,128)S(1)} %copy-done.7, bf16[128,4096]{1,0:T(8,128)(2,1)S(1)} %get-tuple-element.67.refs_0_, bf16[64,4096]{1,0:T(8,128)(2,1)S(1)} %collective-permute-done.2.refs_1_, bf16[128,4096]{1,0:T(8,128)(2,1)S(1)} %copy-done, ...), custom_call_target="tpu_custom_call" | custom-call | tf_op jit(solution)/shard_map/own/pallas_call | solution.py:393
  131.6 1.1 collective-permute-done.26.refs_4_
  132.7 2.0 %inner.1 = (f32[128,4096]{1,0:T(8,128)S(1)}, f32[1,128]{1,0:T(1,128)S(1)}) custom-call(s32[1]{0:T(128)} %bitcast.place_ref, s32[2,2]{1,0:T(2,128)S(1)} %copy-done.7, bf16[64,4096]{1,0:T(8,128)(2,1)S(1)} %get-tuple-element.113.refs_0_, bf16[64,4096]{1,0:T(8,128)(2,1)S(1)} %get-tuple-element.114.refs_1_, bf16[64,4096]{1,0:T(8,128)(2,1)S(1)} %collective-permute-done.24.refs_2_, ...), custom_call_target="tpu_custom_call" | custom-call | tf_op jit(solution)/shard_map/inner/pallas_call | solution.py:393
  134.7 0.1 collective-permute-start.29
  134.8 1.1 collective-permute-done.29.refs_3_
  135.9 1.6 %finish.1 = bf16[128,4096]{1,0:T(8,128)(2,1)} custom-call(f32[128,4096]{1,0:T(8,128)S(1)} %get-tuple-element.127.scaled_ref, bf16[128,4096]{1,0:T(8,128)(2,1)S(1)} %copy-done.3, f32[1,128]{1,0:T(1,128)S(1)} %squares.1.refs_0_, f32[1,128]{1,0:T(1,128)S(1)} %collective-permute-done.1.refs_1_, f32[1,128]{1,0:T(1,128)S(1)} %get-tuple-element.128.refs_2_, ...), custom_call_target="tpu_custom_call" | custom-call | tf_op jit(solution)/shard_map/finish/pallas_call | solution.py:393
  (30 shorter events, 0.1 us)
Async XLA Ops:
  0.6 14.0 %copy-start = (bf16[128,4096]{1,0:T(8,128)(2,1)S(1)}, bf16[128,4096]{1,0:T(8,128)(2,1)}, u32[]{:S(2)}) copy-start(bf16[128,4096]{1,0:T(8,128)(2,1)} %refs_2_.1) | copy-start | bytes 3145732
  0.6 1.3 copy-start.1
  2.0 12.7 %copy-start.7 = (s32[2,2]{1,0:T(2,128)S(1)}, s32[2,2]{1,0:T(2,128)}, u32[]{:S(2)}) copy-start(s32[2,2]{1,0:T(2,128)} %near_ref.21) | copy-start | bytes 52
  2.3 3.1 %collective-permute-start.1 = (f32[1,128]{1,0:T(1,128)S(1)}, f32[1,128]{1,0:T(1,128)S(1)}, u32[]{:S(2)}, u32[]{:S(2)}) collective-permute-start(f32[1,128]{1,0:T(1,128)S(1)} %squares.1.refs_0_), channel_id=1, source_target_pairs={{0,1},{1,0},{2,3},{3,2},{4,5},{5,4},{6,7},{7,6},{8,9},{9,8},{10,11... | collective-permute-start | bytes 1544 | tf_op jit(solution)/shard_map/ppermute | solution.py:373
  2.8 35.0 %collective-permute-start.5 = (bf16[128,4096]{1,0:T(8,128)(2,1)}, bf16[128,4096]{1,0:T(8,128)(2,1)S(1)}, u32[]{:S(2)}, u32[]{:S(2)}) collective-permute-start(bf16[128,4096]{1,0:T(8,128)(2,1)} %refs_4_.5), channel_id=1, source_target_pairs={{0,4},{2,6},{4,0},{6,2},{8,12},{10,14},{12,8},{14,10},{16,20},{18,... | collective-permute-start | bytes 3145736 | tf_op jit(solution)/shard_map/ppermute | solution.py:39
  5.4 1.2 copy-start.2
  6.6 0.7 copy-start.6
  7.3 0.7 copy-start.8
  8.0 19.5 %copy-start.4 = (bf16[128,4096]{1,0:T(8,128)(2,1)S(1)}, bf16[128,4096]{1,0:T(8,128)(2,1)}, u32[]{:S(2)}) copy-start(bf16[128,4096]{1,0:T(8,128)(2,1)} %refs_4_.4) | copy-start | bytes 3145732
  8.0 29.8 %copy-start.5 = (bf16[128,4096]{1,0:T(8,128)(2,1)S(1)}, bf16[128,4096]{1,0:T(8,128)(2,1)}, u32[]{:S(2)}) copy-start(bf16[128,4096]{1,0:T(8,128)(2,1)} %refs_4_.5) | copy-start | bytes 3145732
  9.0 14.8 %collective-permute-start.2 = (bf16[64,4096]{1,0:T(8,128)(2,1)S(1)}, bf16[64,4096]{1,0:T(8,128)(2,1)S(1)}, u32[]{:S(2)}, u32[]{:S(2)}) collective-permute-start(bf16[64,4096]{1,0:T(8,128)(2,1)S(1)} %get-tuple-element.68), channel_id=1, source_target_pairs={{0,2},{2,0},{4,6},{6,4},{8,10},{10,8},{12,14},{14,12},{16,18},{18,... | collective-permute-start | bytes 1572872 | tf_op jit(solution)/shard_map/ppermute | solution.py:39
  10.6 16.9 %collective-permute-start.3 = (bf16[64,4096]{1,0:T(8,128)(2,1)S(1)}, bf16[64,4096]{1,0:T(8,128)(2,1)S(1)}, u32[]{:S(2)}, u32[]{:S(2)}) collective-permute-start(bf16[64,4096]{1,0:T(8,128)(2,1)S(1)} %get-tuple-element.69), channel_id=1, source_target_pairs={{0,24},{2,26},{4,12},{6,14},{8,0},{10,2},{12,20},{14,22},{16,8},{1... | collective-permute-start | bytes 1572872 | tf_op jit(solution)/shard_map/ppermute | solution.py:39
  14.2 23.6 %collective-permute-start.4 = (bf16[64,4096]{1,0:T(8,128)(2,1)S(1)}, bf16[64,4096]{1,0:T(8,128)(2,1)S(1)}, u32[]{:S(2)}, u32[]{:S(2)}) collective-permute-start(bf16[64,4096]{1,0:T(8,128)(2,1)S(1)} %get-tuple-element.70), channel_id=1, source_target_pairs={{0,26},{2,0},{4,6},{6,12},{8,2},{10,8},{12,14},{14,20},{16,10},{18... | collective-permute-start | bytes 1572872 | tf_op jit(solution)/shard_map/ppermute | solution.py:39
  15.3 30.3 %collective-permute-start.6 = (bf16[64,4096]{1,0:T(8,128)(2,1)S(1)}, bf16[64,4096]{1,0:T(8,128)(2,1)S(1)}, u32[]{:S(2)}, u32[]{:S(2)}) collective-permute-start(bf16[64,4096]{1,0:T(8,128)(2,1)S(1)} %get-tuple-element.79), channel_id=1, source_target_pairs={{0,2},{2,0},{4,6},{6,4},{8,10},{10,8},{12,14},{14,12},{16,18},{18,... | collective-permute-start | bytes 1572872 | tf_op jit(solution)/shard_map/ppermute | solution.py:39
  23.9 24.0 %collective-permute-start.7 = (bf16[64,4096]{1,0:T(8,128)(2,1)S(1)}, bf16[64,4096]{1,0:T(8,128)(2,1)S(1)}, u32[]{:S(2)}, u32[]{:S(2)}) collective-permute-start(bf16[64,4096]{1,0:T(8,128)(2,1)S(1)} %get-tuple-element.80), channel_id=1, source_target_pairs={{0,24},{2,26},{4,12},{6,14},{8,0},{10,2},{12,20},{14,22},{16,8},{1... | collective-permute-start | bytes 1572872 | tf_op jit(solution)/shard_map/ppermute | solution.py:39
  27.5 40.8 %collective-permute-start = (bf16[128,4096]{1,0:T(8,128)(2,1)S(1)}, bf16[128,4096]{1,0:T(8,128)(2,1)S(1)}, u32[]{:S(2)}, u32[]{:S(2)}) collective-permute-start(bf16[128,4096]{1,0:T(8,128)(2,1)S(1)} %copy-done.4), channel_id=1, source_target_pairs={{0,4},{2,6},{4,0},{6,2},{8,12},{10,14},{12,8},{14,10},{16,20},{18,... | collective-permute-start | bytes 3145736 | tf_op jit(solution)/shard_map/ppermute | solution.py:39
  47.9 3.7 %collective-permute-start.8 = (f32[32,128]{1,0:T(8,128)S(1)}, f32[32,128]{1,0:T(8,128)S(1)}, u32[]{:S(2)}, u32[]{:S(2)}) collective-permute-start(f32[32,128]{1,0:T(8,128)S(1)} %get-tuple-element.81), channel_id=1, source_target_pairs={{2,0},{0,2},{6,4},{4,6},{10,8},{8,10},{14,12},{12,14},{18,16},{16,... | collective-permute-start | bytes 49160 | tf_op jit(solution)/shard_map/ppermute | solution.py:39
  47.9 6.0 %collective-permute-start.9 = (f32[32,128]{1,0:T(8,128)S(1)}, f32[32,128]{1,0:T(8,128)S(1)}, u32[]{:S(2)}, u32[]{:S(2)}) collective-permute-start(f32[32,128]{1,0:T(8,128)S(1)} %get-tuple-element.82), channel_id=1, source_target_pairs={{24,0},{26,2},{12,4},{14,6},{0,8},{2,10},{20,12},{22,14},{8,16},{1... | collective-permute-start | bytes 49160 | tf_op jit(solution)/shard_map/ppermute | solution.py:39
  48.6 6.9 %collective-permute-start.10 = (f32[32,128]{1,0:T(8,128)S(1)}, f32[32,128]{1,0:T(8,128)S(1)}, u32[]{:S(2)}, u32[]{:S(2)}) collective-permute-start(f32[32,128]{1,0:T(8,128)S(1)} %get-tuple-element.83), channel_id=1, source_target_pairs={{26,0},{0,2},{6,4},{12,6},{2,8},{8,10},{14,12},{20,14},{10,16},{16... | collective-permute-start | bytes 49160 | tf_op jit(solution)/shard_map/ppermute | solution.py:39
  56.2 12.1 %collective-permute-start.11 = (bf16[64,4096]{1,0:T(8,128)(2,1)S(1)}, bf16[64,4096]{1,0:T(8,128)(2,1)S(1)}, u32[]{:S(2)}, u32[]{:S(2)}) collective-permute-start(bf16[64,4096]{1,0:T(8,128)(2,1)S(1)} %pick.3), channel_id=1, source_target_pairs={{0,26},{2,0},{4,6},{6,12},{8,2},{10,8},{12,14},{14,20},{16,10},{18... | collective-permute-start | bytes 1572872 | tf_op jit(solution)/shard_map/ppermute | solution.py:39
  58.9 9.5 %collective-permute-start.12 = (f32[32,128]{1,0:T(8,128)S(1)}, f32[32,128]{1,0:T(8,128)S(1)}, u32[]{:S(2)}, u32[]{:S(2)}) collective-permute-start(f32[32,128]{1,0:T(8,128)S(1)} %get-tuple-element.88), channel_id=1, source_target_pairs={{0,2},{2,0},{4,6},{6,4},{8,10},{10,8},{12,14},{14,12},{16,18},{18,... | collective-permute-start | bytes 49160 | tf_op jit(solution)/shard_map/ppermute | solution.py:39
  59.1 9.3 %collective-permute-start.13 = (f32[32,128]{1,0:T(8,128)S(1)}, f32[32,128]{1,0:T(8,128)S(1)}, u32[]{:S(2)}, u32[]{:S(2)}) collective-permute-start(f32[32,128]{1,0:T(8,128)S(1)} %get-tuple-element.89), channel_id=1, source_target_pairs={{0,24},{2,26},{4,12},{6,14},{8,0},{10,2},{12,20},{14,22},{16,8},{1... | collective-permute-start | bytes 49160 | tf_op jit(solution)/shard_map/ppermute | solution.py:39
  61.1 7.5 %collective-permute-start.14 = (f32[32,128]{1,0:T(8,128)S(1)}, f32[32,128]{1,0:T(8,128)S(1)}, u32[]{:S(2)}, u32[]{:S(2)}) collective-permute-start(f32[32,128]{1,0:T(8,128)S(1)} %get-tuple-element.90), channel_id=1, source_target_pairs={{0,26},{2,0},{4,6},{6,12},{8,2},{10,8},{12,14},{14,20},{16,10},{18... | collective-permute-start | bytes 49160 | tf_op jit(solution)/shard_map/ppermute | solution.py:39
  70.7 10.8 %collective-permute-start.15 = (bf16[64,4096]{1,0:T(8,128)(2,1)S(1)}, bf16[64,4096]{1,0:T(8,128)(2,1)S(1)}, u32[]{:S(2)}, u32[]{:S(2)}) collective-permute-start(bf16[64,4096]{1,0:T(8,128)(2,1)S(1)} %get-tuple-element.93), channel_id=1, source_target_pairs={{2,0},{0,2},{6,4},{4,6},{10,8},{8,10},{14,12},{12,14},{18,16},{16,... | collective-permute-start | bytes 1572872 | tf_op jit(solution)/shard_map/ppermute | solution.py:39
  72.1 12.5 %collective-permute-start.16 = (bf16[64,4096]{1,0:T(8,128)(2,1)S(1)}, bf16[64,4096]{1,0:T(8,128)(2,1)S(1)}, u32[]{:S(2)}, u32[]{:S(2)}) collective-permute-start(bf16[64,4096]{1,0:T(8,128)(2,1)S(1)} %get-tuple-element.94), channel_id=1, source_target_pairs={{24,0},{26,2},{12,4},{14,6},{0,8},{2,10},{20,12},{22,14},{8,16},{1... | collective-permute-start | bytes 1572872 | tf_op jit(solution)/shard_map/ppermute | solution.py:39
  84.7 23.3 %collective-permute-start.27 = (bf16[128,4096]{1,0:T(8,128)(2,1)S(1)}, bf16[128,4096]{1,0:T(8,128)(2,1)S(1)}, u32[]{:S(2)}, u32[]{:S(2)}) collective-permute-start(bf16[128,4096]{1,0:T(8,128)(2,1)S(1)} %get-tuple-element.120), channel_id=1, source_target_pairs={{0,4},{2,6},{4,0},{6,2},{8,12},{10,14},{12,8},{14,10},{16,20},{18,... | collective-permute-start | bytes 3145736 | tf_op jit(solution)/shard_map/ppermute | solution.py:39
  84.7 3.7 %collective-permute-start.17 = (f32[32,128]{1,0:T(8,128)S(1)}, f32[32,128]{1,0:T(8,128)S(1)}, u32[]{:S(2)}, u32[]{:S(2)}) collective-permute-start(f32[32,128]{1,0:T(8,128)S(1)} %get-tuple-element.102), channel_id=1, source_target_pairs={{2,0},{0,2},{6,4},{4,6},{10,8},{8,10},{14,12},{12,14},{18,16},{16,... | collective-permute-start | bytes 49160 | tf_op jit(solution)/shard_map/ppermute | solution.py:39
  85.9 5.5 %collective-permute-start.18 = (f32[32,128]{1,0:T(8,128)S(1)}, f32[32,128]{1,0:T(8,128)S(1)}, u32[]{:S(2)}, u32[]{:S(2)}) collective-permute-start(f32[32,128]{1,0:T(8,128)S(1)} %get-tuple-element.103), channel_id=1, source_target_pairs={{24,0},{26,2},{12,4},{14,6},{0,8},{2,10},{20,12},{22,14},{8,16},{1... | collective-permute-start | bytes 49160 | tf_op jit(solution)/shard_map/ppermute | solution.py:39
  85.9 6.4 %collective-permute-start.19 = (f32[32,128]{1,0:T(8,128)S(1)}, f32[32,128]{1,0:T(8,128)S(1)}, u32[]{:S(2)}, u32[]{:S(2)}) collective-permute-start(f32[32,128]{1,0:T(8,128)S(1)} %get-tuple-element.104), channel_id=1, source_target_pairs={{26,0},{0,2},{6,4},{12,6},{2,8},{8,10},{14,12},{20,14},{10,16},{16... | collective-permute-start | bytes 49160 | tf_op jit(solution)/shard_map/ppermute | solution.py:39
  92.9 5.4 %collective-permute-start.20 = (f32[32,128]{1,0:T(8,128)S(1)}, f32[32,128]{1,0:T(8,128)S(1)}, u32[]{:S(2)}, u32[]{:S(2)}) collective-permute-start(f32[32,128]{1,0:T(8,128)S(1)} %get-tuple-element.105), channel_id=1, source_target_pairs={{0,2},{2,0},{4,6},{6,4},{8,10},{10,8},{12,14},{14,12},{16,18},{18,... | collective-permute-start | bytes 49160 | tf_op jit(solution)/shard_map/ppermute | solution.py:39
  93.0 5.3 %collective-permute-start.22 = (f32[32,128]{1,0:T(8,128)S(1)}, f32[32,128]{1,0:T(8,128)S(1)}, u32[]{:S(2)}, u32[]{:S(2)}) collective-permute-start(f32[32,128]{1,0:T(8,128)S(1)} %get-tuple-element.111), channel_id=1, source_target_pairs={{0,24},{2,26},{4,12},{6,14},{8,0},{10,2},{12,20},{14,22},{16,8},{1... | collective-permute-start | bytes 49160 | tf_op jit(solution)/shard_map/ppermute | solution.py:39
  95.2 6.0 %collective-permute-start.23 = (f32[32,128]{1,0:T(8,128)S(1)}, f32[32,128]{1,0:T(8,128)S(1)}, u32[]{:S(2)}, u32[]{:S(2)}) collective-permute-start(f32[32,128]{1,0:T(8,128)S(1)} %get-tuple-element.112), channel_id=1, source_target_pairs={{0,26},{2,0},{4,6},{6,12},{8,2},{10,8},{12,14},{14,20},{16,10},{18... | collective-permute-start | bytes 49160 | tf_op jit(solution)/shard_map/ppermute | solution.py:39
  98.3 15.5 %collective-permute-start.21 = (bf16[64,4096]{1,0:T(8,128)(2,1)S(1)}, bf16[64,4096]{1,0:T(8,128)(2,1)S(1)}, u32[]{:S(2)}, u32[]{:S(2)}) collective-permute-start(bf16[64,4096]{1,0:T(8,128)(2,1)S(1)} %get-tuple-element.106), channel_id=1, source_target_pairs={{26,0},{0,2},{6,4},{12,6},{2,8},{8,10},{14,12},{20,14},{10,16},{16... | collective-permute-start | bytes 1572872 | tf_op jit(solution)/shard_map/ppermute | solution.py:39
  108.0 20.2 %collective-permute-start.28 = (bf16[128,4096]{1,0:T(8,128)(2,1)S(1)}, bf16[128,4096]{1,0:T(8,128)(2,1)S(1)}, u32[]{:S(2)}, u32[]{:S(2)}) collective-permute-start(bf16[128,4096]{1,0:T(8,128)(2,1)S(1)} %get-tuple-element.122), channel_id=1, source_target_pairs={{0,4},{2,6},{4,0},{6,2},{8,12},{10,14},{12,8},{14,10},{16,20},{18,... | collective-permute-start | bytes 3145736 | tf_op jit(solution)/shard_map/ppermute | solution.py:39
  108.0 23.7 %collective-permute-start.24 = (bf16[64,4096]{1,0:T(8,128)(2,1)S(1)}, bf16[64,4096]{1,0:T(8,128)(2,1)S(1)}, u32[]{:S(2)}, u32[]{:S(2)}) collective-permute-start(bf16[64,4096]{1,0:T(8,128)(2,1)S(1)} %get-tuple-element.115), channel_id=1, source_target_pairs={{2,0},{0,2},{6,4},{4,6},{10,8},{8,10},{14,12},{12,14},{18,16},{16,... | collective-permute-start | bytes 1572872 | tf_op jit(solution)/shard_map/ppermute | solution.py:39
  109.2 22.4 %collective-permute-start.25 = (bf16[64,4096]{1,0:T(8,128)(2,1)S(1)}, bf16[64,4096]{1,0:T(8,128)(2,1)S(1)}, u32[]{:S(2)}, u32[]{:S(2)}) collective-permute-start(bf16[64,4096]{1,0:T(8,128)(2,1)S(1)} %get-tuple-element.116), channel_id=1, source_target_pairs={{24,0},{26,2},{12,4},{14,6},{0,8},{2,10},{20,12},{22,14},{8,16},{1... | collective-permute-start | bytes 1572872 | tf_op jit(solution)/shard_map/ppermute | solution.py:39
  113.8 18.9 %collective-permute-start.26 = (bf16[64,4096]{1,0:T(8,128)(2,1)S(1)}, bf16[64,4096]{1,0:T(8,128)(2,1)S(1)}, u32[]{:S(2)}, u32[]{:S(2)}) collective-permute-start(bf16[64,4096]{1,0:T(8,128)(2,1)S(1)} %get-tuple-element.118), channel_id=1, source_target_pairs={{26,0},{0,2},{6,4},{12,6},{2,8},{8,10},{14,12},{20,14},{10,16},{16... | collective-permute-start | bytes 1572872 | tf_op jit(solution)/shard_map/ppermute | solution.py:39
  116.6 16.1 %copy-start.3 = (bf16[128,4096]{1,0:T(8,128)(2,1)S(1)}, bf16[128,4096]{1,0:T(8,128)(2,1)}, u32[]{:S(2)}) copy-start(bf16[128,4096]{1,0:T(8,128)(2,1)} %q_ref.5) | copy-start | bytes 3145732
  116.6 16.1 %copy-start.9 = (f32[4096]{0:T(1024)S(1)}, f32[4096]{0:T(1024)}, u32[]{:S(2)}) copy-start(f32[4096]{0:T(1024)} %param.7) | copy-start | bytes 49156
  134.7 1.2 collective-permute-start.29

commit v3 on v2

--- a/solution.py
+++ b/solution.py
@@ -14,7 +14,7 @@
 EPSILON = 1e-06
 SCALING = 1.0 / HS**0.5
 LANES = 128
-CHUNK = 8
+CHUNK = 16
 VMEM_LIMIT = 8 * 1024 * 1024
 WORK = 8 * 1024 * 1024
 SLOTS = 5
@@ -476,8 +476,8 @@
     centres[2:] = after(centres[2:], contexts[2], contexts[3])
     centres = come(centres)
     centres = placed(combine_centres_kernel, "combine_centres", [stat] * SLOTS)(*centres)
+    contexts[4] = home(after(contexts[4], centres[1]), 4)
     centres = go(centres)
-    contexts[4] = home(after(contexts[4], centres[2]), 4)
 
     *grads, far_dk = placed(gradient_kernel, "gradient", [slot] * SLOTS + [tall])(
         normed, *q_slots, keys, far_keys, own_weights, far_weights, own_products, far_products,

time: 138 us -> 136 us (0.986)
  Pallas kernels: 27.2 us -> 25.6 us
    pallas_call x14, Pallas kernels: 27.2 us -> 25.6 us  [call(): pl.pallas_call(body, in_specs=[pl.BlockSpec(memory_space=pltpu.SMEM)] * s...]
  transfers between devices with their start and end apart: 30 -> 30, of which waited for: 22 -> 21; matrix products, arithmetic and copies ran while one was open for 0% -> 0% of each run, Pallas kernels for 15% -> 15%
where the time goes in v3:
time: 136 us
  waiting for transfers between devices  73.8 us (54%)
  starting transfers between devices  31.8 us (23%)
  Pallas kernels  25.6 us (19%)
  local copies, waits for them, and re-layouts  3.95 us (3%)
    ppermute x28, waiting for transfers between devices, sent(): return lax.ppermute(array, 'dp', route)  72.7 us
    ppermute x28, starting transfers between devices, sent(): return lax.ppermute(array, 'dp', route)  31.2 us
    pallas_call x14, Pallas kernels, call(): pl.pallas_call(body, in_specs=[pl.BlockSpec(memory_space=pltpu.SMEM)] * s...  25.6 us
    unnamed x20, local copies, waits for them, and re-layouts  3.95 us
  transfers between devices with their start and end apart: 30, of which 21 were waited for; matrix products, arithmetic and copies ran while one was open for 0% of the time, Pallas kernels for 15%

profile of v3, /device:TPU:0, one launch (start us, length us, event | category | flops | bytes accessed | tf_op | source)
XLA Modules:
  0.0 136.0 jit_solution(11291585846733962622)
XLA Ops:
  0.6 0.0 copy-start.1
  0.7 1.3 copy-done.1
  2.0 0.3 squares.1.refs_0_
  2.3 0.5 collective-permute-start.1
  2.8 2.6 %collective-permute-start.5 = (bf16[128,4096]{1,0:T(8,128)(2,1)}, bf16[128,4096]{1,0:T(8,128)(2,1)S(1)}, u32[]{:S(2)}, u32[]{:S(2)}) collective-permute-start(bf16[128,4096]{1,0:T(8,128)(2,1)} %refs_4_.5), channel_id=1, source_target_pairs={{0,4},{2,6},{4,0},{6,2},{8,12},{10,14},{12,8},{14,10},{16,20},{18,... | collective-permute-start | bytes 3145736 | tf_op jit(solution)/shard_map/ppermute | solution.py:39
  5.4 1.2 copy-done.2
  6.6 0.7 copy-done.6
  7.3 0.7 copy-done.8
  8.0 1.0 prepare_queries.1
  9.0 1.6 %collective-permute-start.2 = (bf16[64,4096]{1,0:T(8,128)(2,1)S(1)}, bf16[64,4096]{1,0:T(8,128)(2,1)S(1)}, u32[]{:S(2)}, u32[]{:S(2)}) collective-permute-start(bf16[64,4096]{1,0:T(8,128)(2,1)S(1)} %get-tuple-element.68), channel_id=1, source_target_pairs={{0,2},{2,0},{4,6},{6,4},{8,10},{10,8},{12,14},{14,12},{16,18},{18,... | collective-permute-start | bytes 1572872 | tf_op jit(solution)/shard_map/ppermute | solution.py:39
  10.6 3.6 %collective-permute-start.3 = (bf16[64,4096]{1,0:T(8,128)(2,1)S(1)}, bf16[64,4096]{1,0:T(8,128)(2,1)S(1)}, u32[]{:S(2)}, u32[]{:S(2)}) collective-permute-start(bf16[64,4096]{1,0:T(8,128)(2,1)S(1)} %get-tuple-element.69), channel_id=1, source_target_pairs={{0,24},{2,26},{4,12},{6,14},{8,0},{10,2},{12,20},{14,22},{16,8},{1... | collective-permute-start | bytes 1572872 | tf_op jit(solution)/shard_map/ppermute | solution.py:39
  14.2 0.4 collective-permute-start.4
  14.6 0.6 pick.2
  15.3 1.7 %collective-permute-start.6 = (bf16[64,4096]{1,0:T(8,128)(2,1)S(1)}, bf16[64,4096]{1,0:T(8,128)(2,1)S(1)}, u32[]{:S(2)}, u32[]{:S(2)}) collective-permute-start(bf16[64,4096]{1,0:T(8,128)(2,1)S(1)} %get-tuple-element.79), channel_id=1, source_target_pairs={{0,2},{2,0},{4,6},{6,4},{8,10},{10,8},{12,14},{14,12},{16,18},{18,... | collective-permute-start | bytes 1572872 | tf_op jit(solution)/shard_map/ppermute | solution.py:39
  16.9 6.9 %collective-permute-done.2.refs_1_ = bf16[64,4096]{1,0:T(8,128)(2,1)S(1)} collective-permute-done((bf16[64,4096]{1,0:T(8,128)(2,1)S(1)}, bf16[64,4096]{1,0:T(8,128)(2,1)S(1)}, u32[]{:S(2)}, u32[]{:S(2)}) %collective-permute-start.2) | collective-permute-done | bytes 524320 | tf_op jit(solution)/shard_map/ppermute | solution.py:39
  23.9 3.6 %collective-permute-start.7 = (bf16[64,4096]{1,0:T(8,128)(2,1)S(1)}, bf16[64,4096]{1,0:T(8,128)(2,1)S(1)}, u32[]{:S(2)}, u32[]{:S(2)}) collective-permute-start(bf16[64,4096]{1,0:T(8,128)(2,1)S(1)} %get-tuple-element.80), channel_id=1, source_target_pairs={{0,24},{2,26},{4,12},{6,14},{8,0},{10,2},{12,20},{14,22},{16,8},{1... | collective-permute-start | bytes 1572872 | tf_op jit(solution)/shard_map/ppermute | solution.py:39
  27.5 10.3 %collective-permute-done.4.refs_3_ = bf16[64,4096]{1,0:T(8,128)(2,1)S(1)} collective-permute-done((bf16[64,4096]{1,0:T(8,128)(2,1)S(1)}, bf16[64,4096]{1,0:T(8,128)(2,1)S(1)}, u32[]{:S(2)}, u32[]{:S(2)}) %collective-permute-start.4) | collective-permute-done | bytes 524320 | tf_op jit(solution)/shard_map/ppermute | solution.py:39
  37.8 3.6 %scores.1 = (f32[32,128]{1,0:T(8,128)S(1)}, f32[32,128]{1,0:T(8,128)S(1)}, f32[32,128]{1,0:T(8,128)S(1)}, f32[32,128]{1,0:T(8,128)S(1)}, f32[32,128]{1,0:T(8,128...) custom-call(s32[1]{0:T(128)} %bitcast.place_ref, s32[2,2]{1,0:T(2,128)S(1)} %copy-done.7, ...), custom_call_target="tpu_custom_call" | custom-call | tf_op jit(solution)/shard_map/scores/pallas_call | solution.py:393
  41.4 4.2 %collective-permute-done.6.refs_1_.refs_3_ = bf16[64,4096]{1,0:T(8,128)(2,1)S(1)} collective-permute-done((bf16[64,4096]{1,0:T(8,128)(2,1)S(1)}, bf16[64,4096]{1,0:T(8,128)(2,1)S(1)}, u32[]{:S(2)}, u32[]{:S(2)}) %collective-permute-start.6) | collective-permute-done | bytes 524320 | tf_op jit(solution)/shard_map/ppermute | solution.py:39
  45.6 2.3 %collective-permute-done.7.refs_2_ = bf16[64,4096]{1,0:T(8,128)(2,1)S(1)} collective-permute-done((bf16[64,4096]{1,0:T(8,128)(2,1)S(1)}, bf16[64,4096]{1,0:T(8,128)(2,1)S(1)}, u32[]{:S(2)}, u32[]{:S(2)}) %collective-permute-start.7) | collective-permute-done | bytes 524320 | tf_op jit(solution)/shard_map/ppermute | solution.py:39
  47.9 0.7 collective-permute-start.9
  48.6 1.8 %collective-permute-start.10 = (f32[32,128]{1,0:T(8,128)S(1)}, f32[32,128]{1,0:T(8,128)S(1)}, u32[]{:S(2)}, u32[]{:S(2)}) collective-permute-start(f32[32,128]{1,0:T(8,128)S(1)} %get-tuple-element.83), channel_id=1, source_target_pairs={{26,0},{0,2},{6,4},{12,6},{2,8},{8,10},{14,12},{20,14},{10,16},{16... | collective-permute-start | bytes 49160 | tf_op jit(solution)/shard_map/ppermute | solution.py:39
  50.4 1.2 collective-permute-done.8.refs_2_
  51.6 2.3 %collective-permute-done.9.refs_3_ = f32[32,128]{1,0:T(8,128)S(1)} collective-permute-done((f32[32,128]{1,0:T(8,128)S(1)}, f32[32,128]{1,0:T(8,128)S(1)}, u32[]{:S(2)}, u32[]{:S(2)}) %collective-permute-start.9) | collective-permute-done | bytes 16416 | tf_op jit(solution)/shard_map/ppermute | solution.py:39
  54.0 1.6 %collective-permute-done.10.refs_4_ = f32[32,128]{1,0:T(8,128)S(1)} collective-permute-done((f32[32,128]{1,0:T(8,128)S(1)}, f32[32,128]{1,0:T(8,128)S(1)}, u32[]{:S(2)}, u32[]{:S(2)}) %collective-permute-start.10) | collective-permute-done | bytes 16416 | tf_op jit(solution)/shard_map/ppermute | solution.py:39
  55.6 0.6 pick.3
  56.2 1.9 %collective-permute-start.11 = (bf16[64,4096]{1,0:T(8,128)(2,1)S(1)}, bf16[64,4096]{1,0:T(8,128)(2,1)S(1)}, u32[]{:S(2)}, u32[]{:S(2)}) collective-permute-start(bf16[64,4096]{1,0:T(8,128)(2,1)S(1)} %pick.3), channel_id=1, source_target_pairs={{0,26},{2,0},{4,6},{6,12},{8,2},{10,8},{12,14},{14,20},{16,10},{18... | collective-permute-start | bytes 1572872 | tf_op jit(solution)/shard_map/ppermute | solution.py:39
  58.1 0.8 combine_scores.1
  58.9 0.2 collective-permute-start.12
  59.1 2.0 %collective-permute-start.13 = (f32[32,128]{1,0:T(8,128)S(1)}, f32[32,128]{1,0:T(8,128)S(1)}, u32[]{:S(2)}, u32[]{:S(2)}) collective-permute-start(f32[32,128]{1,0:T(8,128)S(1)} %get-tuple-element.89), channel_id=1, source_target_pairs={{0,24},{2,26},{4,12},{6,14},{8,0},{10,2},{12,20},{14,22},{16,8},{1... | collective-permute-start | bytes 49160 | tf_op jit(solution)/shard_map/ppermute | solution.py:39
  61.1 1.3 collective-permute-start.14
  62.4 5.8 %collective-permute-done.11.refs_3_ = bf16[64,4096]{1,0:T(8,128)(2,1)S(1)} collective-permute-done((bf16[64,4096]{1,0:T(8,128)(2,1)S(1)}, bf16[64,4096]{1,0:T(8,128)(2,1)S(1)}, u32[]{:S(2)}, u32[]{:S(2)}) %collective-permute-start.11) | collective-permute-done | bytes 524320 | tf_op jit(solution)/shard_map/ppermute | solution.py:39
  68.2 0.2 collective-permute-done.12.refs_6_.refs_10_.refs_12_.refs_7_
  68.4 0.2 collective-permute-done.14.refs_8_.refs_12_.refs_14_
  68.6 1.6 %context.1 = (bf16[64,4096]{1,0:T(8,128)(2,1)S(1)}, bf16[64,4096]{1,0:T(8,128)(2,1)S(1)}, bf16[64,4096]{1,0:T(8,128)(2,1)S(1)}, bf16[64,4096]{1,0:T(8,128)(2,1)S(1)}, bf16[64,4096]{1,0:T(8,128)(2,1)S(1)}) custom-call(bf16[128,4096]{1,0:T(8,128)(2,1)S(1)} %copy-done.4, bf16[128,4096]{1,0:T(8,128)(2,1)S(1)} %collective-permute-done.refs_1_.refs_5_, ...), custom_call_target="tpu_custom_call" | custom-call | tf_op jit(solution)/shard_map/context/pallas_call | solution.py:393
  70.2 1.4 %collective-permute-start.15 = (bf16[64,4096]{1,0:T(8,128)(2,1)S(1)}, bf16[64,4096]{1,0:T(8,128)(2,1)S(1)}, u32[]{:S(2)}, u32[]{:S(2)}) collective-permute-start(bf16[64,4096]{1,0:T(8,128)(2,1)S(1)} %get-tuple-element.93), channel_id=1, source_target_pairs={{2,0},{0,2},{6,4},{4,6},{10,8},{8,10},{14,12},{12,14},{18,16},{16,... | collective-permute-start | bytes 1572872 | tf_op jit(solution)/shard_map/ppermute | solution.py:39
  71.6 0.6 collective-permute-start.16
  72.2 3.6 %centres.1 = (f32[32,128]{1,0:T(8,128)S(1)}, f32[32,128]{1,0:T(8,128)S(1)}, f32[32,128]{1,0:T(8,128)S(1)}, f32[32,128]{1,0:T(8,128)S(1)}, f32[32,128]{1,0:T(8,12...) custom-call(s32[1]{0:T(128)} %bitcast.place_ref, s32[2,2]{1,0:T(2,128)S(1)} %copy-done.7, ...), custom_call_target="tpu_custom_call" | custom-call | tf_op jit(solution)/shard_map/centres/pallas_call | solution.py:393
  75.8 5.2 %collective-permute-done.15.refs_2_ = bf16[64,4096]{1,0:T(8,128)(2,1)S(1)} collective-permute-done((bf16[64,4096]{1,0:T(8,128)(2,1)S(1)}, bf16[64,4096]{1,0:T(8,128)(2,1)S(1)}, u32[]{:S(2)}, u32[]{:S(2)}) %collective-permute-start.15) | collective-permute-done | bytes 524320 | tf_op jit(solution)/shard_map/ppermute | solution.py:39
  81.0 3.1 %collective-permute-done.16.refs_3_ = bf16[64,4096]{1,0:T(8,128)(2,1)S(1)} collective-permute-done((bf16[64,4096]{1,0:T(8,128)(2,1)S(1)}, bf16[64,4096]{1,0:T(8,128)(2,1)S(1)}, u32[]{:S(2)}, u32[]{:S(2)}) %collective-permute-start.16) | collective-permute-done | bytes 524320 | tf_op jit(solution)/shard_map/ppermute | solution.py:39
  84.1 1.2 collective-permute-start.17
  85.4 0.8 collective-permute-start.19
  86.2 1.7 %collective-permute-done.17.refs_2_ = f32[32,128]{1,0:T(8,128)S(1)} collective-permute-done((f32[32,128]{1,0:T(8,128)S(1)}, f32[32,128]{1,0:T(8,128)S(1)}, u32[]{:S(2)}, u32[]{:S(2)}) %collective-permute-start.17) | collective-permute-done | bytes 16416 | tf_op jit(solution)/shard_map/ppermute | solution.py:39
  87.9 3.0 %collective-permute-done.18.refs_3_ = f32[32,128]{1,0:T(8,128)S(1)} collective-permute-done((f32[32,128]{1,0:T(8,128)S(1)}, f32[32,128]{1,0:T(8,128)S(1)}, u32[]{:S(2)}, u32[]{:S(2)}) %collective-permute-start.18) | collective-permute-done | bytes 16416 | tf_op jit(solution)/shard_map/ppermute | solution.py:39
  90.9 0.9 collective-permute-done.19.refs_4_
  91.8 0.6 combine_centres.1
  92.4 0.1 collective-permute-start.21
  92.5 2.4 %collective-permute-start.22 = (f32[32,128]{1,0:T(8,128)S(1)}, f32[32,128]{1,0:T(8,128)S(1)}, u32[]{:S(2)}, u32[]{:S(2)}) collective-permute-start(f32[32,128]{1,0:T(8,128)S(1)} %get-tuple-element.111), channel_id=1, source_target_pairs={{0,24},{2,26},{4,12},{6,14},{8,0},{10,2},{12,20},{14,22},{16,8},{1... | collective-permute-start | bytes 49160 | tf_op jit(solution)/shard_map/ppermute | solution.py:39
  94.9 1.4 %collective-permute-start.23 = (f32[32,128]{1,0:T(8,128)S(1)}, f32[32,128]{1,0:T(8,128)S(1)}, u32[]{:S(2)}, u32[]{:S(2)}) collective-permute-start(f32[32,128]{1,0:T(8,128)S(1)} %get-tuple-element.112), channel_id=1, source_target_pairs={{0,26},{2,0},{4,6},{6,12},{8,2},{10,8},{12,14},{14,20},{16,10},{18... | collective-permute-start | bytes 49160 | tf_op jit(solution)/shard_map/ppermute | solution.py:39
  96.3 0.6 collective-permute-start.20
  96.9 0.9 collective-permute-done.21.refs_17_.refs_9_
  97.8 2.7 %collective-permute-done.23.refs_19_ = f32[32,128]{1,0:T(8,128)S(1)} collective-permute-done((f32[32,128]{1,0:T(8,128)S(1)}, f32[32,128]{1,0:T(8,128)S(1)}, u32[]{:S(2)}, u32[]{:S(2)}) %collective-permute-start.23) | collective-permute-done | bytes 16416 | tf_op jit(solution)/shard_map/ppermute | solution.py:39
  100.5 3.2 %gradient.1 = (bf16[64,4096]{1,0:T(8,128)(2,1)S(1)}, bf16[64,4096]{1,0:T(8,128)(2,1)S(1)}, bf16[64,4096]{1,0:T(8,128)(2,1)S(1)}, bf16[64,4096]{1,0:T(8,128)(2,1)...) custom-call(s32[1]{0:T(128)} %bitcast.place_ref, s32[2,2]{1,0:T(2,128)S(1)} %copy-done.7, ...), custom_call_target="tpu_custom_call" | custom-call | tf_op jit(solution)/shard_map/gradient/pallas_call | solution.py:393
  103.6 3.8 %collective-permute-done.27.refs_10_ = bf16[128,4096]{1,0:T(8,128)(2,1)S(1)} collective-permute-done((bf16[128,4096]{1,0:T(8,128)(2,1)S(1)}, bf16[128,4096]{1,0:T(8,128)(2,1)S(1)}, u32[]{:S(2)}, u32[]{:S(2)}) %collective-permute-start.27) | collective-permute-done | bytes 1048608 | tf_op jit(solution)/shard_map/ppermute | solution.py:39
  107.5 1.2 collective-permute-start.24
  108.7 1.5 %collective-permute-done.20.refs_4_ = bf16[64,4096]{1,0:T(8,128)(2,1)S(1)} collective-permute-done((bf16[64,4096]{1,0:T(8,128)(2,1)S(1)}, bf16[64,4096]{1,0:T(8,128)(2,1)S(1)}, u32[]{:S(2)}, u32[]{:S(2)}) %collective-permute-start.20) | collective-permute-done | bytes 524320 | tf_op jit(solution)/shard_map/ppermute | solution.py:39
  110.2 0.1 collective-permute-start.26
  110.3 2.6 %attended.1 = bf16[128,4096]{1,0:T(8,128)(2,1)} custom-call(s32[1]{0:T(128)} %bitcast.place_ref, s32[2,2]{1,0:T(2,128)S(1)} %copy-done.7, bf16[64,4096]{1,0:T(8,128)(2,1)S(1)} %get-tuple-element.91.refs_0_, bf16[64,4096]{1,0:T(8,128)(2,1)S(1)} %get-tuple-element.92.refs_1_, bf16[64,4096]{1,0:T(8,128)(2,1)S(1)} %collective-permute-done.15.refs_2_, ...), custom_call_target="tpu_custom_call" | custom-call | tf_op jit(solution)/shard_map/attended/pallas_call | solution.py:393
  112.9 14.7 %collective-permute-done.28.refs_11_ = bf16[128,4096]{1,0:T(8,128)(2,1)S(1)} collective-permute-done((bf16[128,4096]{1,0:T(8,128)(2,1)S(1)}, bf16[128,4096]{1,0:T(8,128)(2,1)S(1)}, u32[]{:S(2)}, u32[]{:S(2)}) %collective-permute-start.28) | collective-permute-done | bytes 1048608 | tf_op jit(solution)/shard_map/ppermute | solution.py:39
  127.6 3.5 %own.1 = (bf16[128,4096]{1,0:T(8,128)(2,1)}, bf16[128,4096]{1,0:T(8,128)(2,1)}) custom-call(s32[1]{0:T(128)} %bitcast.place_ref, s32[2,2]{1,0:T(2,128)S(1)} %copy-done.7, bf16[128,4096]{1,0:T(8,128)(2,1)S(1)} %get-tuple-element.67.refs_0_, bf16[64,4096]{1,0:T(8,128)(2,1)S(1)} %collective-permute-done.2.refs_1_, bf16[128,4096]{1,0:T(8,128)(2,1)S(1)} %copy-done, ...), custom_call_target="tpu_custom_call" | custom-call | tf_op jit(solution)/shard_map/own/pallas_call | solution.py:393
  131.1 2.0 %inner.1 = (f32[128,4096]{1,0:T(8,128)S(1)}, f32[1,128]{1,0:T(1,128)S(1)}) custom-call(s32[1]{0:T(128)} %bitcast.place_ref, s32[2,2]{1,0:T(2,128)S(1)} %copy-done.7, bf16[64,4096]{1,0:T(8,128)(2,1)S(1)} %get-tuple-element.113.refs_0_, bf16[64,4096]{1,0:T(8,128)(2,1)S(1)} %get-tuple-element.114.refs_1_, bf16[64,4096]{1,0:T(8,128)(2,1)S(1)} %collective-permute-done.24.refs_2_, ...), custom_call_target="tpu_custom_call" | custom-call | tf_op jit(solution)/shard_map/inner/pallas_call | solution.py:393
  133.1 0.1 collective-permute-start.29
  133.2 1.1 collective-permute-done.29.refs_3_
  134.3 1.6 %finish.1 = bf16[128,4096]{1,0:T(8,128)(2,1)} custom-call(f32[128,4096]{1,0:T(8,128)S(1)} %get-tuple-element.127.scaled_ref, bf16[128,4096]{1,0:T(8,128)(2,1)S(1)} %copy-done.3, f32[1,128]{1,0:T(1,128)S(1)} %squares.1.refs_0_, f32[1,128]{1,0:T(1,128)S(1)} %collective-permute-done.1.refs_1_, f32[1,128]{1,0:T(1,128)S(1)} %get-tuple-element.128.refs_2_, ...), custom_call_target="tpu_custom_call" | custom-call | tf_op jit(solution)/shard_map/finish/pallas_call | solution.py:393
  (30 shorter events, 0.1 us)
Async XLA Ops:
  0.6 14.0 %copy-start = (bf16[128,4096]{1,0:T(8,128)(2,1)S(1)}, bf16[128,4096]{1,0:T(8,128)(2,1)}, u32[]{:S(2)}) copy-start(bf16[128,4096]{1,0:T(8,128)(2,1)} %refs_2_.1) | copy-start | bytes 3145732
  0.6 1.3 copy-start.1
  2.0 12.7 %copy-start.7 = (s32[2,2]{1,0:T(2,128)S(1)}, s32[2,2]{1,0:T(2,128)}, u32[]{:S(2)}) copy-start(s32[2,2]{1,0:T(2,128)} %near_ref.21) | copy-start | bytes 52
  2.3 3.1 %collective-permute-start.1 = (f32[1,128]{1,0:T(1,128)S(1)}, f32[1,128]{1,0:T(1,128)S(1)}, u32[]{:S(2)}, u32[]{:S(2)}) collective-permute-start(f32[1,128]{1,0:T(1,128)S(1)} %squares.1.refs_0_), channel_id=1, source_target_pairs={{0,1},{1,0},{2,3},{3,2},{4,5},{5,4},{6,7},{7,6},{8,9},{9,8},{10,11... | collective-permute-start | bytes 1544 | tf_op jit(solution)/shard_map/ppermute | solution.py:373
  2.8 35.0 %collective-permute-start.5 = (bf16[128,4096]{1,0:T(8,128)(2,1)}, bf16[128,4096]{1,0:T(8,128)(2,1)S(1)}, u32[]{:S(2)}, u32[]{:S(2)}) collective-permute-start(bf16[128,4096]{1,0:T(8,128)(2,1)} %refs_4_.5), channel_id=1, source_target_pairs={{0,4},{2,6},{4,0},{6,2},{8,12},{10,14},{12,8},{14,10},{16,20},{18,... | collective-permute-start | bytes 3145736 | tf_op jit(solution)/shard_map/ppermute | solution.py:39
  5.4 1.2 copy-start.2
  6.6 0.7 copy-start.6
  7.3 0.7 copy-start.8
  8.0 19.5 %copy-start.4 = (bf16[128,4096]{1,0:T(8,128)(2,1)S(1)}, bf16[128,4096]{1,0:T(8,128)(2,1)}, u32[]{:S(2)}) copy-start(bf16[128,4096]{1,0:T(8,128)(2,1)} %refs_4_.4) | copy-start | bytes 3145732
  8.0 29.8 %copy-start.5 = (bf16[128,4096]{1,0:T(8,128)(2,1)S(1)}, bf16[128,4096]{1,0:T(8,128)(2,1)}, u32[]{:S(2)}) copy-start(bf16[128,4096]{1,0:T(8,128)(2,1)} %refs_4_.5) | copy-start | bytes 3145732
  9.0 14.8 %collective-permute-start.2 = (bf16[64,4096]{1,0:T(8,128)(2,1)S(1)}, bf16[64,4096]{1,0:T(8,128)(2,1)S(1)}, u32[]{:S(2)}, u32[]{:S(2)}) collective-permute-start(bf16[64,4096]{1,0:T(8,128)(2,1)S(1)} %get-tuple-element.68), channel_id=1, source_target_pairs={{0,2},{2,0},{4,6},{6,4},{8,10},{10,8},{12,14},{14,12},{16,18},{18,... | collective-permute-start | bytes 1572872 | tf_op jit(solution)/shard_map/ppermute | solution.py:39
  10.6 16.9 %collective-permute-start.3 = (bf16[64,4096]{1,0:T(8,128)(2,1)S(1)}, bf16[64,4096]{1,0:T(8,128)(2,1)S(1)}, u32[]{:S(2)}, u32[]{:S(2)}) collective-permute-start(bf16[64,4096]{1,0:T(8,128)(2,1)S(1)} %get-tuple-element.69), channel_id=1, source_target_pairs={{0,24},{2,26},{4,12},{6,14},{8,0},{10,2},{12,20},{14,22},{16,8},{1... | collective-permute-start | bytes 1572872 | tf_op jit(solution)/shard_map/ppermute | solution.py:39
  14.2 23.6 %collective-permute-start.4 = (bf16[64,4096]{1,0:T(8,128)(2,1)S(1)}, bf16[64,4096]{1,0:T(8,128)(2,1)S(1)}, u32[]{:S(2)}, u32[]{:S(2)}) collective-permute-start(bf16[64,4096]{1,0:T(8,128)(2,1)S(1)} %get-tuple-element.70), channel_id=1, source_target_pairs={{0,26},{2,0},{4,6},{6,12},{8,2},{10,8},{12,14},{14,20},{16,10},{18... | collective-permute-start | bytes 1572872 | tf_op jit(solution)/shard_map/ppermute | solution.py:39
  15.3 30.3 %collective-permute-start.6 = (bf16[64,4096]{1,0:T(8,128)(2,1)S(1)}, bf16[64,4096]{1,0:T(8,128)(2,1)S(1)}, u32[]{:S(2)}, u32[]{:S(2)}) collective-permute-start(bf16[64,4096]{1,0:T(8,128)(2,1)S(1)} %get-tuple-element.79), channel_id=1, source_target_pairs={{0,2},{2,0},{4,6},{6,4},{8,10},{10,8},{12,14},{14,12},{16,18},{18,... | collective-permute-start | bytes 1572872 | tf_op jit(solution)/shard_map/ppermute | solution.py:39
  23.9 24.0 %collective-permute-start.7 = (bf16[64,4096]{1,0:T(8,128)(2,1)S(1)}, bf16[64,4096]{1,0:T(8,128)(2,1)S(1)}, u32[]{:S(2)}, u32[]{:S(2)}) collective-permute-start(bf16[64,4096]{1,0:T(8,128)(2,1)S(1)} %get-tuple-element.80), channel_id=1, source_target_pairs={{0,24},{2,26},{4,12},{6,14},{8,0},{10,2},{12,20},{14,22},{16,8},{1... | collective-permute-start | bytes 1572872 | tf_op jit(solution)/shard_map/ppermute | solution.py:39
  27.5 40.8 %collective-permute-start = (bf16[128,4096]{1,0:T(8,128)(2,1)S(1)}, bf16[128,4096]{1,0:T(8,128)(2,1)S(1)}, u32[]{:S(2)}, u32[]{:S(2)}) collective-permute-start(bf16[128,4096]{1,0:T(8,128)(2,1)S(1)} %copy-done.4), channel_id=1, source_target_pairs={{0,4},{2,6},{4,0},{6,2},{8,12},{10,14},{12,8},{14,10},{16,20},{18,... | collective-permute-start | bytes 3145736 | tf_op jit(solution)/shard_map/ppermute | solution.py:39
  47.9 3.7 %collective-permute-start.8 = (f32[32,128]{1,0:T(8,128)S(1)}, f32[32,128]{1,0:T(8,128)S(1)}, u32[]{:S(2)}, u32[]{:S(2)}) collective-permute-start(f32[32,128]{1,0:T(8,128)S(1)} %get-tuple-element.81), channel_id=1, source_target_pairs={{2,0},{0,2},{6,4},{4,6},{10,8},{8,10},{14,12},{12,14},{18,16},{16,... | collective-permute-start | bytes 49160 | tf_op jit(solution)/shard_map/ppermute | solution.py:39
  47.9 6.0 %collective-permute-start.9 = (f32[32,128]{1,0:T(8,128)S(1)}, f32[32,128]{1,0:T(8,128)S(1)}, u32[]{:S(2)}, u32[]{:S(2)}) collective-permute-start(f32[32,128]{1,0:T(8,128)S(1)} %get-tuple-element.82), channel_id=1, source_target_pairs={{24,0},{26,2},{12,4},{14,6},{0,8},{2,10},{20,12},{22,14},{8,16},{1... | collective-permute-start | bytes 49160 | tf_op jit(solution)/shard_map/ppermute | solution.py:39
  48.6 6.9 %collective-permute-start.10 = (f32[32,128]{1,0:T(8,128)S(1)}, f32[32,128]{1,0:T(8,128)S(1)}, u32[]{:S(2)}, u32[]{:S(2)}) collective-permute-start(f32[32,128]{1,0:T(8,128)S(1)} %get-tuple-element.83), channel_id=1, source_target_pairs={{26,0},{0,2},{6,4},{12,6},{2,8},{8,10},{14,12},{20,14},{10,16},{16... | collective-permute-start | bytes 49160 | tf_op jit(solution)/shard_map/ppermute | solution.py:39
  56.2 12.1 %collective-permute-start.11 = (bf16[64,4096]{1,0:T(8,128)(2,1)S(1)}, bf16[64,4096]{1,0:T(8,128)(2,1)S(1)}, u32[]{:S(2)}, u32[]{:S(2)}) collective-permute-start(bf16[64,4096]{1,0:T(8,128)(2,1)S(1)} %pick.3), channel_id=1, source_target_pairs={{0,26},{2,0},{4,6},{6,12},{8,2},{10,8},{12,14},{14,20},{16,10},{18... | collective-permute-start | bytes 1572872 | tf_op jit(solution)/shard_map/ppermute | solution.py:39
  58.9 9.5 %collective-permute-start.12 = (f32[32,128]{1,0:T(8,128)S(1)}, f32[32,128]{1,0:T(8,128)S(1)}, u32[]{:S(2)}, u32[]{:S(2)}) collective-permute-start(f32[32,128]{1,0:T(8,128)S(1)} %get-tuple-element.88), channel_id=1, source_target_pairs={{0,2},{2,0},{4,6},{6,4},{8,10},{10,8},{12,14},{14,12},{16,18},{18,... | collective-permute-start | bytes 49160 | tf_op jit(solution)/shard_map/ppermute | solution.py:39
  59.1 9.3 %collective-permute-start.13 = (f32[32,128]{1,0:T(8,128)S(1)}, f32[32,128]{1,0:T(8,128)S(1)}, u32[]{:S(2)}, u32[]{:S(2)}) collective-permute-start(f32[32,128]{1,0:T(8,128)S(1)} %get-tuple-element.89), channel_id=1, source_target_pairs={{0,24},{2,26},{4,12},{6,14},{8,0},{10,2},{12,20},{14,22},{16,8},{1... | collective-permute-start | bytes 49160 | tf_op jit(solution)/shard_map/ppermute | solution.py:39
  61.1 7.5 %collective-permute-start.14 = (f32[32,128]{1,0:T(8,128)S(1)}, f32[32,128]{1,0:T(8,128)S(1)}, u32[]{:S(2)}, u32[]{:S(2)}) collective-permute-start(f32[32,128]{1,0:T(8,128)S(1)} %get-tuple-element.90), channel_id=1, source_target_pairs={{0,26},{2,0},{4,6},{6,12},{8,2},{10,8},{12,14},{14,20},{16,10},{18... | collective-permute-start | bytes 49160 | tf_op jit(solution)/shard_map/ppermute | solution.py:39
  70.2 10.8 %collective-permute-start.15 = (bf16[64,4096]{1,0:T(8,128)(2,1)S(1)}, bf16[64,4096]{1,0:T(8,128)(2,1)S(1)}, u32[]{:S(2)}, u32[]{:S(2)}) collective-permute-start(bf16[64,4096]{1,0:T(8,128)(2,1)S(1)} %get-tuple-element.93), channel_id=1, source_target_pairs={{2,0},{0,2},{6,4},{4,6},{10,8},{8,10},{14,12},{12,14},{18,16},{16,... | collective-permute-start | bytes 1572872 | tf_op jit(solution)/shard_map/ppermute | solution.py:39
  71.6 12.5 %collective-permute-start.16 = (bf16[64,4096]{1,0:T(8,128)(2,1)S(1)}, bf16[64,4096]{1,0:T(8,128)(2,1)S(1)}, u32[]{:S(2)}, u32[]{:S(2)}) collective-permute-start(bf16[64,4096]{1,0:T(8,128)(2,1)S(1)} %get-tuple-element.94), channel_id=1, source_target_pairs={{24,0},{26,2},{12,4},{14,6},{0,8},{2,10},{20,12},{22,14},{8,16},{1... | collective-permute-start | bytes 1572872 | tf_op jit(solution)/shard_map/ppermute | solution.py:39
  84.1 23.3 %collective-permute-start.27 = (bf16[128,4096]{1,0:T(8,128)(2,1)S(1)}, bf16[128,4096]{1,0:T(8,128)(2,1)S(1)}, u32[]{:S(2)}, u32[]{:S(2)}) collective-permute-start(bf16[128,4096]{1,0:T(8,128)(2,1)S(1)} %get-tuple-element.120), channel_id=1, source_target_pairs={{0,4},{2,6},{4,0},{6,2},{8,12},{10,14},{12,8},{14,10},{16,20},{18,... | collective-permute-start | bytes 3145736 | tf_op jit(solution)/shard_map/ppermute | solution.py:39
  84.1 3.7 %collective-permute-start.17 = (f32[32,128]{1,0:T(8,128)S(1)}, f32[32,128]{1,0:T(8,128)S(1)}, u32[]{:S(2)}, u32[]{:S(2)}) collective-permute-start(f32[32,128]{1,0:T(8,128)S(1)} %get-tuple-element.102), channel_id=1, source_target_pairs={{2,0},{0,2},{6,4},{4,6},{10,8},{8,10},{14,12},{12,14},{18,16},{16,... | collective-permute-start | bytes 49160 | tf_op jit(solution)/shard_map/ppermute | solution.py:39
  85.4 5.5 %collective-permute-start.18 = (f32[32,128]{1,0:T(8,128)S(1)}, f32[32,128]{1,0:T(8,128)S(1)}, u32[]{:S(2)}, u32[]{:S(2)}) collective-permute-start(f32[32,128]{1,0:T(8,128)S(1)} %get-tuple-element.103), channel_id=1, source_target_pairs={{24,0},{26,2},{12,4},{14,6},{0,8},{2,10},{20,12},{22,14},{8,16},{1... | collective-permute-start | bytes 49160 | tf_op jit(solution)/shard_map/ppermute | solution.py:39
  85.4 6.4 %collective-permute-start.19 = (f32[32,128]{1,0:T(8,128)S(1)}, f32[32,128]{1,0:T(8,128)S(1)}, u32[]{:S(2)}, u32[]{:S(2)}) collective-permute-start(f32[32,128]{1,0:T(8,128)S(1)} %get-tuple-element.104), channel_id=1, source_target_pairs={{26,0},{0,2},{6,4},{12,6},{2,8},{8,10},{14,12},{20,14},{10,16},{16... | collective-permute-start | bytes 49160 | tf_op jit(solution)/shard_map/ppermute | solution.py:39
  92.4 5.4 %collective-permute-start.21 = (f32[32,128]{1,0:T(8,128)S(1)}, f32[32,128]{1,0:T(8,128)S(1)}, u32[]{:S(2)}, u32[]{:S(2)}) collective-permute-start(f32[32,128]{1,0:T(8,128)S(1)} %get-tuple-element.110), channel_id=1, source_target_pairs={{0,2},{2,0},{4,6},{6,4},{8,10},{10,8},{12,14},{14,12},{16,18},{18,... | collective-permute-start | bytes 49160 | tf_op jit(solution)/shard_map/ppermute | solution.py:39
  92.5 5.3 %collective-permute-start.22 = (f32[32,128]{1,0:T(8,128)S(1)}, f32[32,128]{1,0:T(8,128)S(1)}, u32[]{:S(2)}, u32[]{:S(2)}) collective-permute-start(f32[32,128]{1,0:T(8,128)S(1)} %get-tuple-element.111), channel_id=1, source_target_pairs={{0,24},{2,26},{4,12},{6,14},{8,0},{10,2},{12,20},{14,22},{16,8},{1... | collective-permute-start | bytes 49160 | tf_op jit(solution)/shard_map/ppermute | solution.py:39
  94.9 5.6 %collective-permute-start.23 = (f32[32,128]{1,0:T(8,128)S(1)}, f32[32,128]{1,0:T(8,128)S(1)}, u32[]{:S(2)}, u32[]{:S(2)}) collective-permute-start(f32[32,128]{1,0:T(8,128)S(1)} %get-tuple-element.112), channel_id=1, source_target_pairs={{0,26},{2,0},{4,6},{6,12},{8,2},{10,8},{12,14},{14,20},{16,10},{18... | collective-permute-start | bytes 49160 | tf_op jit(solution)/shard_map/ppermute | solution.py:39
  96.3 14.0 %collective-permute-start.20 = (bf16[64,4096]{1,0:T(8,128)(2,1)S(1)}, bf16[64,4096]{1,0:T(8,128)(2,1)S(1)}, u32[]{:S(2)}, u32[]{:S(2)}) collective-permute-start(bf16[64,4096]{1,0:T(8,128)(2,1)S(1)} %get-tuple-element.106), channel_id=1, source_target_pairs={{26,0},{0,2},{6,4},{12,6},{2,8},{8,10},{14,12},{20,14},{10,16},{16... | collective-permute-start | bytes 1572872 | tf_op jit(solution)/shard_map/ppermute | solution.py:39
  107.5 20.1 %collective-permute-start.28 = (bf16[128,4096]{1,0:T(8,128)(2,1)S(1)}, bf16[128,4096]{1,0:T(8,128)(2,1)S(1)}, u32[]{:S(2)}, u32[]{:S(2)}) collective-permute-start(bf16[128,4096]{1,0:T(8,128)(2,1)S(1)} %get-tuple-element.122), channel_id=1, source_target_pairs={{0,4},{2,6},{4,0},{6,2},{8,12},{10,14},{12,8},{14,10},{16,20},{18,... | collective-permute-start | bytes 3145736 | tf_op jit(solution)/shard_map/ppermute | solution.py:39
  107.5 23.6 %collective-permute-start.24 = (bf16[64,4096]{1,0:T(8,128)(2,1)S(1)}, bf16[64,4096]{1,0:T(8,128)(2,1)S(1)}, u32[]{:S(2)}, u32[]{:S(2)}) collective-permute-start(bf16[64,4096]{1,0:T(8,128)(2,1)S(1)} %get-tuple-element.115), channel_id=1, source_target_pairs={{2,0},{0,2},{6,4},{4,6},{10,8},{8,10},{14,12},{12,14},{18,16},{16,... | collective-permute-start | bytes 1572872 | tf_op jit(solution)/shard_map/ppermute | solution.py:39
  108.7 22.4 %collective-permute-start.25 = (bf16[64,4096]{1,0:T(8,128)(2,1)S(1)}, bf16[64,4096]{1,0:T(8,128)(2,1)S(1)}, u32[]{:S(2)}, u32[]{:S(2)}) collective-permute-start(bf16[64,4096]{1,0:T(8,128)(2,1)S(1)} %get-tuple-element.116), channel_id=1, source_target_pairs={{24,0},{26,2},{12,4},{14,6},{0,8},{2,10},{20,12},{22,14},{8,16},{1... | collective-permute-start | bytes 1572872 | tf_op jit(solution)/shard_map/ppermute | solution.py:39
  110.2 20.9 %collective-permute-start.26 = (bf16[64,4096]{1,0:T(8,128)(2,1)S(1)}, bf16[64,4096]{1,0:T(8,128)(2,1)S(1)}, u32[]{:S(2)}, u32[]{:S(2)}) collective-permute-start(bf16[64,4096]{1,0:T(8,128)(2,1)S(1)} %get-tuple-element.118), channel_id=1, source_target_pairs={{26,0},{0,2},{6,4},{12,6},{2,8},{8,10},{14,12},{20,14},{10,16},{16... | collective-permute-start | bytes 1572872 | tf_op jit(solution)/shard_map/ppermute | solution.py:39
  112.9 18.2 %copy-start.3 = (bf16[128,4096]{1,0:T(8,128)(2,1)S(1)}, bf16[128,4096]{1,0:T(8,128)(2,1)}, u32[]{:S(2)}) copy-start(bf16[128,4096]{1,0:T(8,128)(2,1)} %q_ref.5) | copy-start | bytes 3145732
  112.9 18.2 %copy-start.9 = (f32[4096]{0:T(1024)S(1)}, f32[4096]{0:T(1024)}, u32[]{:S(2)}) copy-start(f32[4096]{0:T(1024)} %param.7) | copy-start | bytes 49156
  133.1 1.2 collective-permute-start.29

commit v4 on v3

--- a/solution.py
+++ b/solution.py
@@ -301,7 +301,7 @@
     q_refs = dict(zip(OWN, (normed_ref.at[rows_of(numbers[0])], q_ref)))
     g_refs = dict(zip(OWN, (grad_ref.at[rows_of(numbers[0])], g_ref)))
     back_refs, centre_refs = dict(zip(OWN, refs[6:8])), dict(zip(OWN, refs[8:10]))
-    far_dv_ref, far_dk_ref, dv_ref, dk_ref = refs[10:]
+    far_dv_ref, dv_ref, dk_ref = refs[10:]
 
     def body(rows, cols):
         probs, lows = grad_scores_of(
@@ -311,11 +311,15 @@
             total = dot(p.astype(jnp.bfloat16), head(g_refs, OWN, c), 1, 0)
             total = total + far_dv_ref[:, c].astype(jnp.float32)
             dv_ref[:, c] = total.astype(jnp.bfloat16)
-            total = dot(low, head(q_refs, OWN, c), 1, 0) * SCALING
-            total = total + far_dk_ref[:, c].astype(jnp.float32)
-            dk_ref[:, c] = total.astype(jnp.bfloat16)
+            dk_ref[:, c] = dot(low, head(q_refs, OWN, c), 1, 0) * SCALING
 
     each_chunk(refs[6].shape[0], CHUNK, body)
+
+
+def add_kernel(own_ref, far_ref, out_ref):
+    for t in range(out_ref.shape[1] // LANES):
+        total = own_ref[:, tile(t)] + far_ref[:, tile(t)].astype(jnp.float32)
+        out_ref[:, tile(t)] = total.astype(jnp.bfloat16)
 
 
 def gathered(weights, refs, t):
@@ -484,15 +488,19 @@
         *back, *centres,
     )
     far_dk = across(after(far_dk, far_dv))
-    grads[4] = after(grads[4], contexts[4])
+    grads[2:] = after(grads[2:], contexts[4])
     grads = come(grads)
 
-    d_values, d_keys = placed(own_kernel, "own", [tall, tall], last=(0, 1))(
-        normed, q_slots[0], d_out, g2, own_weights, own_products, back[0], back[2], centres[0], centres[2],
-        far_dv, far_dk,
+    d_values, own_dk = placed(
+        own_kernel, "own", [tall, ((rows, width), jnp.float32)], last=(0,)
+    )(
+        normed, q_slots[0], d_out, g2, own_weights, own_products, back[0], back[2], centres[0],
+        centres[2], far_dv,
     )
+    far_dk = after(far_dk, d_values)
+    (d_keys,) = kernel_call(add_kernel, "add", [tall], last=(0,))(own_dk, far_dk)
     (attended,) = placed(attended_kernel, "attended", [tall], last=(0,))(*contexts)
-    grads[2:] = after(grads[2:], attended, d_values)
+    grads[2:] = after(grads[2:], attended, d_values, d_keys)
     scaled, inner = placed(inner_kernel, "inner", [((rows, width), jnp.float32), row])(
         *grads, queries, gain
     )

time: 136 us -> 136 us (level)
  waiting for transfers between devices: 73.8 us -> 69.9 us
  starting transfers between devices: 31.8 us -> 34.5 us
    ppermute x28, waiting for transfers between devices: 72.7 us -> 68.8 us  [sent(): return lax.ppermute(array, 'dp', route)]
    ppermute x28, starting transfers between devices: 31.2 us -> 34 us  [sent(): return lax.ppermute(array, 'dp', route)]
    pallas_call x14 -> x15, Pallas kernels: 25.6 us -> 26.3 us  [call(): pl.pallas_call(body, in_specs=[pl.BlockSpec(memory_space=pltpu.SMEM)] * s...]
  transfers between devices with their start and end apart: 30 -> 30, of which waited for: 21 -> 22; matrix products, arithmetic and copies ran while one was open for 0% -> 0% of each run, Pallas kernels for 15% -> 15%
where the time goes in v4:
time: 136 us
  waiting for transfers between devices  69.9 us (51%)
  starting transfers between devices  34.5 us (25%)
  Pallas kernels  26.3 us (19%)
  local copies, waits for them, and re-layouts  3.95 us (3%)
    ppermute x28, waiting for transfers between devices, sent(): return lax.ppermute(array, 'dp', route)  68.8 us
    ppermute x28, starting transfers between devices, sent(): return lax.ppermute(array, 'dp', route)  34 us
    pallas_call x15, Pallas kernels, call(): pl.pallas_call(body, in_specs=[pl.BlockSpec(memory_space=pltpu.SMEM)] * s...  26.3 us
    unnamed x20, local copies, waits for them, and re-layouts  3.95 us
  transfers between devices with their start and end apart: 30, of which 22 were waited for; matrix products, arithmetic and copies ran while one was open for 0% of the time, Pallas kernels for 15%

profile of v4, /device:TPU:0, one launch (start us, length us, event | category | flops | bytes accessed | tf_op | source)
XLA Modules:
  0.0 135.5 jit_solution(6627535893834831455)
XLA Ops:
  0.7 1.3 copy-done.1
  2.0 0.3 squares.1.refs_0_
  2.3 0.5 collective-permute-start.1
  2.8 2.6 %collective-permute-start.5 = (bf16[128,4096]{1,0:T(8,128)(2,1)}, bf16[128,4096]{1,0:T(8,128)(2,1)S(1)}, u32[]{:S(2)}, u32[]{:S(2)}) collective-permute-start(bf16[128,4096]{1,0:T(8,128)(2,1)} %refs_4_.5), channel_id=1, source_target_pairs={{0,4},{2,6},{4,0},{6,2},{8,12},{10,14},{12,8},{14,10},{16,20},{18,... | collective-permute-start | bytes 3145736 | tf_op jit(solution)/shard_map/ppermute | solution.py:39
  5.4 1.2 copy-done.2
  6.6 0.7 copy-done.6
  7.3 0.7 copy-done.8
  8.0 1.0 prepare_queries.1
  9.0 1.6 %collective-permute-start.2 = (bf16[64,4096]{1,0:T(8,128)(2,1)S(1)}, bf16[64,4096]{1,0:T(8,128)(2,1)S(1)}, u32[]{:S(2)}, u32[]{:S(2)}) collective-permute-start(bf16[64,4096]{1,0:T(8,128)(2,1)S(1)} %get-tuple-element.71), channel_id=1, source_target_pairs={{0,2},{2,0},{4,6},{6,4},{8,10},{10,8},{12,14},{14,12},{16,18},{18,... | collective-permute-start | bytes 1572872 | tf_op jit(solution)/shard_map/ppermute | solution.py:39
  10.6 3.6 %collective-permute-start.3 = (bf16[64,4096]{1,0:T(8,128)(2,1)S(1)}, bf16[64,4096]{1,0:T(8,128)(2,1)S(1)}, u32[]{:S(2)}, u32[]{:S(2)}) collective-permute-start(bf16[64,4096]{1,0:T(8,128)(2,1)S(1)} %get-tuple-element.72), channel_id=1, source_target_pairs={{0,24},{2,26},{4,12},{6,14},{8,0},{10,2},{12,20},{14,22},{16,8},{1... | collective-permute-start | bytes 1572872 | tf_op jit(solution)/shard_map/ppermute | solution.py:39
  14.2 0.4 collective-permute-start.4
  14.6 0.6 pick.2
  15.3 1.7 %collective-permute-start.6 = (bf16[64,4096]{1,0:T(8,128)(2,1)S(1)}, bf16[64,4096]{1,0:T(8,128)(2,1)S(1)}, u32[]{:S(2)}, u32[]{:S(2)}) collective-permute-start(bf16[64,4096]{1,0:T(8,128)(2,1)S(1)} %get-tuple-element.82), channel_id=1, source_target_pairs={{0,2},{2,0},{4,6},{6,4},{8,10},{10,8},{12,14},{14,12},{16,18},{18,... | collective-permute-start | bytes 1572872 | tf_op jit(solution)/shard_map/ppermute | solution.py:39
  16.9 6.9 %collective-permute-done.2.refs_1_ = bf16[64,4096]{1,0:T(8,128)(2,1)S(1)} collective-permute-done((bf16[64,4096]{1,0:T(8,128)(2,1)S(1)}, bf16[64,4096]{1,0:T(8,128)(2,1)S(1)}, u32[]{:S(2)}, u32[]{:S(2)}) %collective-permute-start.2) | collective-permute-done | bytes 524320 | tf_op jit(solution)/shard_map/ppermute | solution.py:39
  23.9 3.6 %collective-permute-start.7 = (bf16[64,4096]{1,0:T(8,128)(2,1)S(1)}, bf16[64,4096]{1,0:T(8,128)(2,1)S(1)}, u32[]{:S(2)}, u32[]{:S(2)}) collective-permute-start(bf16[64,4096]{1,0:T(8,128)(2,1)S(1)} %get-tuple-element.83), channel_id=1, source_target_pairs={{0,24},{2,26},{4,12},{6,14},{8,0},{10,2},{12,20},{14,22},{16,8},{1... | collective-permute-start | bytes 1572872 | tf_op jit(solution)/shard_map/ppermute | solution.py:39
  27.5 10.3 %collective-permute-done.4.refs_3_ = bf16[64,4096]{1,0:T(8,128)(2,1)S(1)} collective-permute-done((bf16[64,4096]{1,0:T(8,128)(2,1)S(1)}, bf16[64,4096]{1,0:T(8,128)(2,1)S(1)}, u32[]{:S(2)}, u32[]{:S(2)}) %collective-permute-start.4) | collective-permute-done | bytes 524320 | tf_op jit(solution)/shard_map/ppermute | solution.py:39
  37.8 3.6 %scores.1 = (f32[32,128]{1,0:T(8,128)S(1)}, f32[32,128]{1,0:T(8,128)S(1)}, f32[32,128]{1,0:T(8,128)S(1)}, f32[32,128]{1,0:T(8,128)S(1)}, f32[32,128]{1,0:T(8,128...) custom-call(s32[1]{0:T(128)} %bitcast.place_ref, s32[2,2]{1,0:T(2,128)S(1)} %copy-done.7, ...), custom_call_target="tpu_custom_call" | custom-call | tf_op jit(solution)/shard_map/scores/pallas_call | solution.py:397
  41.4 4.2 %collective-permute-done.6.refs_1_.refs_3_ = bf16[64,4096]{1,0:T(8,128)(2,1)S(1)} collective-permute-done((bf16[64,4096]{1,0:T(8,128)(2,1)S(1)}, bf16[64,4096]{1,0:T(8,128)(2,1)S(1)}, u32[]{:S(2)}, u32[]{:S(2)}) %collective-permute-start.6) | collective-permute-done | bytes 524320 | tf_op jit(solution)/shard_map/ppermute | solution.py:39
  45.6 2.3 %collective-permute-done.7.refs_2_ = bf16[64,4096]{1,0:T(8,128)(2,1)S(1)} collective-permute-done((bf16[64,4096]{1,0:T(8,128)(2,1)S(1)}, bf16[64,4096]{1,0:T(8,128)(2,1)S(1)}, u32[]{:S(2)}, u32[]{:S(2)}) %collective-permute-start.7) | collective-permute-done | bytes 524320 | tf_op jit(solution)/shard_map/ppermute | solution.py:39
  47.9 0.7 collective-permute-start.9
  48.6 1.8 %collective-permute-start.10 = (f32[32,128]{1,0:T(8,128)S(1)}, f32[32,128]{1,0:T(8,128)S(1)}, u32[]{:S(2)}, u32[]{:S(2)}) collective-permute-start(f32[32,128]{1,0:T(8,128)S(1)} %get-tuple-element.86), channel_id=1, source_target_pairs={{26,0},{0,2},{6,4},{12,6},{2,8},{8,10},{14,12},{20,14},{10,16},{16... | collective-permute-start | bytes 49160 | tf_op jit(solution)/shard_map/ppermute | solution.py:39
  50.4 1.2 collective-permute-done.8.refs_2_
  51.6 2.3 %collective-permute-done.9.refs_3_ = f32[32,128]{1,0:T(8,128)S(1)} collective-permute-done((f32[32,128]{1,0:T(8,128)S(1)}, f32[32,128]{1,0:T(8,128)S(1)}, u32[]{:S(2)}, u32[]{:S(2)}) %collective-permute-start.9) | collective-permute-done | bytes 16416 | tf_op jit(solution)/shard_map/ppermute | solution.py:39
  54.0 1.6 %collective-permute-done.10.refs_4_ = f32[32,128]{1,0:T(8,128)S(1)} collective-permute-done((f32[32,128]{1,0:T(8,128)S(1)}, f32[32,128]{1,0:T(8,128)S(1)}, u32[]{:S(2)}, u32[]{:S(2)}) %collective-permute-start.10) | collective-permute-done | bytes 16416 | tf_op jit(solution)/shard_map/ppermute | solution.py:39
  55.6 0.6 pick.3
  56.2 1.9 %collective-permute-start.11 = (bf16[64,4096]{1,0:T(8,128)(2,1)S(1)}, bf16[64,4096]{1,0:T(8,128)(2,1)S(1)}, u32[]{:S(2)}, u32[]{:S(2)}) collective-permute-start(bf16[64,4096]{1,0:T(8,128)(2,1)S(1)} %pick.3), channel_id=1, source_target_pairs={{0,26},{2,0},{4,6},{6,12},{8,2},{10,8},{12,14},{14,20},{16,10},{18... | collective-permute-start | bytes 1572872 | tf_op jit(solution)/shard_map/ppermute | solution.py:39
  58.1 0.8 combine_scores.1
  58.9 0.2 collective-permute-start.12
  59.1 2.0 %collective-permute-start.13 = (f32[32,128]{1,0:T(8,128)S(1)}, f32[32,128]{1,0:T(8,128)S(1)}, u32[]{:S(2)}, u32[]{:S(2)}) collective-permute-start(f32[32,128]{1,0:T(8,128)S(1)} %get-tuple-element.92), channel_id=1, source_target_pairs={{0,24},{2,26},{4,12},{6,14},{8,0},{10,2},{12,20},{14,22},{16,8},{1... | collective-permute-start | bytes 49160 | tf_op jit(solution)/shard_map/ppermute | solution.py:39
  61.1 1.3 collective-permute-start.14
  62.4 5.8 %collective-permute-done.11.refs_3_ = bf16[64,4096]{1,0:T(8,128)(2,1)S(1)} collective-permute-done((bf16[64,4096]{1,0:T(8,128)(2,1)S(1)}, bf16[64,4096]{1,0:T(8,128)(2,1)S(1)}, u32[]{:S(2)}, u32[]{:S(2)}) %collective-permute-start.11) | collective-permute-done | bytes 524320 | tf_op jit(solution)/shard_map/ppermute | solution.py:39
  68.3 0.2 collective-permute-done.12.refs_6_.refs_10_.refs_12_.refs_7_
  68.4 0.2 collective-permute-done.14.refs_8_.refs_12_.refs_14_
  68.6 1.6 %context.1 = (bf16[64,4096]{1,0:T(8,128)(2,1)S(1)}, bf16[64,4096]{1,0:T(8,128)(2,1)S(1)}, bf16[64,4096]{1,0:T(8,128)(2,1)S(1)}, bf16[64,4096]{1,0:T(8,128)(2,1)S(1)}, bf16[64,4096]{1,0:T(8,128)(2,1)S(1)}) custom-call(bf16[128,4096]{1,0:T(8,128)(2,1)S(1)} %copy-done.4, bf16[128,4096]{1,0:T(8,128)(2,1)S(1)} %collective-permute-done.refs_1_.refs_5_, ...), custom_call_target="tpu_custom_call" | custom-call | tf_op jit(solution)/shard_map/context/pallas_call | solution.py:397
  70.2 1.4 %collective-permute-start.15 = (bf16[64,4096]{1,0:T(8,128)(2,1)S(1)}, bf16[64,4096]{1,0:T(8,128)(2,1)S(1)}, u32[]{:S(2)}, u32[]{:S(2)}) collective-permute-start(bf16[64,4096]{1,0:T(8,128)(2,1)S(1)} %get-tuple-element.96), channel_id=1, source_target_pairs={{2,0},{0,2},{6,4},{4,6},{10,8},{8,10},{14,12},{12,14},{18,16},{16,... | collective-permute-start | bytes 1572872 | tf_op jit(solution)/shard_map/ppermute | solution.py:39
  71.6 0.6 collective-permute-start.16
  72.2 3.6 %centres.1 = (f32[32,128]{1,0:T(8,128)S(1)}, f32[32,128]{1,0:T(8,128)S(1)}, f32[32,128]{1,0:T(8,128)S(1)}, f32[32,128]{1,0:T(8,128)S(1)}, f32[32,128]{1,0:T(8,12...) custom-call(s32[1]{0:T(128)} %bitcast.place_ref, s32[2,2]{1,0:T(2,128)S(1)} %copy-done.7, ...), custom_call_target="tpu_custom_call" | custom-call | tf_op jit(solution)/shard_map/centres/pallas_call | solution.py:397
  75.8 5.2 %collective-permute-done.15.refs_2_ = bf16[64,4096]{1,0:T(8,128)(2,1)S(1)} collective-permute-done((bf16[64,4096]{1,0:T(8,128)(2,1)S(1)}, bf16[64,4096]{1,0:T(8,128)(2,1)S(1)}, u32[]{:S(2)}, u32[]{:S(2)}) %collective-permute-start.15) | collective-permute-done | bytes 524320 | tf_op jit(solution)/shard_map/ppermute | solution.py:39
  81.0 3.1 %collective-permute-done.16.refs_3_ = bf16[64,4096]{1,0:T(8,128)(2,1)S(1)} collective-permute-done((bf16[64,4096]{1,0:T(8,128)(2,1)S(1)}, bf16[64,4096]{1,0:T(8,128)(2,1)S(1)}, u32[]{:S(2)}, u32[]{:S(2)}) %collective-permute-start.16) | collective-permute-done | bytes 524320 | tf_op jit(solution)/shard_map/ppermute | solution.py:39
  84.2 1.2 collective-permute-start.17
  85.4 0.8 collective-permute-start.19
  86.2 1.7 %collective-permute-done.17.refs_2_ = f32[32,128]{1,0:T(8,128)S(1)} collective-permute-done((f32[32,128]{1,0:T(8,128)S(1)}, f32[32,128]{1,0:T(8,128)S(1)}, u32[]{:S(2)}, u32[]{:S(2)}) %collective-permute-start.17) | collective-permute-done | bytes 16416 | tf_op jit(solution)/shard_map/ppermute | solution.py:39
  87.9 3.0 %collective-permute-done.18.refs_3_ = f32[32,128]{1,0:T(8,128)S(1)} collective-permute-done((f32[32,128]{1,0:T(8,128)S(1)}, f32[32,128]{1,0:T(8,128)S(1)}, u32[]{:S(2)}, u32[]{:S(2)}) %collective-permute-start.18) | collective-permute-done | bytes 16416 | tf_op jit(solution)/shard_map/ppermute | solution.py:39
  90.9 0.9 collective-permute-done.19.refs_4_
  91.8 0.6 combine_centres.1
  92.5 2.4 %collective-permute-start.22 = (f32[32,128]{1,0:T(8,128)S(1)}, f32[32,128]{1,0:T(8,128)S(1)}, u32[]{:S(2)}, u32[]{:S(2)}) collective-permute-start(f32[32,128]{1,0:T(8,128)S(1)} %get-tuple-element.114), channel_id=1, source_target_pairs={{0,24},{2,26},{4,12},{6,14},{8,0},{10,2},{12,20},{14,22},{16,8},{1... | collective-permute-start | bytes 49160 | tf_op jit(solution)/shard_map/ppermute | solution.py:39
  94.9 1.4 %collective-permute-start.23 = (f32[32,128]{1,0:T(8,128)S(1)}, f32[32,128]{1,0:T(8,128)S(1)}, u32[]{:S(2)}, u32[]{:S(2)}) collective-permute-start(f32[32,128]{1,0:T(8,128)S(1)} %get-tuple-element.115), channel_id=1, source_target_pairs={{0,26},{2,0},{4,6},{6,12},{8,2},{10,8},{12,14},{14,20},{16,10},{18... | collective-permute-start | bytes 49160 | tf_op jit(solution)/shard_map/ppermute | solution.py:39
  96.3 0.6 collective-permute-start.20
  96.9 0.9 collective-permute-done.21.refs_17_.refs_9_
  97.8 2.7 %collective-permute-done.23.refs_19_ = f32[32,128]{1,0:T(8,128)S(1)} collective-permute-done((f32[32,128]{1,0:T(8,128)S(1)}, f32[32,128]{1,0:T(8,128)S(1)}, u32[]{:S(2)}, u32[]{:S(2)}) %collective-permute-start.23) | collective-permute-done | bytes 16416 | tf_op jit(solution)/shard_map/ppermute | solution.py:39
  100.5 3.2 %gradient.1 = (bf16[64,4096]{1,0:T(8,128)(2,1)S(1)}, bf16[64,4096]{1,0:T(8,128)(2,1)S(1)}, bf16[64,4096]{1,0:T(8,128)(2,1)S(1)}, bf16[64,4096]{1,0:T(8,128)(2,1)...) custom-call(s32[1]{0:T(128)} %bitcast.place_ref, s32[2,2]{1,0:T(2,128)S(1)} %copy-done.7, ...), custom_call_target="tpu_custom_call" | custom-call | tf_op jit(solution)/shard_map/gradient/pallas_call | solution.py:397
  103.6 3.9 %collective-permute-done.27.refs_10_ = bf16[128,4096]{1,0:T(8,128)(2,1)S(1)} collective-permute-done((bf16[128,4096]{1,0:T(8,128)(2,1)S(1)}, bf16[128,4096]{1,0:T(8,128)(2,1)S(1)}, u32[]{:S(2)}, u32[]{:S(2)}) %collective-permute-start.27) | collective-permute-done | bytes 1048608 | tf_op jit(solution)/shard_map/ppermute | solution.py:39
  107.5 2.7 %collective-permute-done.20.refs_4_ = bf16[64,4096]{1,0:T(8,128)(2,1)S(1)} collective-permute-done((bf16[64,4096]{1,0:T(8,128)(2,1)S(1)}, bf16[64,4096]{1,0:T(8,128)(2,1)S(1)}, u32[]{:S(2)}, u32[]{:S(2)}) %collective-permute-start.20) | collective-permute-done | bytes 524320 | tf_op jit(solution)/shard_map/ppermute | solution.py:39
  110.2 0.1 collective-permute-start.24
  110.3 2.1 %collective-permute-start.25 = (bf16[64,4096]{1,0:T(8,128)(2,1)S(1)}, bf16[64,4096]{1,0:T(8,128)(2,1)S(1)}, u32[]{:S(2)}, u32[]{:S(2)}) collective-permute-start(bf16[64,4096]{1,0:T(8,128)(2,1)S(1)} %get-tuple-element.122), channel_id=1, source_target_pairs={{24,0},{26,2},{12,4},{14,6},{0,8},{2,10},{20,12},{22,14},{8,16},{1... | collective-permute-start | bytes 1572872 | tf_op jit(solution)/shard_map/ppermute | solution.py:39
  112.4 1.8 %collective-permute-start.26 = (bf16[64,4096]{1,0:T(8,128)(2,1)S(1)}, bf16[64,4096]{1,0:T(8,128)(2,1)S(1)}, u32[]{:S(2)}, u32[]{:S(2)}) collective-permute-start(bf16[64,4096]{1,0:T(8,128)(2,1)S(1)} %get-tuple-element.123), channel_id=1, source_target_pairs={{26,0},{0,2},{6,4},{12,6},{2,8},{8,10},{14,12},{20,14},{10,16},{16... | collective-permute-start | bytes 1572872 | tf_op jit(solution)/shard_map/ppermute | solution.py:39
  114.2 2.6 %attended.1 = bf16[128,4096]{1,0:T(8,128)(2,1)} custom-call(s32[1]{0:T(128)} %bitcast.place_ref, s32[2,2]{1,0:T(2,128)S(1)} %copy-done.7, bf16[64,4096]{1,0:T(8,128)(2,1)S(1)} %get-tuple-element.94.refs_0_, bf16[64,4096]{1,0:T(8,128)(2,1)S(1)} %get-tuple-element.95.refs_1_, bf16[64,4096]{1,0:T(8,128)(2,1)S(1)} %collective-permute-done.15.refs_2_, ...), custom_call_target="tpu_custom_call" | custom-call | tf_op jit(solution)/shard_map/attended/pallas_call | solution.py:397
  116.8 3.0 %own.1 = (bf16[128,4096]{1,0:T(8,128)(2,1)}, f32[128,4096]{1,0:T(8,128)S(1)}) custom-call(s32[1]{0:T(128)} %bitcast.place_ref, s32[2,2]{1,0:T(2,128)S(1)} %copy-done.7, bf16[128,4096]{1,0:T(8,128)(2,1)S(1)} %get-tuple-element.70.refs_0_, bf16[64,4096]{1,0:T(8,128)(2,1)S(1)} %collective-permute-done.2.refs_1_, bf16[128,4096]{1,0:T(8,128)(2,1)S(1)} %copy-done, ...), custom_call_target="tpu_custom_call" | custom-call | tf_op jit(solution)/shard_map/own/pallas_call | solution.py:397
  119.8 7.9 %collective-permute-done.28.far_ref = bf16[128,4096]{1,0:T(8,128)(2,1)S(1)} collective-permute-done((bf16[128,4096]{1,0:T(8,128)(2,1)S(1)}, bf16[128,4096]{1,0:T(8,128)(2,1)S(1)}, u32[]{:S(2)}, u32[]{:S(2)}) %collective-permute-start.28) | collective-permute-done | bytes 1048608 | tf_op jit(solution)/shard_map/ppermute | solution.py:39
  127.7 1.2 add.1
  128.9 1.8 %collective-permute-done.26.refs_4_ = bf16[64,4096]{1,0:T(8,128)(2,1)S(1)} collective-permute-done((bf16[64,4096]{1,0:T(8,128)(2,1)S(1)}, bf16[64,4096]{1,0:T(8,128)(2,1)S(1)}, u32[]{:S(2)}, u32[]{:S(2)}) %collective-permute-start.26) | collective-permute-done | bytes 524320 | tf_op jit(solution)/shard_map/ppermute | solution.py:39
  130.7 2.0 %inner.1 = (f32[128,4096]{1,0:T(8,128)S(1)}, f32[1,128]{1,0:T(1,128)S(1)}) custom-call(s32[1]{0:T(128)} %bitcast.place_ref, s32[2,2]{1,0:T(2,128)S(1)} %copy-done.7, bf16[64,4096]{1,0:T(8,128)(2,1)S(1)} %get-tuple-element.116.refs_0_, bf16[64,4096]{1,0:T(8,128)(2,1)S(1)} %get-tuple-element.117.refs_1_, bf16[64,4096]{1,0:T(8,128)(2,1)S(1)} %collective-permute-done.24.refs_2_, ...), custom_call_target="tpu_custom_call" | custom-call | tf_op jit(solution)/shard_map/inner/pallas_call | solution.py:397
  132.8 1.1 collective-permute-done.29.refs_3_
  133.9 1.7 %finish.1 = bf16[128,4096]{1,0:T(8,128)(2,1)} custom-call(f32[128,4096]{1,0:T(8,128)S(1)} %get-tuple-element.134.scaled_ref, bf16[128,4096]{1,0:T(8,128)(2,1)S(1)} %copy-done.3, f32[1,128]{1,0:T(1,128)S(1)} %squares.1.refs_0_, f32[1,128]{1,0:T(1,128)S(1)} %collective-permute-done.1.refs_1_, f32[1,128]{1,0:T(1,128)S(1)} %get-tuple-element.135.refs_2_, ...), custom_call_target="tpu_custom_call" | custom-call | tf_op jit(solution)/shard_map/finish/pallas_call | solution.py:397
  (31 shorter events, 0.2 us)
Async XLA Ops:
  0.6 14.0 %copy-start = (bf16[128,4096]{1,0:T(8,128)(2,1)S(1)}, bf16[128,4096]{1,0:T(8,128)(2,1)}, u32[]{:S(2)}) copy-start(bf16[128,4096]{1,0:T(8,128)(2,1)} %refs_2_.1) | copy-start | bytes 3145732
  0.6 1.3 copy-start.1
  2.0 12.7 %copy-start.7 = (s32[2,2]{1,0:T(2,128)S(1)}, s32[2,2]{1,0:T(2,128)}, u32[]{:S(2)}) copy-start(s32[2,2]{1,0:T(2,128)} %near_ref.21) | copy-start | bytes 52
  2.3 3.1 %collective-permute-start.1 = (f32[1,128]{1,0:T(1,128)S(1)}, f32[1,128]{1,0:T(1,128)S(1)}, u32[]{:S(2)}, u32[]{:S(2)}) collective-permute-start(f32[1,128]{1,0:T(1,128)S(1)} %squares.1.refs_0_), channel_id=1, source_target_pairs={{0,1},{1,0},{2,3},{3,2},{4,5},{5,4},{6,7},{7,6},{8,9},{9,8},{10,11... | collective-permute-start | bytes 1544 | tf_op jit(solution)/shard_map/ppermute | solution.py:377
  2.8 35.0 %collective-permute-start.5 = (bf16[128,4096]{1,0:T(8,128)(2,1)}, bf16[128,4096]{1,0:T(8,128)(2,1)S(1)}, u32[]{:S(2)}, u32[]{:S(2)}) collective-permute-start(bf16[128,4096]{1,0:T(8,128)(2,1)} %refs_4_.5), channel_id=1, source_target_pairs={{0,4},{2,6},{4,0},{6,2},{8,12},{10,14},{12,8},{14,10},{16,20},{18,... | collective-permute-start | bytes 3145736 | tf_op jit(solution)/shard_map/ppermute | solution.py:39
  5.4 1.2 copy-start.2
  6.6 0.7 copy-start.6
  7.3 0.7 copy-start.8
  8.0 19.5 %copy-start.4 = (bf16[128,4096]{1,0:T(8,128)(2,1)S(1)}, bf16[128,4096]{1,0:T(8,128)(2,1)}, u32[]{:S(2)}) copy-start(bf16[128,4096]{1,0:T(8,128)(2,1)} %refs_4_.4) | copy-start | bytes 3145732
  8.0 29.8 %copy-start.5 = (bf16[128,4096]{1,0:T(8,128)(2,1)S(1)}, bf16[128,4096]{1,0:T(8,128)(2,1)}, u32[]{:S(2)}) copy-start(bf16[128,4096]{1,0:T(8,128)(2,1)} %refs_4_.5) | copy-start | bytes 3145732
  9.0 14.8 %collective-permute-start.2 = (bf16[64,4096]{1,0:T(8,128)(2,1)S(1)}, bf16[64,4096]{1,0:T(8,128)(2,1)S(1)}, u32[]{:S(2)}, u32[]{:S(2)}) collective-permute-start(bf16[64,4096]{1,0:T(8,128)(2,1)S(1)} %get-tuple-element.71), channel_id=1, source_target_pairs={{0,2},{2,0},{4,6},{6,4},{8,10},{10,8},{12,14},{14,12},{16,18},{18,... | collective-permute-start | bytes 1572872 | tf_op jit(solution)/shard_map/ppermute | solution.py:39
  10.6 16.9 %collective-permute-start.3 = (bf16[64,4096]{1,0:T(8,128)(2,1)S(1)}, bf16[64,4096]{1,0:T(8,128)(2,1)S(1)}, u32[]{:S(2)}, u32[]{:S(2)}) collective-permute-start(bf16[64,4096]{1,0:T(8,128)(2,1)S(1)} %get-tuple-element.72), channel_id=1, source_target_pairs={{0,24},{2,26},{4,12},{6,14},{8,0},{10,2},{12,20},{14,22},{16,8},{1... | collective-permute-start | bytes 1572872 | tf_op jit(solution)/shard_map/ppermute | solution.py:39
  14.2 23.6 %collective-permute-start.4 = (bf16[64,4096]{1,0:T(8,128)(2,1)S(1)}, bf16[64,4096]{1,0:T(8,128)(2,1)S(1)}, u32[]{:S(2)}, u32[]{:S(2)}) collective-permute-start(bf16[64,4096]{1,0:T(8,128)(2,1)S(1)} %get-tuple-element.73), channel_id=1, source_target_pairs={{0,26},{2,0},{4,6},{6,12},{8,2},{10,8},{12,14},{14,20},{16,10},{18... | collective-permute-start | bytes 1572872 | tf_op jit(solution)/shard_map/ppermute | solution.py:39
  15.3 30.3 %collective-permute-start.6 = (bf16[64,4096]{1,0:T(8,128)(2,1)S(1)}, bf16[64,4096]{1,0:T(8,128)(2,1)S(1)}, u32[]{:S(2)}, u32[]{:S(2)}) collective-permute-start(bf16[64,4096]{1,0:T(8,128)(2,1)S(1)} %get-tuple-element.82), channel_id=1, source_target_pairs={{0,2},{2,0},{4,6},{6,4},{8,10},{10,8},{12,14},{14,12},{16,18},{18,... | collective-permute-start | bytes 1572872 | tf_op jit(solution)/shard_map/ppermute | solution.py:39
  23.9 24.0 %collective-permute-start.7 = (bf16[64,4096]{1,0:T(8,128)(2,1)S(1)}, bf16[64,4096]{1,0:T(8,128)(2,1)S(1)}, u32[]{:S(2)}, u32[]{:S(2)}) collective-permute-start(bf16[64,4096]{1,0:T(8,128)(2,1)S(1)} %get-tuple-element.83), channel_id=1, source_target_pairs={{0,24},{2,26},{4,12},{6,14},{8,0},{10,2},{12,20},{14,22},{16,8},{1... | collective-permute-start | bytes 1572872 | tf_op jit(solution)/shard_map/ppermute | solution.py:39
  27.5 40.8 %collective-permute-start = (bf16[128,4096]{1,0:T(8,128)(2,1)S(1)}, bf16[128,4096]{1,0:T(8,128)(2,1)S(1)}, u32[]{:S(2)}, u32[]{:S(2)}) collective-permute-start(bf16[128,4096]{1,0:T(8,128)(2,1)S(1)} %copy-done.4), channel_id=1, source_target_pairs={{0,4},{2,6},{4,0},{6,2},{8,12},{10,14},{12,8},{14,10},{16,20},{18,... | collective-permute-start | bytes 3145736 | tf_op jit(solution)/shard_map/ppermute | solution.py:39
  47.9 3.7 %collective-permute-start.8 = (f32[32,128]{1,0:T(8,128)S(1)}, f32[32,128]{1,0:T(8,128)S(1)}, u32[]{:S(2)}, u32[]{:S(2)}) collective-permute-start(f32[32,128]{1,0:T(8,128)S(1)} %get-tuple-element.84), channel_id=1, source_target_pairs={{2,0},{0,2},{6,4},{4,6},{10,8},{8,10},{14,12},{12,14},{18,16},{16,... | collective-permute-start | bytes 49160 | tf_op jit(solution)/shard_map/ppermute | solution.py:39
  47.9 6.0 %collective-permute-start.9 = (f32[32,128]{1,0:T(8,128)S(1)}, f32[32,128]{1,0:T(8,128)S(1)}, u32[]{:S(2)}, u32[]{:S(2)}) collective-permute-start(f32[32,128]{1,0:T(8,128)S(1)} %get-tuple-element.85), channel_id=1, source_target_pairs={{24,0},{26,2},{12,4},{14,6},{0,8},{2,10},{20,12},{22,14},{8,16},{1... | collective-permute-start | bytes 49160 | tf_op jit(solution)/shard_map/ppermute | solution.py:39
  48.6 6.9 %collective-permute-start.10 = (f32[32,128]{1,0:T(8,128)S(1)}, f32[32,128]{1,0:T(8,128)S(1)}, u32[]{:S(2)}, u32[]{:S(2)}) collective-permute-start(f32[32,128]{1,0:T(8,128)S(1)} %get-tuple-element.86), channel_id=1, source_target_pairs={{26,0},{0,2},{6,4},{12,6},{2,8},{8,10},{14,12},{20,14},{10,16},{16... | collective-permute-start | bytes 49160 | tf_op jit(solution)/shard_map/ppermute | solution.py:39
  56.2 12.1 %collective-permute-start.11 = (bf16[64,4096]{1,0:T(8,128)(2,1)S(1)}, bf16[64,4096]{1,0:T(8,128)(2,1)S(1)}, u32[]{:S(2)}, u32[]{:S(2)}) collective-permute-start(bf16[64,4096]{1,0:T(8,128)(2,1)S(1)} %pick.3), channel_id=1, source_target_pairs={{0,26},{2,0},{4,6},{6,12},{8,2},{10,8},{12,14},{14,20},{16,10},{18... | collective-permute-start | bytes 1572872 | tf_op jit(solution)/shard_map/ppermute | solution.py:39
  58.9 9.5 %collective-permute-start.12 = (f32[32,128]{1,0:T(8,128)S(1)}, f32[32,128]{1,0:T(8,128)S(1)}, u32[]{:S(2)}, u32[]{:S(2)}) collective-permute-start(f32[32,128]{1,0:T(8,128)S(1)} %get-tuple-element.91), channel_id=1, source_target_pairs={{0,2},{2,0},{4,6},{6,4},{8,10},{10,8},{12,14},{14,12},{16,18},{18,... | collective-permute-start | bytes 49160 | tf_op jit(solution)/shard_map/ppermute | solution.py:39
  59.1 9.3 %collective-permute-start.13 = (f32[32,128]{1,0:T(8,128)S(1)}, f32[32,128]{1,0:T(8,128)S(1)}, u32[]{:S(2)}, u32[]{:S(2)}) collective-permute-start(f32[32,128]{1,0:T(8,128)S(1)} %get-tuple-element.92), channel_id=1, source_target_pairs={{0,24},{2,26},{4,12},{6,14},{8,0},{10,2},{12,20},{14,22},{16,8},{1... | collective-permute-start | bytes 49160 | tf_op jit(solution)/shard_map/ppermute | solution.py:39
  61.1 7.5 %collective-permute-start.14 = (f32[32,128]{1,0:T(8,128)S(1)}, f32[32,128]{1,0:T(8,128)S(1)}, u32[]{:S(2)}, u32[]{:S(2)}) collective-permute-start(f32[32,128]{1,0:T(8,128)S(1)} %get-tuple-element.93), channel_id=1, source_target_pairs={{0,26},{2,0},{4,6},{6,12},{8,2},{10,8},{12,14},{14,20},{16,10},{18... | collective-permute-start | bytes 49160 | tf_op jit(solution)/shard_map/ppermute | solution.py:39
  70.2 10.8 %collective-permute-start.15 = (bf16[64,4096]{1,0:T(8,128)(2,1)S(1)}, bf16[64,4096]{1,0:T(8,128)(2,1)S(1)}, u32[]{:S(2)}, u32[]{:S(2)}) collective-permute-start(bf16[64,4096]{1,0:T(8,128)(2,1)S(1)} %get-tuple-element.96), channel_id=1, source_target_pairs={{2,0},{0,2},{6,4},{4,6},{10,8},{8,10},{14,12},{12,14},{18,16},{16,... | collective-permute-start | bytes 1572872 | tf_op jit(solution)/shard_map/ppermute | solution.py:39
  71.6 12.5 %collective-permute-start.16 = (bf16[64,4096]{1,0:T(8,128)(2,1)S(1)}, bf16[64,4096]{1,0:T(8,128)(2,1)S(1)}, u32[]{:S(2)}, u32[]{:S(2)}) collective-permute-start(bf16[64,4096]{1,0:T(8,128)(2,1)S(1)} %get-tuple-element.97), channel_id=1, source_target_pairs={{24,0},{26,2},{12,4},{14,6},{0,8},{2,10},{20,12},{22,14},{8,16},{1... | collective-permute-start | bytes 1572872 | tf_op jit(solution)/shard_map/ppermute | solution.py:39
  84.2 23.3 %collective-permute-start.27 = (bf16[128,4096]{1,0:T(8,128)(2,1)S(1)}, bf16[128,4096]{1,0:T(8,128)(2,1)S(1)}, u32[]{:S(2)}, u32[]{:S(2)}) collective-permute-start(bf16[128,4096]{1,0:T(8,128)(2,1)S(1)} %get-tuple-element.125), channel_id=1, source_target_pairs={{0,4},{2,6},{4,0},{6,2},{8,12},{10,14},{12,8},{14,10},{16,20},{18,... | collective-permute-start | bytes 3145736 | tf_op jit(solution)/shard_map/ppermute | solution.py:39
  84.2 3.7 %collective-permute-start.17 = (f32[32,128]{1,0:T(8,128)S(1)}, f32[32,128]{1,0:T(8,128)S(1)}, u32[]{:S(2)}, u32[]{:S(2)}) collective-permute-start(f32[32,128]{1,0:T(8,128)S(1)} %get-tuple-element.105), channel_id=1, source_target_pairs={{2,0},{0,2},{6,4},{4,6},{10,8},{8,10},{14,12},{12,14},{18,16},{16,... | collective-permute-start | bytes 49160 | tf_op jit(solution)/shard_map/ppermute | solution.py:39
  85.4 5.5 %collective-permute-start.18 = (f32[32,128]{1,0:T(8,128)S(1)}, f32[32,128]{1,0:T(8,128)S(1)}, u32[]{:S(2)}, u32[]{:S(2)}) collective-permute-start(f32[32,128]{1,0:T(8,128)S(1)} %get-tuple-element.106), channel_id=1, source_target_pairs={{24,0},{26,2},{12,4},{14,6},{0,8},{2,10},{20,12},{22,14},{8,16},{1... | collective-permute-start | bytes 49160 | tf_op jit(solution)/shard_map/ppermute | solution.py:39
  85.4 6.4 %collective-permute-start.19 = (f32[32,128]{1,0:T(8,128)S(1)}, f32[32,128]{1,0:T(8,128)S(1)}, u32[]{:S(2)}, u32[]{:S(2)}) collective-permute-start(f32[32,128]{1,0:T(8,128)S(1)} %get-tuple-element.107), channel_id=1, source_target_pairs={{26,0},{0,2},{6,4},{12,6},{2,8},{8,10},{14,12},{20,14},{10,16},{16... | collective-permute-start | bytes 49160 | tf_op jit(solution)/shard_map/ppermute | solution.py:39
  92.4 5.4 %collective-permute-start.21 = (f32[32,128]{1,0:T(8,128)S(1)}, f32[32,128]{1,0:T(8,128)S(1)}, u32[]{:S(2)}, u32[]{:S(2)}) collective-permute-start(f32[32,128]{1,0:T(8,128)S(1)} %get-tuple-element.113), channel_id=1, source_target_pairs={{0,2},{2,0},{4,6},{6,4},{8,10},{10,8},{12,14},{14,12},{16,18},{18,... | collective-permute-start | bytes 49160 | tf_op jit(solution)/shard_map/ppermute | solution.py:39
  92.5 5.3 %collective-permute-start.22 = (f32[32,128]{1,0:T(8,128)S(1)}, f32[32,128]{1,0:T(8,128)S(1)}, u32[]{:S(2)}, u32[]{:S(2)}) collective-permute-start(f32[32,128]{1,0:T(8,128)S(1)} %get-tuple-element.114), channel_id=1, source_target_pairs={{0,24},{2,26},{4,12},{6,14},{8,0},{10,2},{12,20},{14,22},{16,8},{1... | collective-permute-start | bytes 49160 | tf_op jit(solution)/shard_map/ppermute | solution.py:39
  94.9 5.6 %collective-permute-start.23 = (f32[32,128]{1,0:T(8,128)S(1)}, f32[32,128]{1,0:T(8,128)S(1)}, u32[]{:S(2)}, u32[]{:S(2)}) collective-permute-start(f32[32,128]{1,0:T(8,128)S(1)} %get-tuple-element.115), channel_id=1, source_target_pairs={{0,26},{2,0},{4,6},{6,12},{8,2},{10,8},{12,14},{14,20},{16,10},{18... | collective-permute-start | bytes 49160 | tf_op jit(solution)/shard_map/ppermute | solution.py:39
  96.3 13.9 %collective-permute-start.20 = (bf16[64,4096]{1,0:T(8,128)(2,1)S(1)}, bf16[64,4096]{1,0:T(8,128)(2,1)S(1)}, u32[]{:S(2)}, u32[]{:S(2)}) collective-permute-start(bf16[64,4096]{1,0:T(8,128)(2,1)S(1)} %get-tuple-element.109), channel_id=1, source_target_pairs={{26,0},{0,2},{6,4},{12,6},{2,8},{8,10},{14,12},{20,14},{10,16},{16... | collective-permute-start | bytes 1572872 | tf_op jit(solution)/shard_map/ppermute | solution.py:39
  107.5 20.2 %collective-permute-start.28 = (bf16[128,4096]{1,0:T(8,128)(2,1)S(1)}, bf16[128,4096]{1,0:T(8,128)(2,1)S(1)}, u32[]{:S(2)}, u32[]{:S(2)}) collective-permute-start(bf16[128,4096]{1,0:T(8,128)(2,1)S(1)} %get-tuple-element.129), channel_id=1, source_target_pairs={{0,4},{2,6},{4,0},{6,2},{8,12},{10,14},{12,8},{14,10},{16,20},{18,... | collective-permute-start | bytes 3145736 | tf_op jit(solution)/shard_map/ppermute | solution.py:39
  110.2 18.7 %collective-permute-start.24 = (bf16[64,4096]{1,0:T(8,128)(2,1)S(1)}, bf16[64,4096]{1,0:T(8,128)(2,1)S(1)}, u32[]{:S(2)}, u32[]{:S(2)}) collective-permute-start(bf16[64,4096]{1,0:T(8,128)(2,1)S(1)} %get-tuple-element.121), channel_id=1, source_target_pairs={{2,0},{0,2},{6,4},{4,6},{10,8},{8,10},{14,12},{12,14},{18,16},{16,... | collective-permute-start | bytes 1572872 | tf_op jit(solution)/shard_map/ppermute | solution.py:39
  110.3 18.6 %collective-permute-start.25 = (bf16[64,4096]{1,0:T(8,128)(2,1)S(1)}, bf16[64,4096]{1,0:T(8,128)(2,1)S(1)}, u32[]{:S(2)}, u32[]{:S(2)}) collective-permute-start(bf16[64,4096]{1,0:T(8,128)(2,1)S(1)} %get-tuple-element.122), channel_id=1, source_target_pairs={{24,0},{26,2},{12,4},{14,6},{0,8},{2,10},{20,12},{22,14},{8,16},{1... | collective-permute-start | bytes 1572872 | tf_op jit(solution)/shard_map/ppermute | solution.py:39
  112.4 18.3 %collective-permute-start.26 = (bf16[64,4096]{1,0:T(8,128)(2,1)S(1)}, bf16[64,4096]{1,0:T(8,128)(2,1)S(1)}, u32[]{:S(2)}, u32[]{:S(2)}) collective-permute-start(bf16[64,4096]{1,0:T(8,128)(2,1)S(1)} %get-tuple-element.123), channel_id=1, source_target_pairs={{26,0},{0,2},{6,4},{12,6},{2,8},{8,10},{14,12},{20,14},{10,16},{16... | collective-permute-start | bytes 1572872 | tf_op jit(solution)/shard_map/ppermute | solution.py:39
  127.7 3.0 %copy-start.3 = (bf16[128,4096]{1,0:T(8,128)(2,1)S(1)}, bf16[128,4096]{1,0:T(8,128)(2,1)}, u32[]{:S(2)}) copy-start(bf16[128,4096]{1,0:T(8,128)(2,1)} %q_ref.5) | copy-start | bytes 3145732
  127.7 3.0 %copy-start.9 = (f32[4096]{0:T(1024)S(1)}, f32[4096]{0:T(1024)}, u32[]{:S(2)}) copy-start(f32[4096]{0:T(1024)} %param.7) | copy-start | bytes 49156
  132.7 1.2 collective-permute-start.29

commit v5 on v4

--- a/solution.py
+++ b/solution.py
@@ -487,7 +487,7 @@
         normed, *q_slots, keys, far_keys, own_weights, far_weights, own_products, far_products,
         *back, *centres,
     )
-    far_dk = across(after(far_dk, far_dv))
+    far_dk = across(after(far_dk, contexts[4]))
     grads[2:] = after(grads[2:], contexts[4])
     grads = come(grads)
 

time: 136 us -> 145 us (1.066)
  waiting for transfers between devices: 69.9 us -> 80 us
    ppermute x28, waiting for transfers between devices: 68.8 us -> 78.9 us  [sent(): return lax.ppermute(array, 'dp', route)]
  transfers between devices with their start and end apart: 30 -> 30, of which waited for: 22 -> 20; matrix products, arithmetic and copies ran while one was open for 0% -> 0% of each run, Pallas kernels for 15% -> 14%
where the time goes in v5:
time: 145 us
  waiting for transfers between devices  80 us (55%)
  starting transfers between devices  33.5 us (23%)
  Pallas kernels  26.3 us (18%)
  local copies, waits for them, and re-layouts  3.99 us (3%)
    ppermute x28, waiting for transfers between devices, sent(): return lax.ppermute(array, 'dp', route)  78.9 us
    ppermute x28, starting transfers between devices, sent(): return lax.ppermute(array, 'dp', route)  32.9 us
    pallas_call x15, Pallas kernels, call(): pl.pallas_call(body, in_specs=[pl.BlockSpec(memory_space=pltpu.SMEM)] * s...  26.3 us
    unnamed x20, local copies, waits for them, and re-layouts  3.99 us
  transfers between devices with their start and end apart: 30, of which 20 were waited for; matrix products, arithmetic and copies ran while one was open for 0% of the time, Pallas kernels for 14%

profile of v5, /device:TPU:0, one launch (start us, length us, event | category | flops | bytes accessed | tf_op | source)
XLA Modules:
  0.0 144.6 jit_solution(13505936307342670606)
XLA Ops:
  0.7 1.3 copy-done.1
  2.0 0.3 squares.1.refs_0_
  2.3 0.5 collective-permute-start.1
  2.8 2.6 %collective-permute-start.5 = (bf16[128,4096]{1,0:T(8,128)(2,1)}, bf16[128,4096]{1,0:T(8,128)(2,1)S(1)}, u32[]{:S(2)}, u32[]{:S(2)}) collective-permute-start(bf16[128,4096]{1,0:T(8,128)(2,1)} %refs_4_.5), channel_id=1, source_target_pairs={{0,4},{2,6},{4,0},{6,2},{8,12},{10,14},{12,8},{14,10},{16,20},{18,... | collective-permute-start | bytes 3145736 | tf_op jit(solution)/shard_map/ppermute | solution.py:39
  5.4 1.2 copy-done.2
  6.6 0.7 copy-done.6
  7.3 0.7 copy-done.8
  8.0 1.0 prepare_queries.1
  9.0 1.6 %collective-permute-start.2 = (bf16[64,4096]{1,0:T(8,128)(2,1)S(1)}, bf16[64,4096]{1,0:T(8,128)(2,1)S(1)}, u32[]{:S(2)}, u32[]{:S(2)}) collective-permute-start(bf16[64,4096]{1,0:T(8,128)(2,1)S(1)} %get-tuple-element.71), channel_id=1, source_target_pairs={{0,2},{2,0},{4,6},{6,4},{8,10},{10,8},{12,14},{14,12},{16,18},{18,... | collective-permute-start | bytes 1572872 | tf_op jit(solution)/shard_map/ppermute | solution.py:39
  10.6 3.6 %collective-permute-start.3 = (bf16[64,4096]{1,0:T(8,128)(2,1)S(1)}, bf16[64,4096]{1,0:T(8,128)(2,1)S(1)}, u32[]{:S(2)}, u32[]{:S(2)}) collective-permute-start(bf16[64,4096]{1,0:T(8,128)(2,1)S(1)} %get-tuple-element.72), channel_id=1, source_target_pairs={{0,24},{2,26},{4,12},{6,14},{8,0},{10,2},{12,20},{14,22},{16,8},{1... | collective-permute-start | bytes 1572872 | tf_op jit(solution)/shard_map/ppermute | solution.py:39
  14.2 0.4 collective-permute-start.4
  14.6 0.6 pick.2
  15.3 1.7 %collective-permute-start.6 = (bf16[64,4096]{1,0:T(8,128)(2,1)S(1)}, bf16[64,4096]{1,0:T(8,128)(2,1)S(1)}, u32[]{:S(2)}, u32[]{:S(2)}) collective-permute-start(bf16[64,4096]{1,0:T(8,128)(2,1)S(1)} %get-tuple-element.82), channel_id=1, source_target_pairs={{0,2},{2,0},{4,6},{6,4},{8,10},{10,8},{12,14},{14,12},{16,18},{18,... | collective-permute-start | bytes 1572872 | tf_op jit(solution)/shard_map/ppermute | solution.py:39
  16.9 6.9 %collective-permute-done.2.refs_1_ = bf16[64,4096]{1,0:T(8,128)(2,1)S(1)} collective-permute-done((bf16[64,4096]{1,0:T(8,128)(2,1)S(1)}, bf16[64,4096]{1,0:T(8,128)(2,1)S(1)}, u32[]{:S(2)}, u32[]{:S(2)}) %collective-permute-start.2) | collective-permute-done | bytes 524320 | tf_op jit(solution)/shard_map/ppermute | solution.py:39
  23.9 3.6 %collective-permute-start.7 = (bf16[64,4096]{1,0:T(8,128)(2,1)S(1)}, bf16[64,4096]{1,0:T(8,128)(2,1)S(1)}, u32[]{:S(2)}, u32[]{:S(2)}) collective-permute-start(bf16[64,4096]{1,0:T(8,128)(2,1)S(1)} %get-tuple-element.83), channel_id=1, source_target_pairs={{0,24},{2,26},{4,12},{6,14},{8,0},{10,2},{12,20},{14,22},{16,8},{1... | collective-permute-start | bytes 1572872 | tf_op jit(solution)/shard_map/ppermute | solution.py:39
  27.5 10.3 %collective-permute-done.4.refs_3_ = bf16[64,4096]{1,0:T(8,128)(2,1)S(1)} collective-permute-done((bf16[64,4096]{1,0:T(8,128)(2,1)S(1)}, bf16[64,4096]{1,0:T(8,128)(2,1)S(1)}, u32[]{:S(2)}, u32[]{:S(2)}) %collective-permute-start.4) | collective-permute-done | bytes 524320 | tf_op jit(solution)/shard_map/ppermute | solution.py:39
  37.8 3.6 %scores.1 = (f32[32,128]{1,0:T(8,128)S(1)}, f32[32,128]{1,0:T(8,128)S(1)}, f32[32,128]{1,0:T(8,128)S(1)}, f32[32,128]{1,0:T(8,128)S(1)}, f32[32,128]{1,0:T(8,128...) custom-call(s32[1]{0:T(128)} %bitcast.place_ref, s32[2,2]{1,0:T(2,128)S(1)} %copy-done.7, ...), custom_call_target="tpu_custom_call" | custom-call | tf_op jit(solution)/shard_map/scores/pallas_call | solution.py:397
  41.4 4.2 %collective-permute-done.6.refs_1_.refs_3_ = bf16[64,4096]{1,0:T(8,128)(2,1)S(1)} collective-permute-done((bf16[64,4096]{1,0:T(8,128)(2,1)S(1)}, bf16[64,4096]{1,0:T(8,128)(2,1)S(1)}, u32[]{:S(2)}, u32[]{:S(2)}) %collective-permute-start.6) | collective-permute-done | bytes 524320 | tf_op jit(solution)/shard_map/ppermute | solution.py:39
  45.6 2.3 %collective-permute-done.7.refs_2_ = bf16[64,4096]{1,0:T(8,128)(2,1)S(1)} collective-permute-done((bf16[64,4096]{1,0:T(8,128)(2,1)S(1)}, bf16[64,4096]{1,0:T(8,128)(2,1)S(1)}, u32[]{:S(2)}, u32[]{:S(2)}) %collective-permute-start.7) | collective-permute-done | bytes 524320 | tf_op jit(solution)/shard_map/ppermute | solution.py:39
  47.9 0.7 collective-permute-start.9
  48.6 1.8 %collective-permute-start.10 = (f32[32,128]{1,0:T(8,128)S(1)}, f32[32,128]{1,0:T(8,128)S(1)}, u32[]{:S(2)}, u32[]{:S(2)}) collective-permute-start(f32[32,128]{1,0:T(8,128)S(1)} %get-tuple-element.86), channel_id=1, source_target_pairs={{26,0},{0,2},{6,4},{12,6},{2,8},{8,10},{14,12},{20,14},{10,16},{16... | collective-permute-start | bytes 49160 | tf_op jit(solution)/shard_map/ppermute | solution.py:39
  50.4 1.2 collective-permute-done.8.refs_2_
  51.6 2.3 %collective-permute-done.9.refs_3_ = f32[32,128]{1,0:T(8,128)S(1)} collective-permute-done((f32[32,128]{1,0:T(8,128)S(1)}, f32[32,128]{1,0:T(8,128)S(1)}, u32[]{:S(2)}, u32[]{:S(2)}) %collective-permute-start.9) | collective-permute-done | bytes 16416 | tf_op jit(solution)/shard_map/ppermute | solution.py:39
  54.0 1.6 %collective-permute-done.10.refs_4_ = f32[32,128]{1,0:T(8,128)S(1)} collective-permute-done((f32[32,128]{1,0:T(8,128)S(1)}, f32[32,128]{1,0:T(8,128)S(1)}, u32[]{:S(2)}, u32[]{:S(2)}) %collective-permute-start.10) | collective-permute-done | bytes 16416 | tf_op jit(solution)/shard_map/ppermute | solution.py:39
  55.6 0.6 pick.3
  56.2 1.9 %collective-permute-start.11 = (bf16[64,4096]{1,0:T(8,128)(2,1)S(1)}, bf16[64,4096]{1,0:T(8,128)(2,1)S(1)}, u32[]{:S(2)}, u32[]{:S(2)}) collective-permute-start(bf16[64,4096]{1,0:T(8,128)(2,1)S(1)} %pick.3), channel_id=1, source_target_pairs={{0,26},{2,0},{4,6},{6,12},{8,2},{10,8},{12,14},{14,20},{16,10},{18... | collective-permute-start | bytes 1572872 | tf_op jit(solution)/shard_map/ppermute | solution.py:39
  58.1 0.8 combine_scores.1
  58.9 0.2 collective-permute-start.12
  59.1 2.0 %collective-permute-start.13 = (f32[32,128]{1,0:T(8,128)S(1)}, f32[32,128]{1,0:T(8,128)S(1)}, u32[]{:S(2)}, u32[]{:S(2)}) collective-permute-start(f32[32,128]{1,0:T(8,128)S(1)} %get-tuple-element.92), channel_id=1, source_target_pairs={{0,24},{2,26},{4,12},{6,14},{8,0},{10,2},{12,20},{14,22},{16,8},{1... | collective-permute-start | bytes 49160 | tf_op jit(solution)/shard_map/ppermute | solution.py:39
  61.1 1.3 collective-permute-start.14
  62.4 5.8 %collective-permute-done.11.refs_3_ = bf16[64,4096]{1,0:T(8,128)(2,1)S(1)} collective-permute-done((bf16[64,4096]{1,0:T(8,128)(2,1)S(1)}, bf16[64,4096]{1,0:T(8,128)(2,1)S(1)}, u32[]{:S(2)}, u32[]{:S(2)}) %collective-permute-start.11) | collective-permute-done | bytes 524320 | tf_op jit(solution)/shard_map/ppermute | solution.py:39
  68.3 0.2 collective-permute-done.12.refs_6_.refs_10_.refs_12_.refs_7_
  68.4 0.2 collective-permute-done.14.refs_8_.refs_12_.refs_14_
  68.6 1.6 %context.1 = (bf16[64,4096]{1,0:T(8,128)(2,1)S(1)}, bf16[64,4096]{1,0:T(8,128)(2,1)S(1)}, bf16[64,4096]{1,0:T(8,128)(2,1)S(1)}, bf16[64,4096]{1,0:T(8,128)(2,1)S(1)}, bf16[64,4096]{1,0:T(8,128)(2,1)S(1)}) custom-call(bf16[128,4096]{1,0:T(8,128)(2,1)S(1)} %copy-done.4, bf16[128,4096]{1,0:T(8,128)(2,1)S(1)} %collective-permute-done.refs_1_.refs_5_, ...), custom_call_target="tpu_custom_call" | custom-call | tf_op jit(solution)/shard_map/context/pallas_call | solution.py:397
  70.2 1.4 collective-permute-start.15
  71.6 0.6 collective-permute-start.16
  72.2 3.6 %centres.1 = (f32[32,128]{1,0:T(8,128)S(1)}, f32[32,128]{1,0:T(8,128)S(1)}, f32[32,128]{1,0:T(8,128)S(1)}, f32[32,128]{1,0:T(8,128)S(1)}, f32[32,128]{1,0:T(8,12...) custom-call(s32[1]{0:T(128)} %bitcast.place_ref, s32[2,2]{1,0:T(2,128)S(1)} %copy-done.7, ...), custom_call_target="tpu_custom_call" | custom-call | tf_op jit(solution)/shard_map/centres/pallas_call | solution.py:397
  75.8 5.2 %collective-permute-done.15.refs_2_ = bf16[64,4096]{1,0:T(8,128)(2,1)S(1)} collective-permute-done((bf16[64,4096]{1,0:T(8,128)(2,1)S(1)}, bf16[64,4096]{1,0:T(8,128)(2,1)S(1)}, u32[]{:S(2)}, u32[]{:S(2)}) %collective-permute-start.15) | collective-permute-done | bytes 524320 | tf_op jit(solution)/shard_map/ppermute | solution.py:39
  81.0 3.1 %collective-permute-done.16.refs_3_ = bf16[64,4096]{1,0:T(8,128)(2,1)S(1)} collective-permute-done((bf16[64,4096]{1,0:T(8,128)(2,1)S(1)}, bf16[64,4096]{1,0:T(8,128)(2,1)S(1)}, u32[]{:S(2)}, u32[]{:S(2)}) %collective-permute-start.16) | collective-permute-done | bytes 524320 | tf_op jit(solution)/shard_map/ppermute | solution.py:39
  84.2 0.4 collective-permute-start.17
  84.6 1.6 %collective-permute-start.19 = (f32[32,128]{1,0:T(8,128)S(1)}, f32[32,128]{1,0:T(8,128)S(1)}, u32[]{:S(2)}, u32[]{:S(2)}) collective-permute-start(f32[32,128]{1,0:T(8,128)S(1)} %get-tuple-element.107), channel_id=1, source_target_pairs={{26,0},{0,2},{6,4},{12,6},{2,8},{8,10},{14,12},{20,14},{10,16},{16... | collective-permute-start | bytes 49160 | tf_op jit(solution)/shard_map/ppermute | solution.py:39
  86.2 1.7 %collective-permute-done.17.refs_2_ = f32[32,128]{1,0:T(8,128)S(1)} collective-permute-done((f32[32,128]{1,0:T(8,128)S(1)}, f32[32,128]{1,0:T(8,128)S(1)}, u32[]{:S(2)}, u32[]{:S(2)}) %collective-permute-start.17) | collective-permute-done | bytes 16416 | tf_op jit(solution)/shard_map/ppermute | solution.py:39
  87.9 2.2 %collective-permute-done.18.refs_3_ = f32[32,128]{1,0:T(8,128)S(1)} collective-permute-done((f32[32,128]{1,0:T(8,128)S(1)}, f32[32,128]{1,0:T(8,128)S(1)}, u32[]{:S(2)}, u32[]{:S(2)}) %collective-permute-start.18) | collective-permute-done | bytes 16416 | tf_op jit(solution)/shard_map/ppermute | solution.py:39
  90.1 1.2 collective-permute-done.19.refs_4_
  91.3 0.6 combine_centres.1
  91.9 0.4 collective-permute-start.20
  92.4 0.1 collective-permute-start.21
  92.5 4.8 %collective-permute-start.22 = (f32[32,128]{1,0:T(8,128)S(1)}, f32[32,128]{1,0:T(8,128)S(1)}, u32[]{:S(2)}, u32[]{:S(2)}) collective-permute-start(f32[32,128]{1,0:T(8,128)S(1)} %get-tuple-element.114), channel_id=1, source_target_pairs={{0,24},{2,26},{4,12},{6,14},{8,0},{10,2},{12,20},{14,22},{16,8},{1... | collective-permute-start | bytes 49160 | tf_op jit(solution)/shard_map/ppermute | solution.py:39
  97.3 2.0 %collective-permute-done.21.refs_17_.refs_9_ = f32[32,128]{1,0:T(8,128)S(1)} collective-permute-done((f32[32,128]{1,0:T(8,128)S(1)}, f32[32,128]{1,0:T(8,128)S(1)}, u32[]{:S(2)}, u32[]{:S(2)}) %collective-permute-start.21) | collective-permute-done | bytes 16416 | tf_op jit(solution)/shard_map/ppermute | solution.py:39
  99.3 4.9 %collective-permute-done.23.refs_19_ = f32[32,128]{1,0:T(8,128)S(1)} collective-permute-done((f32[32,128]{1,0:T(8,128)S(1)}, f32[32,128]{1,0:T(8,128)S(1)}, u32[]{:S(2)}, u32[]{:S(2)}) %collective-permute-start.23) | collective-permute-done | bytes 16416 | tf_op jit(solution)/shard_map/ppermute | solution.py:39
  104.1 3.2 %gradient.1 = (bf16[64,4096]{1,0:T(8,128)(2,1)S(1)}, bf16[64,4096]{1,0:T(8,128)(2,1)S(1)}, bf16[64,4096]{1,0:T(8,128)(2,1)S(1)}, bf16[64,4096]{1,0:T(8,128)(2,1)...) custom-call(s32[1]{0:T(128)} %bitcast.place_ref, s32[2,2]{1,0:T(2,128)S(1)} %copy-done.7, ...), custom_call_target="tpu_custom_call" | custom-call | tf_op jit(solution)/shard_map/gradient/pallas_call | solution.py:397
  107.3 0.1 collective-permute-start.28
  107.4 0.1 collective-permute-start.24
  107.4 0.1 collective-permute-start.25
  107.5 1.9 %collective-permute-start.26 = (bf16[64,4096]{1,0:T(8,128)(2,1)S(1)}, bf16[64,4096]{1,0:T(8,128)(2,1)S(1)}, u32[]{:S(2)}, u32[]{:S(2)}) collective-permute-start(bf16[64,4096]{1,0:T(8,128)(2,1)S(1)} %get-tuple-element.123), channel_id=1, source_target_pairs={{26,0},{0,2},{6,4},{12,6},{2,8},{8,10},{14,12},{20,14},{10,16},{16... | collective-permute-start | bytes 1572872 | tf_op jit(solution)/shard_map/ppermute | solution.py:39
  109.5 2.6 %attended.1 = bf16[128,4096]{1,0:T(8,128)(2,1)} custom-call(s32[1]{0:T(128)} %bitcast.place_ref, s32[2,2]{1,0:T(2,128)S(1)} %copy-done.7, bf16[64,4096]{1,0:T(8,128)(2,1)S(1)} %get-tuple-element.94.refs_0_, bf16[64,4096]{1,0:T(8,128)(2,1)S(1)} %get-tuple-element.95.refs_1_, bf16[64,4096]{1,0:T(8,128)(2,1)S(1)} %collective-permute-done.15.refs_2_, ...), custom_call_target="tpu_custom_call" | custom-call | tf_op jit(solution)/shard_map/attended/pallas_call | solution.py:397
  112.0 11.3 %collective-permute-done.27.refs_10_ = bf16[128,4096]{1,0:T(8,128)(2,1)S(1)} collective-permute-done((bf16[128,4096]{1,0:T(8,128)(2,1)S(1)}, bf16[128,4096]{1,0:T(8,128)(2,1)S(1)}, u32[]{:S(2)}, u32[]{:S(2)}) %collective-permute-start.27) | collective-permute-done | bytes 1048608 | tf_op jit(solution)/shard_map/ppermute | solution.py:39
  123.4 3.0 %own.1 = (bf16[128,4096]{1,0:T(8,128)(2,1)}, f32[128,4096]{1,0:T(8,128)S(1)}) custom-call(s32[1]{0:T(128)} %bitcast.place_ref, s32[2,2]{1,0:T(2,128)S(1)} %copy-done.7, bf16[128,4096]{1,0:T(8,128)(2,1)S(1)} %get-tuple-element.70.refs_0_, bf16[64,4096]{1,0:T(8,128)(2,1)S(1)} %collective-permute-done.2.refs_1_, bf16[128,4096]{1,0:T(8,128)(2,1)S(1)} %copy-done, ...), custom_call_target="tpu_custom_call" | custom-call | tf_op jit(solution)/shard_map/own/pallas_call | solution.py:397
  126.4 12.1 %collective-permute-done.28.far_ref = bf16[128,4096]{1,0:T(8,128)(2,1)S(1)} collective-permute-done((bf16[128,4096]{1,0:T(8,128)(2,1)S(1)}, bf16[128,4096]{1,0:T(8,128)(2,1)S(1)}, u32[]{:S(2)}, u32[]{:S(2)}) %collective-permute-start.28) | collective-permute-done | bytes 1048608 | tf_op jit(solution)/shard_map/ppermute | solution.py:39
  138.5 1.2 add.1
  139.8 2.0 %inner.1 = (f32[128,4096]{1,0:T(8,128)S(1)}, f32[1,128]{1,0:T(1,128)S(1)}) custom-call(s32[1]{0:T(128)} %bitcast.place_ref, s32[2,2]{1,0:T(2,128)S(1)} %copy-done.7, bf16[64,4096]{1,0:T(8,128)(2,1)S(1)} %get-tuple-element.116.refs_0_, bf16[64,4096]{1,0:T(8,128)(2,1)S(1)} %get-tuple-element.117.refs_1_, bf16[64,4096]{1,0:T(8,128)(2,1)S(1)} %collective-permute-done.24.refs_2_, ...), custom_call_target="tpu_custom_call" | custom-call | tf_op jit(solution)/shard_map/inner/pallas_call | solution.py:397
  141.8 0.1 collective-permute-start.29
  141.9 1.1 collective-permute-done.29.refs_3_
  143.0 1.7 %finish.1 = bf16[128,4096]{1,0:T(8,128)(2,1)} custom-call(f32[128,4096]{1,0:T(8,128)S(1)} %get-tuple-element.134.scaled_ref, bf16[128,4096]{1,0:T(8,128)(2,1)S(1)} %copy-done.3, f32[1,128]{1,0:T(1,128)S(1)} %squares.1.refs_0_, f32[1,128]{1,0:T(1,128)S(1)} %collective-permute-done.1.refs_1_, f32[1,128]{1,0:T(1,128)S(1)} %get-tuple-element.135.refs_2_, ...), custom_call_target="tpu_custom_call" | custom-call | tf_op jit(solution)/shard_map/finish/pallas_call | solution.py:397
  (31 shorter events, 0.1 us)
Async XLA Ops:
  0.6 14.0 %copy-start = (bf16[128,4096]{1,0:T(8,128)(2,1)S(1)}, bf16[128,4096]{1,0:T(8,128)(2,1)}, u32[]{:S(2)}) copy-start(bf16[128,4096]{1,0:T(8,128)(2,1)} %refs_2_.1) | copy-start | bytes 3145732
  0.6 1.3 copy-start.1
  2.0 12.7 %copy-start.7 = (s32[2,2]{1,0:T(2,128)S(1)}, s32[2,2]{1,0:T(2,128)}, u32[]{:S(2)}) copy-start(s32[2,2]{1,0:T(2,128)} %near_ref.21) | copy-start | bytes 52
  2.3 3.1 %collective-permute-start.1 = (f32[1,128]{1,0:T(1,128)S(1)}, f32[1,128]{1,0:T(1,128)S(1)}, u32[]{:S(2)}, u32[]{:S(2)}) collective-permute-start(f32[1,128]{1,0:T(1,128)S(1)} %squares.1.refs_0_), channel_id=1, source_target_pairs={{0,1},{1,0},{2,3},{3,2},{4,5},{5,4},{6,7},{7,6},{8,9},{9,8},{10,11... | collective-permute-start | bytes 1544 | tf_op jit(solution)/shard_map/ppermute | solution.py:377
  2.8 35.0 %collective-permute-start.5 = (bf16[128,4096]{1,0:T(8,128)(2,1)}, bf16[128,4096]{1,0:T(8,128)(2,1)S(1)}, u32[]{:S(2)}, u32[]{:S(2)}) collective-permute-start(bf16[128,4096]{1,0:T(8,128)(2,1)} %refs_4_.5), channel_id=1, source_target_pairs={{0,4},{2,6},{4,0},{6,2},{8,12},{10,14},{12,8},{14,10},{16,20},{18,... | collective-permute-start | bytes 3145736 | tf_op jit(solution)/shard_map/ppermute | solution.py:39
  5.4 1.2 copy-start.2
  6.6 0.7 copy-start.6
  7.3 0.7 copy-start.8
  8.0 19.5 %copy-start.4 = (bf16[128,4096]{1,0:T(8,128)(2,1)S(1)}, bf16[128,4096]{1,0:T(8,128)(2,1)}, u32[]{:S(2)}) copy-start(bf16[128,4096]{1,0:T(8,128)(2,1)} %refs_4_.4) | copy-start | bytes 3145732
  8.0 29.8 %copy-start.5 = (bf16[128,4096]{1,0:T(8,128)(2,1)S(1)}, bf16[128,4096]{1,0:T(8,128)(2,1)}, u32[]{:S(2)}) copy-start(bf16[128,4096]{1,0:T(8,128)(2,1)} %refs_4_.5) | copy-start | bytes 3145732
  9.0 14.8 %collective-permute-start.2 = (bf16[64,4096]{1,0:T(8,128)(2,1)S(1)}, bf16[64,4096]{1,0:T(8,128)(2,1)S(1)}, u32[]{:S(2)}, u32[]{:S(2)}) collective-permute-start(bf16[64,4096]{1,0:T(8,128)(2,1)S(1)} %get-tuple-element.71), channel_id=1, source_target_pairs={{0,2},{2,0},{4,6},{6,4},{8,10},{10,8},{12,14},{14,12},{16,18},{18,... | collective-permute-start | bytes 1572872 | tf_op jit(solution)/shard_map/ppermute | solution.py:39
  10.6 16.9 %collective-permute-start.3 = (bf16[64,4096]{1,0:T(8,128)(2,1)S(1)}, bf16[64,4096]{1,0:T(8,128)(2,1)S(1)}, u32[]{:S(2)}, u32[]{:S(2)}) collective-permute-start(bf16[64,4096]{1,0:T(8,128)(2,1)S(1)} %get-tuple-element.72), channel_id=1, source_target_pairs={{0,24},{2,26},{4,12},{6,14},{8,0},{10,2},{12,20},{14,22},{16,8},{1... | collective-permute-start | bytes 1572872 | tf_op jit(solution)/shard_map/ppermute | solution.py:39
  14.2 23.6 %collective-permute-start.4 = (bf16[64,4096]{1,0:T(8,128)(2,1)S(1)}, bf16[64,4096]{1,0:T(8,128)(2,1)S(1)}, u32[]{:S(2)}, u32[]{:S(2)}) collective-permute-start(bf16[64,4096]{1,0:T(8,128)(2,1)S(1)} %get-tuple-element.73), channel_id=1, source_target_pairs={{0,26},{2,0},{4,6},{6,12},{8,2},{10,8},{12,14},{14,20},{16,10},{18... | collective-permute-start | bytes 1572872 | tf_op jit(solution)/shard_map/ppermute | solution.py:39
  15.3 30.3 %collective-permute-start.6 = (bf16[64,4096]{1,0:T(8,128)(2,1)S(1)}, bf16[64,4096]{1,0:T(8,128)(2,1)S(1)}, u32[]{:S(2)}, u32[]{:S(2)}) collective-permute-start(bf16[64,4096]{1,0:T(8,128)(2,1)S(1)} %get-tuple-element.82), channel_id=1, source_target_pairs={{0,2},{2,0},{4,6},{6,4},{8,10},{10,8},{12,14},{14,12},{16,18},{18,... | collective-permute-start | bytes 1572872 | tf_op jit(solution)/shard_map/ppermute | solution.py:39
  23.9 24.0 %collective-permute-start.7 = (bf16[64,4096]{1,0:T(8,128)(2,1)S(1)}, bf16[64,4096]{1,0:T(8,128)(2,1)S(1)}, u32[]{:S(2)}, u32[]{:S(2)}) collective-permute-start(bf16[64,4096]{1,0:T(8,128)(2,1)S(1)} %get-tuple-element.83), channel_id=1, source_target_pairs={{0,24},{2,26},{4,12},{6,14},{8,0},{10,2},{12,20},{14,22},{16,8},{1... | collective-permute-start | bytes 1572872 | tf_op jit(solution)/shard_map/ppermute | solution.py:39
  27.5 40.8 %collective-permute-start = (bf16[128,4096]{1,0:T(8,128)(2,1)S(1)}, bf16[128,4096]{1,0:T(8,128)(2,1)S(1)}, u32[]{:S(2)}, u32[]{:S(2)}) collective-permute-start(bf16[128,4096]{1,0:T(8,128)(2,1)S(1)} %copy-done.4), channel_id=1, source_target_pairs={{0,4},{2,6},{4,0},{6,2},{8,12},{10,14},{12,8},{14,10},{16,20},{18,... | collective-permute-start | bytes 3145736 | tf_op jit(solution)/shard_map/ppermute | solution.py:39
  47.9 3.7 %collective-permute-start.8 = (f32[32,128]{1,0:T(8,128)S(1)}, f32[32,128]{1,0:T(8,128)S(1)}, u32[]{:S(2)}, u32[]{:S(2)}) collective-permute-start(f32[32,128]{1,0:T(8,128)S(1)} %get-tuple-element.84), channel_id=1, source_target_pairs={{2,0},{0,2},{6,4},{4,6},{10,8},{8,10},{14,12},{12,14},{18,16},{16,... | collective-permute-start | bytes 49160 | tf_op jit(solution)/shard_map/ppermute | solution.py:39
  47.9 6.0 %collective-permute-start.9 = (f32[32,128]{1,0:T(8,128)S(1)}, f32[32,128]{1,0:T(8,128)S(1)}, u32[]{:S(2)}, u32[]{:S(2)}) collective-permute-start(f32[32,128]{1,0:T(8,128)S(1)} %get-tuple-element.85), channel_id=1, source_target_pairs={{24,0},{26,2},{12,4},{14,6},{0,8},{2,10},{20,12},{22,14},{8,16},{1... | collective-permute-start | bytes 49160 | tf_op jit(solution)/shard_map/ppermute | solution.py:39
  48.6 6.9 %collective-permute-start.10 = (f32[32,128]{1,0:T(8,128)S(1)}, f32[32,128]{1,0:T(8,128)S(1)}, u32[]{:S(2)}, u32[]{:S(2)}) collective-permute-start(f32[32,128]{1,0:T(8,128)S(1)} %get-tuple-element.86), channel_id=1, source_target_pairs={{26,0},{0,2},{6,4},{12,6},{2,8},{8,10},{14,12},{20,14},{10,16},{16... | collective-permute-start | bytes 49160 | tf_op jit(solution)/shard_map/ppermute | solution.py:39
  56.2 12.1 %collective-permute-start.11 = (bf16[64,4096]{1,0:T(8,128)(2,1)S(1)}, bf16[64,4096]{1,0:T(8,128)(2,1)S(1)}, u32[]{:S(2)}, u32[]{:S(2)}) collective-permute-start(bf16[64,4096]{1,0:T(8,128)(2,1)S(1)} %pick.3), channel_id=1, source_target_pairs={{0,26},{2,0},{4,6},{6,12},{8,2},{10,8},{12,14},{14,20},{16,10},{18... | collective-permute-start | bytes 1572872 | tf_op jit(solution)/shard_map/ppermute | solution.py:39
  58.9 9.5 %collective-permute-start.12 = (f32[32,128]{1,0:T(8,128)S(1)}, f32[32,128]{1,0:T(8,128)S(1)}, u32[]{:S(2)}, u32[]{:S(2)}) collective-permute-start(f32[32,128]{1,0:T(8,128)S(1)} %get-tuple-element.91), channel_id=1, source_target_pairs={{0,2},{2,0},{4,6},{6,4},{8,10},{10,8},{12,14},{14,12},{16,18},{18,... | collective-permute-start | bytes 49160 | tf_op jit(solution)/shard_map/ppermute | solution.py:39
  59.1 9.3 %collective-permute-start.13 = (f32[32,128]{1,0:T(8,128)S(1)}, f32[32,128]{1,0:T(8,128)S(1)}, u32[]{:S(2)}, u32[]{:S(2)}) collective-permute-start(f32[32,128]{1,0:T(8,128)S(1)} %get-tuple-element.92), channel_id=1, source_target_pairs={{0,24},{2,26},{4,12},{6,14},{8,0},{10,2},{12,20},{14,22},{16,8},{1... | collective-permute-start | bytes 49160 | tf_op jit(solution)/shard_map/ppermute | solution.py:39
  61.1 7.5 %collective-permute-start.14 = (f32[32,128]{1,0:T(8,128)S(1)}, f32[32,128]{1,0:T(8,128)S(1)}, u32[]{:S(2)}, u32[]{:S(2)}) collective-permute-start(f32[32,128]{1,0:T(8,128)S(1)} %get-tuple-element.93), channel_id=1, source_target_pairs={{0,26},{2,0},{4,6},{6,12},{8,2},{10,8},{12,14},{14,20},{16,10},{18... | collective-permute-start | bytes 49160 | tf_op jit(solution)/shard_map/ppermute | solution.py:39
  70.2 10.8 %collective-permute-start.15 = (bf16[64,4096]{1,0:T(8,128)(2,1)S(1)}, bf16[64,4096]{1,0:T(8,128)(2,1)S(1)}, u32[]{:S(2)}, u32[]{:S(2)}) collective-permute-start(bf16[64,4096]{1,0:T(8,128)(2,1)S(1)} %get-tuple-element.96), channel_id=1, source_target_pairs={{2,0},{0,2},{6,4},{4,6},{10,8},{8,10},{14,12},{12,14},{18,16},{16,... | collective-permute-start | bytes 1572872 | tf_op jit(solution)/shard_map/ppermute | solution.py:39
  71.6 12.5 %collective-permute-start.16 = (bf16[64,4096]{1,0:T(8,128)(2,1)S(1)}, bf16[64,4096]{1,0:T(8,128)(2,1)S(1)}, u32[]{:S(2)}, u32[]{:S(2)}) collective-permute-start(bf16[64,4096]{1,0:T(8,128)(2,1)S(1)} %get-tuple-element.97), channel_id=1, source_target_pairs={{24,0},{26,2},{12,4},{14,6},{0,8},{2,10},{20,12},{22,14},{8,16},{1... | collective-permute-start | bytes 1572872 | tf_op jit(solution)/shard_map/ppermute | solution.py:39
  84.2 3.7 %collective-permute-start.17 = (f32[32,128]{1,0:T(8,128)S(1)}, f32[32,128]{1,0:T(8,128)S(1)}, u32[]{:S(2)}, u32[]{:S(2)}) collective-permute-start(f32[32,128]{1,0:T(8,128)S(1)} %get-tuple-element.105), channel_id=1, source_target_pairs={{2,0},{0,2},{6,4},{4,6},{10,8},{8,10},{14,12},{12,14},{18,16},{16,... | collective-permute-start | bytes 49160 | tf_op jit(solution)/shard_map/ppermute | solution.py:39
  84.6 5.5 %collective-permute-start.18 = (f32[32,128]{1,0:T(8,128)S(1)}, f32[32,128]{1,0:T(8,128)S(1)}, u32[]{:S(2)}, u32[]{:S(2)}) collective-permute-start(f32[32,128]{1,0:T(8,128)S(1)} %get-tuple-element.106), channel_id=1, source_target_pairs={{24,0},{26,2},{12,4},{14,6},{0,8},{2,10},{20,12},{22,14},{8,16},{1... | collective-permute-start | bytes 49160 | tf_op jit(solution)/shard_map/ppermute | solution.py:39
  84.6 6.7 %collective-permute-start.19 = (f32[32,128]{1,0:T(8,128)S(1)}, f32[32,128]{1,0:T(8,128)S(1)}, u32[]{:S(2)}, u32[]{:S(2)}) collective-permute-start(f32[32,128]{1,0:T(8,128)S(1)} %get-tuple-element.107), channel_id=1, source_target_pairs={{26,0},{0,2},{6,4},{12,6},{2,8},{8,10},{14,12},{20,14},{10,16},{16... | collective-permute-start | bytes 49160 | tf_op jit(solution)/shard_map/ppermute | solution.py:39
  91.9 15.3 %collective-permute-start.20 = (bf16[64,4096]{1,0:T(8,128)(2,1)S(1)}, bf16[64,4096]{1,0:T(8,128)(2,1)S(1)}, u32[]{:S(2)}, u32[]{:S(2)}) collective-permute-start(bf16[64,4096]{1,0:T(8,128)(2,1)S(1)} %get-tuple-element.109), channel_id=1, source_target_pairs={{26,0},{0,2},{6,4},{12,6},{2,8},{8,10},{14,12},{20,14},{10,16},{16... | collective-permute-start | bytes 1572872 | tf_op jit(solution)/shard_map/ppermute | solution.py:39
  92.4 6.9 %collective-permute-start.21 = (f32[32,128]{1,0:T(8,128)S(1)}, f32[32,128]{1,0:T(8,128)S(1)}, u32[]{:S(2)}, u32[]{:S(2)}) collective-permute-start(f32[32,128]{1,0:T(8,128)S(1)} %get-tuple-element.113), channel_id=1, source_target_pairs={{0,2},{2,0},{4,6},{6,4},{8,10},{10,8},{12,14},{14,12},{16,18},{18,... | collective-permute-start | bytes 49160 | tf_op jit(solution)/shard_map/ppermute | solution.py:39
  92.5 6.8 %collective-permute-start.22 = (f32[32,128]{1,0:T(8,128)S(1)}, f32[32,128]{1,0:T(8,128)S(1)}, u32[]{:S(2)}, u32[]{:S(2)}) collective-permute-start(f32[32,128]{1,0:T(8,128)S(1)} %get-tuple-element.114), channel_id=1, source_target_pairs={{0,24},{2,26},{4,12},{6,14},{8,0},{10,2},{12,20},{14,22},{16,8},{1... | collective-permute-start | bytes 49160 | tf_op jit(solution)/shard_map/ppermute | solution.py:39
  97.3 6.8 %collective-permute-start.23 = (f32[32,128]{1,0:T(8,128)S(1)}, f32[32,128]{1,0:T(8,128)S(1)}, u32[]{:S(2)}, u32[]{:S(2)}) collective-permute-start(f32[32,128]{1,0:T(8,128)S(1)} %get-tuple-element.115), channel_id=1, source_target_pairs={{0,26},{2,0},{4,6},{6,12},{8,2},{10,8},{12,14},{14,20},{16,10},{18... | collective-permute-start | bytes 49160 | tf_op jit(solution)/shard_map/ppermute | solution.py:39
  97.3 26.1 %collective-permute-start.27 = (bf16[128,4096]{1,0:T(8,128)(2,1)S(1)}, bf16[128,4096]{1,0:T(8,128)(2,1)S(1)}, u32[]{:S(2)}, u32[]{:S(2)}) collective-permute-start(bf16[128,4096]{1,0:T(8,128)(2,1)S(1)} %get-tuple-element.125), channel_id=1, source_target_pairs={{0,4},{2,6},{4,0},{6,2},{8,12},{10,14},{12,8},{14,10},{16,20},{18,... | collective-permute-start | bytes 3145736 | tf_op jit(solution)/shard_map/ppermute | solution.py:39
  107.3 31.2 %collective-permute-start.28 = (bf16[128,4096]{1,0:T(8,128)(2,1)S(1)}, bf16[128,4096]{1,0:T(8,128)(2,1)S(1)}, u32[]{:S(2)}, u32[]{:S(2)}) collective-permute-start(bf16[128,4096]{1,0:T(8,128)(2,1)S(1)} %get-tuple-element.129), channel_id=1, source_target_pairs={{0,4},{2,6},{4,0},{6,2},{8,12},{10,14},{12,8},{14,10},{16,20},{18,... | collective-permute-start | bytes 3145736 | tf_op jit(solution)/shard_map/ppermute | solution.py:39
  107.4 32.4 %collective-permute-start.24 = (bf16[64,4096]{1,0:T(8,128)(2,1)S(1)}, bf16[64,4096]{1,0:T(8,128)(2,1)S(1)}, u32[]{:S(2)}, u32[]{:S(2)}) collective-permute-start(bf16[64,4096]{1,0:T(8,128)(2,1)S(1)} %get-tuple-element.121), channel_id=1, source_target_pairs={{2,0},{0,2},{6,4},{4,6},{10,8},{8,10},{14,12},{12,14},{18,16},{16,... | collective-permute-start | bytes 1572872 | tf_op jit(solution)/shard_map/ppermute | solution.py:39
  107.4 32.3 %collective-permute-start.25 = (bf16[64,4096]{1,0:T(8,128)(2,1)S(1)}, bf16[64,4096]{1,0:T(8,128)(2,1)S(1)}, u32[]{:S(2)}, u32[]{:S(2)}) collective-permute-start(bf16[64,4096]{1,0:T(8,128)(2,1)S(1)} %get-tuple-element.122), channel_id=1, source_target_pairs={{24,0},{26,2},{12,4},{14,6},{0,8},{2,10},{20,12},{22,14},{8,16},{1... | collective-permute-start | bytes 1572872 | tf_op jit(solution)/shard_map/ppermute | solution.py:39
  107.5 32.2 %collective-permute-start.26 = (bf16[64,4096]{1,0:T(8,128)(2,1)S(1)}, bf16[64,4096]{1,0:T(8,128)(2,1)S(1)}, u32[]{:S(2)}, u32[]{:S(2)}) collective-permute-start(bf16[64,4096]{1,0:T(8,128)(2,1)S(1)} %get-tuple-element.123), channel_id=1, source_target_pairs={{26,0},{0,2},{6,4},{12,6},{2,8},{8,10},{14,12},{20,14},{10,16},{16... | collective-permute-start | bytes 1572872 | tf_op jit(solution)/shard_map/ppermute | solution.py:39
  138.5 1.3 copy-start.3
  138.5 1.3 copy-start.9
  141.8 1.2 collective-permute-start.29
